TPU v7x, 32 devices: a whole 2x2x4 slice. The times are simulated.
32 devices in a mesh: frame: 16 (over z, x, core), quad: 2 (over y).
Axes of the slice: x: 2, y: 2, z: 4, core: 2. Of those that a mesh axis runs over, the one named last changes fastest.
Arguments:
- activations: bfloat16 [64, 32, 1280], P('frame', 'quad'), may hold values from -48 to 48
- cotangent: bfloat16 [64, 32, 1280], P('frame', 'quad'), may hold values from -6 to 6
- spatial_weights: bfloat16 [4, 1280, 640], replicated, may hold values from -2 to 2
- spatial_gain: float32 [1280], replicated, may hold values from 0.1 to 1.9
- motion_weights: bfloat16 [4, 1280, 640], P(None, 'quad'), may hold values from -2 to 2
- motion_gain: float32 [1280], replicated, may hold values from 0.1 to 1.9
Outputs:
- block_output: bfloat16 [64, 32, 1280], P('frame', 'quad')
- input_grad: bfloat16 [64, 32, 1280], P('frame', 'quad')
- weight_grad: float32 [4, 1280, 640], P(None, ('frame', 'quad'))
- gain_grad: float32 [1280], P(('frame', 'quad'))
All inputs are finite; a program needn't handle non-finite values.
Results may differ from a plain program's by a relative error of at most 0.03.
Values may be sent and summed in bfloat16 or wider, within the bound.
No kernel may reach another device: no remote copies, remote signals or barrier semaphores. Data moves between devices by JAX's collectives and lax.ppermute only.
A program may use at most 128 MiB of HBM per device.

v0:
```python
import functools
import math

import jax
import jax.numpy as jnp
from jax import lax
from jax.experimental import pallas as pl
from jax.experimental.pallas import tpu as pltpu
from jax.sharding import PartitionSpec as P

HEADS = 4
HEAD_DIM = 160
EPSILON = 1e-05
SCALE = HEAD_DIM ** (-0.5)
F32 = jnp.float32
BF16 = jnp.bfloat16


def log2(n):
    return int(n).bit_length() - 1


def dot(a, b):
    return jnp.dot(a, b, preferred_element_type=F32)


def dot_t(a, b):
    return lax.dot_general(a, b, (((1,), (1,)), ((), ())), preferred_element_type=F32)


def t_dot(a, b):
    return lax.dot_general(a, b, (((0,), (0,)), ((), ())), preferred_element_type=F32)


def normalize(values):
    average = jnp.mean(values, axis=-1, keepdims=True)
    centred = values - average
    inv_scale = lax.rsqrt(jnp.mean(centred * centred, axis=-1, keepdims=True) + EPSILON)
    return centred * inv_scale, inv_scale


def normalize_back(grad_rows, unit_rows, inv_scale, gain):
    scaled = grad_rows * gain
    first_mean = jnp.mean(scaled, axis=-1, keepdims=True)
    second_mean = jnp.mean(scaled * unit_rows, axis=-1, keepdims=True)
    return inv_scale * (scaled - first_mean - unit_rows * second_mean)


def iota(shape, dim):
    return lax.broadcasted_iota(jnp.int32, shape, dim)


def head_mask(dtype):
    lane = iota((1, HEADS * HEAD_DIM), 1)
    return [
        jnp.where((lane >= h * HEAD_DIM) & (lane < (h + 1) * HEAD_DIM), 1.0, 0.0).astype(dtype)
        for h in range(HEADS)
    ]


def stack_heads(rows):
    return jnp.concatenate([rows * mask for mask in head_mask(rows.dtype)], axis=0)


def fold_heads(stacked):
    rows = stacked.shape[0] // HEADS
    total = None
    for h, mask in enumerate(head_mask(F32)):
        piece = stacked[h * rows : (h + 1) * rows] * mask
        total = piece if total is None else total + piece
    return total


def probabilities(query_stack, keys, same):
    scores = dot_t(query_stack, keys) * SCALE
    if same is not None:
        scores = jnp.where(same, scores, -1e30)
    highest = jnp.max(scores, axis=-1, keepdims=True)
    expo = jnp.exp(scores - highest)
    return expo / jnp.sum(expo, axis=-1, keepdims=True)


def attend(query, keys, values, same):
    probs = probabilities(stack_heads(query), keys, same)
    return fold_heads(dot(probs.astype(BF16), values)).astype(BF16)


def attend_back(query, keys, values, grad, same, probs=None):
    query_stack = stack_heads(query)
    grad_stack = stack_heads(grad)
    if probs is None:
        probs = probabilities(query_stack, keys, same)
    grad_probs = dot_t(grad_stack, values)
    inner = jnp.sum(probs * grad_probs, axis=-1, keepdims=True)
    grad_scores = (probs * (grad_probs - inner) * SCALE).astype(BF16)
    grad_query = fold_heads(dot(grad_scores, keys)).astype(BF16)
    grad_key = t_dot(grad_scores, query_stack).astype(BF16)
    grad_value = t_dot(probs.astype(BF16), grad_stack).astype(BF16)
    return grad_query, grad_key, grad_value


def rows_to_sent(quad, nq, fr, pq, transposed):
    rows = nq * fr * pq
    out_dim = 1 if transposed else 0
    out = iota((rows, rows), out_dim)
    src = iota((rows, rows), 1 - out_dim)
    cell = out >> log2(nq * fr)
    other = (out >> log2(fr)) & (nq - 1)
    frame = out & (fr - 1)
    want = (((other - quad) & (nq - 1)) << log2(fr * pq)) + (frame << log2(pq)) + cell
    return jnp.where(want == src, 1.0, 0.0).astype(BF16)


def received_to_rows(quad, nq, nf, fr, transposed):
    rows = nq * nf * fr
    out_dim = 1 if transposed else 0
    out = iota((rows, rows), out_dim)
    src = iota((rows, rows), 1 - out_dim)
    step = out >> log2(nf * fr)
    device = (out >> log2(fr)) & (nf - 1)
    frame = out & (fr - 1)
    want = (device << log2(nq * fr)) + (((step + quad) & (nq - 1)) << log2(fr)) + frame
    return jnp.where(want == src, 1.0, 0.0).astype(BF16)


def own_lanes(values, quad, nq):
    width = values.shape[1] // nq
    picked = values[:, :width]
    for t in range(1, nq):
        picked = jnp.where(quad == t, values[:, t * width : (t + 1) * width], picked)
    return picked


def place_lanes(parts, quad, nq):
    placed = []
    for t in range(nq):
        piece = parts[t]
        for q in range(1, nq):
            piece = jnp.where(quad == q, parts[(t - q) % nq], piece)
        placed.append(piece)
    return jnp.concatenate(placed, axis=1)


def frame_groups(nq, fr, pq):
    size = max(1, min(fr, 128 // (nq * pq)))
    return [(start, size) for start in range(0, fr, size)]


def pick_group(rows, group, nq, fr, pq):
    start, size = group
    if size == fr:
        return rows
    cut = rows.reshape(nq, fr, pq, rows.shape[-1])[:, start : start + size]
    return cut.reshape(nq * size * pq, rows.shape[-1])


def join_groups(pieces, nq, fr, pq):
    if len(pieces) == 1:
        return pieces[0]
    size = fr // len(pieces)
    width = pieces[0].shape[-1]
    joined = jnp.concatenate([p.reshape(nq, size, pq, width) for p in pieces], axis=1)
    return joined.reshape(nq * fr * pq, width)


def same_frame(nq, size, pq):
    if size == 1:
        return None
    rows = nq * size * pq
    shape = (HEADS * rows, rows)
    left = (iota(shape, 0) >> log2(pq)) & (size - 1)
    right = (iota(shape, 1) >> log2(pq)) & (size - 1)
    return left == right


def row_of(ref):
    return ref[...].reshape(1, -1)


def flat(ref):
    value = ref[...]
    return value.reshape(-1, value.shape[-1])


def flat_wide(ref):
    value = ref[...].astype(F32)
    return value.reshape(-1, value.shape[-1])


def spread(rows, like):
    return rows.reshape(like.shape).astype(like.dtype)


def spatial_kernel(dims, *refs):
    nq, nf, fr, pq = dims
    quad, xs, refs = refs[0][0], refs[1 : 1 + nq], refs[1 + nq :]
    gain1, gain2, pos, weights, kept_out, send_out = refs
    width = HEADS * HEAD_DIM
    wide = jnp.concatenate([flat_wide(x) for x in xs], axis=0)
    unit, _ = normalize(wide)
    normed = (unit * row_of(gain1)).astype(BF16)
    query = dot(normed, weights[0]).astype(BF16)
    keys = dot(normed, weights[1]).astype(BF16)
    values = dot(normed, weights[2]).astype(BF16)
    for i, part in enumerate((query, keys, values)):
        kept_out[:, i * width : (i + 1) * width] = part
    pieces = []
    for group in frame_groups(nq, fr, pq):
        same = same_frame(nq, group[1], pq)
        cut = [pick_group(part, group, nq, fr, pq) for part in (query, keys, values)]
        pieces.append(attend(*cut, same))
    out = join_groups(pieces, nq, fr, pq)
    hidden = (wide + dot_t(out, weights[3])).astype(BF16)
    kept_out[:, 3 * width :] = hidden
    unit_two, _ = normalize(hidden.astype(F32))
    table = jnp.broadcast_to(pos[...][:, None, :], (fr, pq, pos.shape[-1]))
    table = table.reshape(fr * pq, pos.shape[-1])
    table = jnp.concatenate([table] * nq, axis=0)
    normed_two = own_lanes(unit_two * row_of(gain2) + table, quad, nq).astype(BF16)
    send_out[...] = spread(dot(rows_to_sent(quad, nq, fr, pq, False), normed_two), send_out)


def order_kernel(dims, geo, cot, weights, send_out):
    nq, nf, fr, pq = dims
    order = rows_to_sent(geo[0], nq, fr, pq, False)[:, : fr * pq]
    send_out[...] = spread(dot(order, own_lanes(flat(cot), geo[0], nq)), send_out)


def join_kernel(dims, geo, normed, own_part, *refs):
    nq, nf, fr, pq = dims
    cots, send_out = refs[:-1], refs[-1]
    order = rows_to_sent(geo[0], nq, fr, pq, False)[:, fr * pq :]
    rows = own_lanes(jnp.concatenate([flat(c) for c in cots], axis=0), geo[0], nq)
    total = own_part[...].astype(F32) + dot(order, rows).reshape(own_part.shape)
    send_out[:, : nq * fr, :] = normed[...]
    send_out[:, nq * fr :, :] = total.astype(BF16)


def sent_part(received, i, rows):
    part = received[:, i * rows : (i + 1) * rows, :].astype(F32)
    return part.reshape(-1, part.shape[-1]).astype(BF16)


def motion_kernel(dims, geo, received, weights, own_out, *sends):
    nq, nf, fr, pq = dims
    order = received_to_rows(geo[0], nq, nf, fr, False)
    normed, cot = [dot(order, sent_part(received, i, nq * fr)).astype(BF16) for i in range(2)]
    tokens = nf * fr
    for k in range(4):
        width = weights.shape[-1]
        lanes = slice(k * width, (k + 1) * width)
        product = dot(normed if k < 3 else cot, weights[k])
        own_out[:, lanes] = product[:tokens]
        for s, send in enumerate(sends):
            send[:, lanes] = product[(s + 1) * tokens : (s + 2) * tokens].astype(BF16)


def quarter_of(four):
    return ((four & 1) << 1) | (four >> 1)


def quarter_lanes(values, quarter):
    width = values.shape[1] // 4
    picked = values[:, :width]
    for t in range(1, 4):
        picked = jnp.where(quarter == t, values[:, t * width : (t + 1) * width], picked)
    return picked


def cut_kernel(dims, geo, received, *outs):
    nq, nf, fr, pq = dims
    order = received_to_rows(geo[0], nq, nf, fr, False)
    for i in range(2):
        rows = dot(order, sent_part(received, i, nq * fr))
        for d in range(4):
            outs[d][i] = quarter_lanes(rows, quarter_of(geo[1] ^ d)).astype(BF16)


def table_kernel(dims, geo, out):
    shape = out.shape
    lane = iota(shape, 1)
    freq = jnp.exp((lane >> 1).astype(F32) * (-2.0 * math.log(10000.0) / shape[1]))
    turn = (lane & 1).astype(F32) * (0.5 * math.pi)
    out[...] = jnp.sin(iota(shape, 0).astype(F32) * freq + turn)


def temporal_kernel(dims, *refs):
    nq, nf, fr, pq = dims
    parts, out = refs[:nq], refs[nq]
    width = HEADS * HEAD_DIM
    total = parts[0][...]
    for part in parts[1:]:
        total = total + part[...].astype(F32)
    query, keys, values, grad = [
        total[:, k * width : (k + 1) * width].astype(BF16) for k in range(4)
    ]
    probs = probabilities(stack_heads(query), keys, None)
    motion_out = fold_heads(dot(probs.astype(BF16), values)).astype(BF16)
    grads = attend_back(query, keys, values, grad, None, probs)
    for k, piece in enumerate(grads + (motion_out,)):
        out[:, k * width : (k + 1) * width] = piece


def part_of(terms, k):
    width = HEADS * HEAD_DIM
    return jnp.concatenate([t[:, k * width : (k + 1) * width] for t in terms], axis=0)


def back_kernel(dims, quad_ref, *refs):
    nq, nf, fr, pq = dims
    terms, (weights, out, quarter_out) = refs[:nq], refs[nq:]
    order = received_to_rows(quad_ref[0], nq, nf, fr, True)
    quarter, rows = quarter_of(quad_ref[1]), quarter_out.shape[1]
    for k in range(3):
        if rows % 16 == 0:
            own = weights[k, pl.ds(pl.multiple_of(quarter * rows, 16), rows), :]
        else:
            wide = weights[k].astype(F32)
            own = wide[:rows]
            for t in range(1, 4):
                own = jnp.where(quarter == t, wide[t * rows : (t + 1) * rows], own)
            own = own.astype(BF16)
        quarter_out[k] = own
    grad = None
    for k in range(3):
        product = dot_t(part_of(terms, k), weights[k])
        grad = product if grad is None else grad + product
    delta = dot_t(part_of(terms, 3), weights[3])
    for i, rows in enumerate((grad, delta)):
        rows = dot(order, rows.astype(BF16))
        out[:, i * nq * fr : (i + 1) * nq * fr, :] = rows.reshape(nf, nq * fr, -1).astype(BF16)


def weight_sums(geo, nq, normed, cot, weights, pos, terms):
    products, grad = [], None
    for k in range(4):
        right = part_of(terms, k)
        products.append(t_dot(normed if k < 3 else cot, right))
        if k < 3:
            back = dot_t(right, weights[k])
            grad = back if grad is None else grad + back
    table = quarter_lanes(own_lanes(pos[...], geo[0], nq), quarter_of(geo[1]))
    table = jnp.concatenate([table] * len(terms), axis=0)
    return products, jnp.sum(grad * (normed.astype(F32) - table), axis=0, keepdims=True)


def first_weight_kernel(dims, geo, *refs):
    nq, nf, fr, pq = dims
    factors, (weights, pos), refs = refs[:4], refs[4:6], refs[6:]
    terms, (blocks, gain_out, late_out) = refs[: 2 * nq + 2], refs[2 * nq + 2 :]
    _, stage, block, _ = blocks.shape
    tokens = nf * fr
    left = []
    for i in range(2):
        early = [factors[0][i], factors[1][i], factors[2][i, :tokens], factors[3][i, :tokens]]
        left.append(jnp.concatenate(early, axis=0))
        late = [factors[2][i, tokens:], factors[3][i, tokens:]]
        late_out[i] = jnp.concatenate(late, axis=0)
    products, gain_out[...] = weight_sums(geo, nq, *left, weights, pos, terms)
    for k in range(4):
        for z in range(stage):
            blocks[k, z] = products[k][z * block : (z + 1) * block]


def second_weight_kernel(dims, geo, sums, gain_sum, left, weights, pos, gain2, *refs):
    nq, nf, fr, pq = dims
    terms, outs, blocks = refs[: 2 * nq - 2], refs[2 * nq - 2 : -1], refs[-1]
    _, stage, block, width = blocks.shape
    products, gain = weight_sums(geo, nq, left[0], left[1], weights, pos, terms)
    for k in range(4):
        for z in range(stage):
            blocks[k, z] = sums[k, z] + products[k][z * block : (z + 1) * block]
    gain = gain + gain_sum[...]
    rows = gain.shape[1]
    gain = gain / quarter_lanes(own_lanes(row_of(gain2), geo[0], nq), quarter_of(geo[1]))
    extra = jnp.concatenate([gain, jnp.zeros((1, width - rows), F32)], axis=1)
    extra = jnp.where(iota((8, width), 0) == 0, extra, 0.0)
    for r in range(stage):
        z = (geo[2] + r) & (stage - 1)
        rows_out = jnp.concatenate([blocks[k, z] for k in range(4)] + [extra], axis=0)
        outs[r][...] = rows_out.astype(BF16)


def middle_kernel(dims, *refs):
    nq, nf, fr, pq = dims
    quad, received, cots = refs[0][0], refs[1 : 1 + nq], refs[1 + nq : 1 + 2 * nq]
    kept, gain2, block_out, grad_out = refs[1 + 2 * nq :]
    own = fr * pq
    order = rows_to_sent(quad, nq, fr, pq, True)

    def lanes(i):
        parts = []
        for r in received:
            parts.append(dot(order, sent_part(r, i, nq * fr)))
        return place_lanes(parts, quad, nq)

    hidden = kept[:, 3 * HEADS * HEAD_DIM :].astype(F32)
    grad_normed, delta = lanes(0), lanes(1)
    block_out[...] = spread(hidden[:own] + delta[:own], block_out)
    unit_two, inv_two = normalize(hidden)
    cot = jnp.concatenate([flat_wide(c) for c in cots], axis=0)
    back = normalize_back(grad_normed, unit_two, inv_two, row_of(gain2))
    grad_out[...] = (cot + back).astype(BF16)


def tail_kernel(dims, grad_hidden, xs, kept, gain1, weights, in_grad):
    nq, nf, fr, pq = dims
    own, width = fr * pq, HEADS * HEAD_DIM
    grad_out = dot(grad_hidden[...], weights[3]).astype(BF16)
    parts = [kept[:, i * width : (i + 1) * width] for i in range(3)] + [grad_out]
    pieces = []
    for group in frame_groups(nq, fr, pq):
        same = same_frame(nq, group[1], pq)
        pieces.append(attend_back(*[pick_group(p, group, nq, fr, pq) for p in parts], same))
    grads = [join_groups([p[i] for p in pieces], nq, fr, pq)[:own] for i in range(3)]
    grad_one = dot_t(grads[0], weights[0]) + dot_t(grads[1], weights[1]) + dot_t(grads[2], weights[2])
    unit_one, inv_one = normalize(flat_wide(xs))
    back = normalize_back(grad_one, unit_one, inv_one, row_of(gain1))
    in_grad[...] = spread(grad_hidden[...][:own].astype(F32) + back, in_grad)


def call(kernel, name, outs, args, vmem, micros, scratch=()):
    in_specs = []
    for arg in args:
        space = pltpu.SMEM if arg.dtype == jnp.int32 else pltpu.VMEM
        in_specs.append(pl.BlockSpec(memory_space=space))
    return list(
        pl.pallas_call(
            kernel,
            out_shape=outs,
            in_specs=in_specs,
            out_specs=[pl.BlockSpec(memory_space=pltpu.VMEM) for _ in outs],
            scratch_shapes=list(scratch),
            compiler_params=pltpu.CompilerParams(vmem_limit_bytes=vmem * 1024 * 1024),
            cost_estimate=pl.CostEstimate(
                flops=int(micros * 1e9), bytes_accessed=2**20, transcendentals=0
            ),
            name=name,
        )(*args)
    )


def after(value, *others):
    return lax.optimization_barrier((value,) + others)[0]


def sds(*shape, dtype=BF16):
    return jax.ShapeDtypeStruct(shape, dtype)


def positional(first, frames, channels):
    frame_pos = (first + lax.broadcasted_iota(jnp.int32, (frames, channels), 0)).astype(F32)
    lane = lax.broadcasted_iota(jnp.int32, (frames, channels), 1)
    freq_index = (lane >> 1).astype(F32)
    phases = frame_pos * jnp.exp(freq_index * (-2.0 * math.log(10000.0) / channels))
    return jnp.sin(phases + (lane & 1).astype(F32) * (0.5 * math.pi))


def local(nq, nf, activations, cotangent, spatial_weights, spatial_gain, motion_weights, motion_gain):
    fr, pq, channels = activations.shape
    dims = (nq, nf, fr, pq)
    width = spatial_weights.shape[-1]
    half = channels // nq
    rows = nq * fr * pq
    tokens = nf * fr
    small = 16 if rows <= 256 else 40
    big = 16 if rows <= 256 else 52
    quad = lax.axis_index("quad")
    frame = lax.axis_index("frame")


    def from_quad(x, s):
        return lax.ppermute(x, "quad", [((d + s) % nq, d) for d in range(nq)])

    def to_quad(x, s):
        return lax.ppermute(x, "quad", [(d, (d + s) % nq) for d in range(nq)])

    def swap(x):
        return lax.all_to_all(x, "frame", split_axis=0, concat_axis=0, tiled=True)

    def run(kernel, name, outs, args, micros, vmem=small, **options):
        kernel = functools.partial(kernel, dims)
        return call(kernel, name, outs, args, vmem, micros, **options)

    def move(x, pairs):
        return lax.ppermute(x, "frame", pairs)

    geo = jnp.stack([quad, frame % 4, frame // 4]).astype(jnp.int32)

    def flipped(bits):
        return [(g, g ^ bits) for g in range(nf)]

    ring = [(g, (g + 4) % nf) for g in range(nf)]

    gain1, gain2 = spatial_gain, motion_gain
    sent = sds(nf, nq * fr, half)
    acts = [activations] + [from_quad(activations, s) for s in range(1, nq)]
    both = sds(nf, 2 * nq * fr, half)
    (own_part,) = run(
        order_kernel, "order_cotangent", [sent], [geo, cotangent, spatial_weights], 0.5, big
    )
    cot_later = after(cotangent, acts[-1])
    cots = [cotangent] + [from_quad(cot_later, s) for s in range(1, nq)]
    pos = positional(frame * fr, fr, channels)
    kept, normed = run(
        spatial_kernel,
        "spatial_forward",
        [sds(rows, 3 * width + channels), sent],
        [geo] + acts + [gain1, gain2, pos, spatial_weights],
        3,
        big,
    )
    (send,) = run(join_kernel, "join_sent", [both], [geo, normed, own_part] + cots[1:], 0.5)
    received = swap(send)
    parts = run(
        motion_kernel,
        "motion_projection",
        [sds(tokens, 4 * width, dtype=F32)] + [sds(tokens, 4 * width)] * (nq - 1),
        [geo, received, motion_weights],
        1.5,
    )
    parts = [parts[0]] + [to_quad(p, s + 1) for s, p in enumerate(parts[1:])]
    (terms,) = run(temporal_kernel, "temporal_attention", [sds(tokens, 4 * width)], parts, 2)
    factors = run(
        cut_kernel,
        "cut_factors",
        [sds(2, rows, half // 4)] * 4,
        [geo, after(received, terms)],
        0.5,
    )
    (table,) = run(
        table_kernel,
        "positional_table",
        [sds(tokens, channels, dtype=F32)],
        [after(geo, terms)],
        1.5,
    )
    all_terms = [terms] + [after(from_quad(terms, s), factors[0], table) for s in range(1, nq)]
    pair_terms = [move(t, flipped(2)) for t in all_terms]
    core_terms = [move(t, flipped(1)) for t in all_terms]
    factors = [factors[0]] + [move(factors[d], flipped(d)) for d in range(1, 4)]
    back_send, quarter = run(
        back_kernel,
        "temporal_back_projection",
        [sds(nf, 2 * nq * fr, half), sds(3, half // 4, width)],
        [geo] + all_terms + [motion_weights],
        3,
    )
    last_terms = [move(t, flipped(1)) for t in pair_terms[:1]]

    stage, block = nf // 4, half // nf
    sums, gain_sum, late_left = run(
        first_weight_kernel,
        "weight_terms_first_tokens",
        [
            sds(4, stage, block, width, dtype=F32),
            sds(1, half // 4, dtype=F32),
            sds(2, 2 * (nq - 1) * tokens, half // 4),
        ],
        [geo] + factors + [quarter, table] + all_terms + core_terms
        + pair_terms[:1] + last_terms,
        3,
    )
    late_terms = [after(t, back_send, sums) for t in pair_terms[1:]]
    late_terms += [move(t, flipped(1)) for t in late_terms]
    parts_w = run(
        second_weight_kernel,
        "weight_terms_last_tokens",
        [sds(4 * block + 8, width)] * stage,
        [geo, sums, gain_sum, late_left, quarter, table, gain2] + late_terms,
        2,
        scratch=[pltpu.VMEM((4, stage, block, width), F32)],
    )

    def add(a, b):
        return (a.astype(F32) + b.astype(F32)).astype(BF16)

    back_recv = swap(back_send)
    backs = [back_recv] + [from_quad(back_recv, s) for s in range(1, nq)]
    block_output, grad_hidden = run(
        middle_kernel,
        "block_output_hidden_gradient",
        [sds(fr, pq, channels), sds(rows, channels)],
        [geo] + backs + cots + [kept, gain2],
        6,
        big,
    )
    total = parts_w[stage - 1]
    for step in range(1, stage):
        if step == stage - 2:
            total = after(total, back_recv)
        moved = move(total, ring)
        if step == stage - 1:
            moved = after(moved, grad_hidden)
        total = add(moved, parts_w[stage - 1 - step])
    final = []
    for g in range(nf):
        for q in range(nq):
            j = quarter_of(g % 4) * stage + g // 4
            final.append((g * nq + q, nf * q + j))
    grad_hidden = after(grad_hidden, total)
    total = lax.ppermute(total, ("frame", "quad"), final)
    (input_grad,) = run(
        tail_kernel,
        "spatial_backward",
        [sds(fr, pq, channels)],
        [grad_hidden, activations, kept, gain1, spatial_weights],
        3.5,
        big,
    )
    everyone = nf * nq
    factor = 1.0 / math.sqrt(everyone * fr * pq)
    weight_grad = total[: 4 * block].reshape(4, block, width).astype(F32) * factor
    place = ((frame * nq + quad) % stage) * block
    gain_grad = lax.dynamic_slice(total[4 * block], (place,), (block,)).astype(F32) * factor
    return block_output, input_grad, weight_grad, gain_grad


def solution(mesh):
    in_specs = (
        P("frame", "quad", None),
        P("frame", "quad", None),
        P(),
        P(),
        P(None, "quad", None),
        P(),
    )
    out_specs = (
        P("frame", "quad", None),
        P("frame", "quad", None),
        P(None, ("frame", "quad"), None),
        P(("frame", "quad")),
    )
    body = functools.partial(local, mesh.shape["quad"], mesh.shape["frame"])
    return jax.shard_map(
        body, mesh=mesh, in_specs=in_specs, out_specs=out_specs, check_vma=False
    )
```

profile of v0, /device:TPU:1, one launch (start us, length us, event | category | flops | bytes accessed | tf_op | source)
XLA Modules:
  0.0 116.6 jit_solution(4650209049570945139)
XLA Ops:
  0.6 2.1 %collective-permute-start = (bf16[4,16,1280]{2,1,0:T(8,128)(2,1)}, bf16[4,16,1280]{2,1,0:T(8,128)(2,1)S(1)}, u32[]{:S(2)}, u32[]{:S(2)}) collective-permute-start(bf16[4,16,1280]{2,1,0:T(8,128)(2,1)} %xs.1), channel_id=1, source_target_pairs={{1,0},{0,1},{3,2},{2,3},{5,4},{4,5},{7,6},{6,7},{9,8},{8,9},{11,10... | collective-permute-start | bytes 491528 | tf_op jit(solution)/shard_map/ppermute | solution.py:473
  3.1 2.9 %copy-done = bf16[4,1280,640]{2,1,0:T(8,128)(2,1)S(1)} copy-done((bf16[4,1280,640]{2,1,0:T(8,128)(2,1)S(1)}, bf16[4,1280,640]{2,1,0:T(8,128)(2,1)}, u32[]{:S(2)}) %copy-start) | copy-done | bytes 6553624
  8.0 1.7 %copy-done.1 = bf16[4,1280,640]{2,1,0:T(8,128)(2,1)S(1)} copy-done((bf16[4,1280,640]{2,1,0:T(8,128)(2,1)S(1)}, bf16[4,1280,640]{2,1,0:T(8,128)(2,1)}, u32[]{:S(2)}) %copy-start.1) | copy-done | bytes 6553624
  9.8 3.4 %spatial_forward.1 = (bf16[128,3200]{1,0:T(8,128)(2,1)S(1)}, bf16[16,8,640]{2,1,0:T(8,128)(2,1)S(1)}) custom-call(s32[3]{0:T(128)S(1)} %pad_add_fusion.refs_0_.geo.quad_ref, bf16[4,16,1280]{2,1,0:T(8,128)(2,1)S(1)} %copy-done.5, bf16[4,16,1280]{2,1,0:T(8,128)(2,1)S(1)} %collective-permute-done.refs_2_, f32[1280]{0:T(1024)S(1)} %copy-done.9, ...), custom_call_target="tpu_custom_call" | custom-call | flops 3000000000 | bytes 1048576 | tf_op jit(solution)/shard_map/spatial_forward/pallas_call | solution.py:428
  14.0 17.5 %all_to_all.10.received = bf16[16,16,640]{2,1,0:T(8,128)(2,1)S(1)} all-to-all(bf16[16,16,640]{2,1,0:T(8,128)(2,1)S(1)} %join_sent.1), channel_id=1, replica_groups=mesh['frame'=16,'quad'=2] {'frame'}, dimensions={0} | all-to-all | bytes 655360 | tf_op jit(solution)/shard_map/all_to_all | solution.py:479
  31.5 1.5 %motion_projection.1 = (f32[64,2560]{1,0:T(8,128)S(1)}, bf16[64,2560]{1,0:T(8,128)(2,1)S(1)}) custom-call(s32[3]{0:T(128)S(1)} %pad_add_fusion.refs_0_.geo.quad_ref, bf16[16,16,640]{2,1,0:T(8,128)(2,1)S(1)} %all_to_all.10.received, bf16[4,640,640]{2,1,0:T(8,128)(2,1)S(1)} %copy-done.4), custom_call_target="tpu_custom_call" | custom-call | flops 1500000000 | bytes 1048576 | tf_op jit(solution)/shard_map/motion_projection/pallas_call | solution.py:428
  33.7 8.3 %collective-permute-done.2.refs_1_ = bf16[64,2560]{1,0:T(8,128)(2,1)S(1)} collective-permute-done((bf16[64,2560]{1,0:T(8,128)(2,1)S(1)}, bf16[64,2560]{1,0:T(8,128)(2,1)S(1)}, u32[]{:S(2)}, u32[]{:S(2)}) %collective-permute-start.2) | collective-permute-done | bytes 327712 | tf_op jit(solution)/shard_map/ppermute | solution.py:476
  48.4 1.6 %positional_table.1.refs_5_.pos = f32[64,1280]{1,0:T(8,128)S(1)} custom-call(s32[3]{0:T(128)S(1)} %pad_add_fusion.refs_0_.geo.quad_ref), custom_call_target="tpu_custom_call" | custom-call | flops 1500000000 | bytes 1048576 | tf_op jit(solution)/shard_map/positional_table/pallas_call | solution.py:428
  51.1 2.2 %collective-permute-start.9 = (bf16[64,2560]{1,0:T(8,128)(2,1)S(1)}, bf16[64,2560]{1,0:T(8,128)(2,1)S(1)}, u32[]{:S(2)}, u32[]{:S(2)}) collective-permute-start(bf16[64,2560]{1,0:T(8,128)(2,1)S(1)} %collective-permute-done.3.refs_1_.refs_7_), channel_id=1, source_target_pairs={{0,2},{2,0},{4,6},{6,4},{8,10},{10,8},{12,14},{14,12},{16,18},{18,... | collective-permute-start | bytes 983048 | tf_op jit(solution)/shard_map/ppermute | solution.py:486
  53.3 2.0 %collective-permute-start.11 = (bf16[64,2560]{1,0:T(8,128)(2,1)S(1)}, bf16[64,2560]{1,0:T(8,128)(2,1)S(1)}, u32[]{:S(2)}, u32[]{:S(2)}) collective-permute-start(bf16[64,2560]{1,0:T(8,128)(2,1)S(1)} %collective-permute-done.10.refs_10_), channel_id=1, source_target_pairs={{0,2},{2,0},{4,6},{6,4},{8,10},{10,8},{12,14},{14,12},{16,18},{18,... | collective-permute-start | bytes 983048 | tf_op jit(solution)/shard_map/ppermute | solution.py:486
  56.6 2.5 %temporal_back_projection.1 = (bf16[16,16,640]{2,1,0:T(8,128)(2,1)}, bf16[3,160,640]{2,1,0:T(8,128)(2,1)S(1)}) custom-call(s32[3]{0:T(128)S(1)} %pad_add_fusion.refs_0_.geo.quad_ref, bf16[64,2560]{1,0:T(8,128)(2,1)S(1)} %temporal_attention.1.refs_0_.refs_6_, bf16[64,2560]{1,0:T(8,128)(2,1)S(1)} %collective-permute-done.3.refs_1_.refs_7_, ...), custom_call_target="tpu_custom_call" | custom-call | flops 3000000000 | bytes 1048576 | tf_op jit(solution)/shard_map/temporal_back_projection/pallas_call | solution.py:428
  59.1 1.9 %collective-permute-done.7.refs_3_ = bf16[2,128,160]{2,1,0:T(8,128)(2,1)S(1)} collective-permute-done((bf16[2,128,160]{2,1,0:T(8,128)(2,1)S(1)}, bf16[2,128,160]{2,1,0:T(8,128)(2,1)S(1)}, u32[]{:S(2)}, u32[]{:S(2)}) %collective-permute-start.7) | collective-permute-done | bytes 81952 | tf_op jit(solution)/shard_map/ppermute | solution.py:486
  61.0 1.7 %weight_terms_first_tokens.1 = (f32[4,4,40,640]{3,2,1,0:T(8,128)S(1)}, f32[1,160]{1,0:T(1,128)S(1)}, bf16[2,128,160]{2,1,0:T(8,128)(2,1)S(1)}) custom-call(s32[3]{0:T(128)S(1)} %pad_add_fusion.refs_0_.geo.quad_ref, bf16[2,128,160]{2,1,0:T(8,128)(2,1)S(1)} %get-tuple-element.36.refs_0_, bf16[2,128,160]{2,1,0:T(8,128)(2,1)S(1)} %collective-permute-done.5.refs_1_, ...), custom_call_target="tpu_custom_call" | custom-call | flops 3000000000 | bytes 1048576 | tf_op jit(solution)/shard_map/weight_terms_first_tokens/pallas_call | solution.py:428
  63.5 3.6 %collective-permute-done.12.refs_0_ = bf16[64,2560]{1,0:T(8,128)(2,1)S(1)} collective-permute-done((bf16[64,2560]{1,0:T(8,128)(2,1)S(1)}, bf16[64,2560]{1,0:T(8,128)(2,1)S(1)}, u32[]{:S(2)}, u32[]{:S(2)}) %collective-permute-start.12) | collective-permute-done | bytes 327712 | tf_op jit(solution)/shard_map/ppermute | solution.py:486
  68.1 3.6 %all-to-all-start.1 = ((bf16[16,16,640]{2,1,0:T(8,128)(2,1)}), bf16[16,16,640]{2,1,0:T(8,128)(2,1)S(1)}, u32[]{:S(2)}, u32[]{:S(2)}) async-start(bf16[16,16,640]{2,1,0:T(8,128)(2,1)} %get-tuple-element.39), calls=%async_computation.1 | async-start | bytes 655360 | tf_op jit(solution)/shard_map/all_to_all | solution.py:479
  74.7 1.5 %weight_terms_last_tokens.1 = (bf16[168,640]{1,0:T(8,128)(2,1)S(1)}, bf16[168,640]{1,0:T(8,128)(2,1)S(1)}, bf16[168,640]{1,0:T(8,128)(2,1)S(1)}, bf16[168,640]{1,0:T(8,128)(2,1)S(1)}) custom-call(s32[3]{0:T(128)S(1)} %pad_add_fusion.refs_0_.geo.quad_ref, f32[4,4,40,640]{3,2,1,0:T(8,128)S(1)} %get-tuple-element.47.sums, ...), custom_call_target="tpu_custom_call" | custom-call | flops 2000000000 | bytes 1048576 | tf_op jit(solution)/shard_map/weight_terms_last_tokens/pallas_call | solution.py:428
  76.1 1.4 %collective-permute-start.14 = (bf16[168,640]{1,0:T(8,128)(2,1)S(1)}, bf16[168,640]{1,0:T(8,128)(2,1)S(1)}, u32[]{:S(2)}, u32[]{:S(2)}) collective-permute-start(bf16[168,640]{1,0:T(8,128)(2,1)S(1)} %get-tuple-element.51), channel_id=1, source_target_pairs={{0,8},{2,10},{4,12},{6,14},{8,16},{10,18},{12,20},{14,22},{16,24},... | collective-permute-start | bytes 645128 | tf_op jit(solution)/shard_map/ppermute | solution.py:486
  77.6 8.2 %collective-permute-done.14 = bf16[168,640]{1,0:T(8,128)(2,1)S(1)} collective-permute-done((bf16[168,640]{1,0:T(8,128)(2,1)S(1)}, bf16[168,640]{1,0:T(8,128)(2,1)S(1)}, u32[]{:S(2)}, u32[]{:S(2)}) %collective-permute-start.14) | collective-permute-done | bytes 215072 | tf_op jit(solution)/shard_map/ppermute | solution.py:486
  88.6 6.6 %collective-permute-done.15 = bf16[168,640]{1,0:T(8,128)(2,1)} collective-permute-done((bf16[168,640]{1,0:T(8,128)(2,1)}, bf16[168,640]{1,0:T(8,128)(2,1)}, u32[]{:S(2)}, u32[]{:S(2)}) %collective-permute-start.15) | collective-permute-done | bytes 215072 | tf_op jit(solution)/shard_map/ppermute | solution.py:486
  99.5 2.2 %block_output_hidden_gradient.1 = (bf16[4,16,1280]{2,1,0:T(8,128)(2,1)}, bf16[128,1280]{1,0:T(8,128)(2,1)S(1)}) custom-call(s32[3]{0:T(128)S(1)} %pad_add_fusion.refs_0_.geo.quad_ref, bf16[16,16,640]{2,1,0:T(8,128)(2,1)S(1)} %all-to-all-done.1.refs_1_, bf16[16,16,640]{2,1,0:T(8,128)(2,1)} %collective-permute-done.4.refs_2_, ...), custom_call_target="tpu_custom_call" | custom-call | flops 6000000000 | bytes 1048576 | tf_op jit(solution)/shard_map/block_output_hidden_gradient/pallas_call | solution.py:428
  101.7 1.7 %collective-permute-done.16 = bf16[168,640]{1,0:T(8,128)(2,1)S(1)} collective-permute-done((bf16[168,640]{1,0:T(8,128)(2,1)S(1)}, bf16[168,640]{1,0:T(8,128)(2,1)S(1)}, u32[]{:S(2)}, u32[]{:S(2)}) %collective-permute-start.16) | collective-permute-done | bytes 215072 | tf_op jit(solution)/shard_map/ppermute | solution.py:486
  103.5 2.4 %collective-permute-start.17 = (bf16[168,640]{1,0:T(8,128)(2,1)S(1)}, bf16[168,640]{1,0:T(8,128)(2,1)S(1)}, u32[]{:S(2)}, u32[]{:S(2)}) collective-permute-start(bf16[168,640]{1,0:T(8,128)(2,1)S(1)} %add_convert_fusion), channel_id=1, source_target_pairs={{0,0},{1,16},{2,8},{3,24},{4,4},{5,20},{6,12},{7,28},{8,1},{9,17},... | collective-permute-start | bytes 645128 | tf_op jit(solution)/shard_map/ppermute | solution.py:602
  105.9 4.1 %spatial_backward.1 = bf16[4,16,1280]{2,1,0:T(8,128)(2,1)} custom-call(bf16[128,1280]{1,0:T(8,128)(2,1)S(1)} %get-tuple-element.57.grad_hidden, bf16[4,16,1280]{2,1,0:T(8,128)(2,1)S(1)} %copy-done.5, bf16[128,3200]{1,0:T(8,128)(2,1)S(1)} %copy-done.11, f32[1280]{0:T(1024)S(1)} %copy-done.9, bf16[4,1280,640]{2,1,0:T(8,128)(2,1)S(1)} %bitcast.7), custom_call_target="tpu_custom_call" | custom-call | flops 3500000000 | bytes 1048576 | tf_op jit(solution)/shard_map/spatial_backward/pallas_call | solution.py:428
  110.0 5.3 %collective-permute-done.17 = bf16[168,640]{1,0:T(8,128)(2,1)S(1)} collective-permute-done((bf16[168,640]{1,0:T(8,128)(2,1)S(1)}, bf16[168,640]{1,0:T(8,128)(2,1)S(1)}, u32[]{:S(2)}, u32[]{:S(2)}) %collective-permute-start.17) | collective-permute-done | bytes 215072 | tf_op jit(solution)/shard_map/ppermute | solution.py:602
  (78 shorter events, 25.9 us)
Async XLA Ops:
  0.6 7.0 %collective-permute-start = (bf16[4,16,1280]{2,1,0:T(8,128)(2,1)}, bf16[4,16,1280]{2,1,0:T(8,128)(2,1)S(1)}, u32[]{:S(2)}, u32[]{:S(2)}) collective-permute-start(bf16[4,16,1280]{2,1,0:T(8,128)(2,1)} %xs.1), channel_id=1, source_target_pairs={{1,0},{0,1},{3,2},{2,3},{5,4},{4,5},{7,6},{6,7},{9,8},{8,9},{11,10... | collective-permute-start | bytes 491528 | tf_op jit(solution)/shard_map/ppermute | solution.py:473
  7.6 23.9 %copy-start.4 = (bf16[4,640,640]{2,1,0:T(8,128)(2,1)S(1)}, bf16[4,640,640]{2,1,0:T(8,128)(2,1)}, u32[]{:S(2)}) copy-start(bf16[4,640,640]{2,1,0:T(8,128)(2,1)} %refs_2_.1) | copy-start | bytes 9830404
  7.6 5.6 %collective-permute-start.1 = (bf16[4,16,1280]{2,1,0:T(8,128)(2,1)S(1)}, bf16[4,16,1280]{2,1,0:T(8,128)(2,1)S(1)}, u32[]{:S(2)}, u32[]{:S(2)}) collective-permute-start(bf16[4,16,1280]{2,1,0:T(8,128)(2,1)S(1)} %copy-done.2), channel_id=1, source_target_pairs={{1,0},{0,1},{3,2},{2,3},{5,4},{4,5},{7,6},{6,7},{9,8},{8,9},{11,10... | collective-permute-start | bytes 491528 | tf_op jit(solution)/shard_map/ppermute | solution.py:473
  13.2 19.8 %copy-start.10 = (bf16[128,3200]{1,0:T(8,128)(2,1)}, bf16[128,3200]{1,0:T(8,128)(2,1)S(1)}, u32[]{:S(2)}) copy-start(bf16[128,3200]{1,0:T(8,128)(2,1)S(1)} %get-tuple-element.40.refs_5_.kept) | copy-start | bytes 2457604
  13.2 19.8 %copy-start.6 = (bf16[4,16,1280]{2,1,0:T(8,128)(2,1)}, bf16[4,16,1280]{2,1,0:T(8,128)(2,1)S(1)}, u32[]{:S(2)}) copy-start(bf16[4,16,1280]{2,1,0:T(8,128)(2,1)S(1)} %collective-permute-done.1.refs_0_.refs_4_) | copy-start | bytes 491524
  33.0 8.9 %collective-permute-start.2 = (bf16[64,2560]{1,0:T(8,128)(2,1)S(1)}, bf16[64,2560]{1,0:T(8,128)(2,1)S(1)}, u32[]{:S(2)}, u32[]{:S(2)}) collective-permute-start(bf16[64,2560]{1,0:T(8,128)(2,1)S(1)} %get-tuple-element.34), channel_id=1, source_target_pairs={{0,1},{1,0},{2,3},{3,2},{4,5},{5,4},{6,7},{7,6},{8,9},{9,8},{10,11... | collective-permute-start | bytes 983048 | tf_op jit(solution)/shard_map/ppermute | solution.py:476
  43.1 8.0 %collective-permute-start.3 = (bf16[64,2560]{1,0:T(8,128)(2,1)S(1)}, bf16[64,2560]{1,0:T(8,128)(2,1)S(1)}, u32[]{:S(2)}, u32[]{:S(2)}) collective-permute-start(bf16[64,2560]{1,0:T(8,128)(2,1)S(1)} %temporal_attention.1.refs_0_.refs_6_), channel_id=1, source_target_pairs={{1,0},{0,1},{3,2},{2,3},{5,4},{4,5},{7,6},{6,7},{9,8},{8,9},{11,10... | collective-permute-start | bytes 983048 | tf_op jit(solution)/shard_map/ppermute | solution.py:473
  43.7 9.5 %collective-permute-start.10 = (bf16[64,2560]{1,0:T(8,128)(2,1)S(1)}, bf16[64,2560]{1,0:T(8,128)(2,1)S(1)}, u32[]{:S(2)}, u32[]{:S(2)}) collective-permute-start(bf16[64,2560]{1,0:T(8,128)(2,1)S(1)} %temporal_attention.1.refs_0_.refs_6_), channel_id=1, source_target_pairs={{0,4},{2,6},{4,0},{6,2},{8,12},{10,14},{12,8},{14,10},{16,20},{18,... | collective-permute-start | bytes 983048 | tf_op jit(solution)/shard_map/ppermute | solution.py:486
  44.9 16.1 %collective-permute-start.8 = (bf16[64,2560]{1,0:T(8,128)(2,1)S(1)}, bf16[64,2560]{1,0:T(8,128)(2,1)S(1)}, u32[]{:S(2)}, u32[]{:S(2)}) collective-permute-start(bf16[64,2560]{1,0:T(8,128)(2,1)S(1)} %temporal_attention.1.refs_0_.refs_6_), channel_id=1, source_target_pairs={{0,2},{2,0},{4,6},{6,4},{8,10},{10,8},{12,14},{14,12},{16,18},{18,... | collective-permute-start | bytes 983048 | tf_op jit(solution)/shard_map/ppermute | solution.py:486
  47.2 8.1 %collective-permute-start.5 = (bf16[2,128,160]{2,1,0:T(8,128)(2,1)S(1)}, bf16[2,128,160]{2,1,0:T(8,128)(2,1)S(1)}, u32[]{:S(2)}, u32[]{:S(2)}) collective-permute-start(bf16[2,128,160]{2,1,0:T(8,128)(2,1)S(1)} %get-tuple-element.43), channel_id=1, source_target_pairs={{0,2},{2,0},{4,6},{6,4},{8,10},{10,8},{12,14},{14,12},{16,18},{18,... | collective-permute-start | bytes 245768 | tf_op jit(solution)/shard_map/ppermute | solution.py:486
  47.3 8.9 %collective-permute-start.6 = (bf16[2,128,160]{2,1,0:T(8,128)(2,1)S(1)}, bf16[2,128,160]{2,1,0:T(8,128)(2,1)S(1)}, u32[]{:S(2)}, u32[]{:S(2)}) collective-permute-start(bf16[2,128,160]{2,1,0:T(8,128)(2,1)S(1)} %get-tuple-element.44), channel_id=1, source_target_pairs={{0,4},{2,6},{4,0},{6,2},{8,12},{10,14},{12,8},{14,10},{16,20},{18,... | collective-permute-start | bytes 245768 | tf_op jit(solution)/shard_map/ppermute | solution.py:486
  51.1 9.9 %collective-permute-start.9 = (bf16[64,2560]{1,0:T(8,128)(2,1)S(1)}, bf16[64,2560]{1,0:T(8,128)(2,1)S(1)}, u32[]{:S(2)}, u32[]{:S(2)}) collective-permute-start(bf16[64,2560]{1,0:T(8,128)(2,1)S(1)} %collective-permute-done.3.refs_1_.refs_7_), channel_id=1, source_target_pairs={{0,2},{2,0},{4,6},{6,4},{8,10},{10,8},{12,14},{14,12},{16,18},{18,... | collective-permute-start | bytes 983048 | tf_op jit(solution)/shard_map/ppermute | solution.py:486
  53.3 7.8 %collective-permute-start.11 = (bf16[64,2560]{1,0:T(8,128)(2,1)S(1)}, bf16[64,2560]{1,0:T(8,128)(2,1)S(1)}, u32[]{:S(2)}, u32[]{:S(2)}) collective-permute-start(bf16[64,2560]{1,0:T(8,128)(2,1)S(1)} %collective-permute-done.10.refs_10_), channel_id=1, source_target_pairs={{0,2},{2,0},{4,6},{6,4},{8,10},{10,8},{12,14},{14,12},{16,18},{18,... | collective-permute-start | bytes 983048 | tf_op jit(solution)/shard_map/ppermute | solution.py:486
  55.3 5.8 %collective-permute-start.7 = (bf16[2,128,160]{2,1,0:T(8,128)(2,1)S(1)}, bf16[2,128,160]{2,1,0:T(8,128)(2,1)S(1)}, u32[]{:S(2)}, u32[]{:S(2)}) collective-permute-start(bf16[2,128,160]{2,1,0:T(8,128)(2,1)S(1)} %get-tuple-element.45), channel_id=1, source_target_pairs={{0,6},{2,4},{4,2},{6,0},{8,14},{10,12},{12,10},{14,8},{16,22},{18,... | collective-permute-start | bytes 245768 | tf_op jit(solution)/shard_map/ppermute | solution.py:486
  56.2 10.9 %collective-permute-start.12 = (bf16[64,2560]{1,0:T(8,128)(2,1)S(1)}, bf16[64,2560]{1,0:T(8,128)(2,1)S(1)}, u32[]{:S(2)}, u32[]{:S(2)}) collective-permute-start(bf16[64,2560]{1,0:T(8,128)(2,1)S(1)} %collective-permute-done.3.refs_1_.refs_7_), channel_id=1, source_target_pairs={{0,4},{2,6},{4,0},{6,2},{8,12},{10,14},{12,8},{14,10},{16,20},{18,... | collective-permute-start | bytes 983048 | tf_op jit(solution)/shard_map/ppermute | solution.py:486
  67.0 4.7 %collective-permute-start.13 = (bf16[64,2560]{1,0:T(8,128)(2,1)S(1)}, bf16[64,2560]{1,0:T(8,128)(2,1)S(1)}, u32[]{:S(2)}, u32[]{:S(2)}) collective-permute-start(bf16[64,2560]{1,0:T(8,128)(2,1)S(1)} %collective-permute-done.12.refs_0_), channel_id=1, source_target_pairs={{0,2},{2,0},{4,6},{6,4},{8,10},{10,8},{12,14},{14,12},{16,18},{18,... | collective-permute-start | bytes 983048 | tf_op jit(solution)/shard_map/ppermute | solution.py:486
  68.1 18.7 %all-to-all-start.1 = ((bf16[16,16,640]{2,1,0:T(8,128)(2,1)}), bf16[16,16,640]{2,1,0:T(8,128)(2,1)S(1)}, u32[]{:S(2)}, u32[]{:S(2)}) async-start(bf16[16,16,640]{2,1,0:T(8,128)(2,1)} %get-tuple-element.39), calls=%async_computation.1 | async-start | bytes 655360 | tf_op jit(solution)/shard_map/all_to_all | solution.py:479
  74.7 22.8 %copy-start.3 = (bf16[4,16,1280]{2,1,0:T(8,128)(2,1)S(1)}, bf16[4,16,1280]{2,1,0:T(8,128)(2,1)}, u32[]{:S(2)}) copy-start(bf16[4,16,1280]{2,1,0:T(8,128)(2,1)} %refs_3_.3) | copy-start | bytes 491524
  76.1 9.6 %collective-permute-start.14 = (bf16[168,640]{1,0:T(8,128)(2,1)S(1)}, bf16[168,640]{1,0:T(8,128)(2,1)S(1)}, u32[]{:S(2)}, u32[]{:S(2)}) collective-permute-start(bf16[168,640]{1,0:T(8,128)(2,1)S(1)} %get-tuple-element.51), channel_id=1, source_target_pairs={{0,8},{2,10},{4,12},{6,14},{8,16},{10,18},{12,20},{14,22},{16,24},... | collective-permute-start | bytes 645128 | tf_op jit(solution)/shard_map/ppermute | solution.py:486
  85.8 20.1 %slice-start = ((s8[6553600]{0:T(1024)(128)(4,1)}), s8[2359296]{0:T(1024)(128)(4,1)S(1)}, s32[]{:S(2)}) async-start(s8[6553600]{0:T(1024)(128)(4,1)} %bitcast.6), calls=%async_computation.2 | async-start | bytes 4718592
  86.8 8.4 %collective-permute-start.15 = (bf16[168,640]{1,0:T(8,128)(2,1)}, bf16[168,640]{1,0:T(8,128)(2,1)}, u32[]{:S(2)}, u32[]{:S(2)}) collective-permute-start(bf16[168,640]{1,0:T(8,128)(2,1)} %add_convert_fusion.2), channel_id=1, source_target_pairs={{0,8},{2,10},{4,12},{6,14},{8,16},{10,18},{12,20},{14,22},{16,24},... | collective-permute-start | bytes 645128 | tf_op jit(solution)/shard_map/ppermute | solution.py:486
  87.7 9.7 %collective-permute-start.4 = (bf16[16,16,640]{2,1,0:T(8,128)(2,1)S(1)}, bf16[16,16,640]{2,1,0:T(8,128)(2,1)}, u32[]{:S(2)}, u32[]{:S(2)}) collective-permute-start(bf16[16,16,640]{2,1,0:T(8,128)(2,1)S(1)} %all-to-all-done.1.refs_1_), channel_id=1, source_target_pairs={{1,0},{0,1},{3,2},{2,3},{5,4},{4,5},{7,6},{6,7},{9,8},{8,9},{11,10... | collective-permute-start | bytes 983048 | tf_op jit(solution)/shard_map/ppermute | solution.py:473
  96.2 7.2 %collective-permute-start.16 = (bf16[168,640]{1,0:T(8,128)(2,1)S(1)}, bf16[168,640]{1,0:T(8,128)(2,1)S(1)}, u32[]{:S(2)}, u32[]{:S(2)}) collective-permute-start(bf16[168,640]{1,0:T(8,128)(2,1)S(1)} %add_convert_fusion.1), channel_id=1, source_target_pairs={{0,8},{2,10},{4,12},{6,14},{8,16},{10,18},{12,20},{14,22},{16,24},... | collective-permute-start | bytes 645128 | tf_op jit(solution)/shard_map/ppermute | solution.py:486
  103.5 11.8 %collective-permute-start.17 = (bf16[168,640]{1,0:T(8,128)(2,1)S(1)}, bf16[168,640]{1,0:T(8,128)(2,1)S(1)}, u32[]{:S(2)}, u32[]{:S(2)}) collective-permute-start(bf16[168,640]{1,0:T(8,128)(2,1)S(1)} %add_convert_fusion), channel_id=1, source_target_pairs={{0,0},{1,16},{2,8},{3,24},{4,4},{5,20},{6,12},{7,28},{8,1},{9,17},... | collective-permute-start | bytes 645128 | tf_op jit(solution)/shard_map/ppermute | solution.py:602
  (15 other events, 42.0 us)
where the time goes:
time: 118 us; the launch traced here: 117 us
  waiting for transfers between devices  38 us (32%)
  starting transfers between devices  23 us (19%)
  Pallas kernels  22.5 us (19%)
  blocking collectives  17.5 us (15%)
  local copies, waits for them, and re-layouts  11.2 us (9%)
  other arithmetic  3.48 us (3%)
    pallas_call x12, Pallas kernels, call(): pl.pallas_call(kernel, out_shape=outs, in_specs=in_specs, out_specs=[pl.B...  22.5 us
    ppermute x12, waiting for transfers between devices, move(): return lax.ppermute(x, 'frame', pairs)  21.9 us
    all_to_all x1, blocking collectives, swap(): return lax.all_to_all(x, 'frame', split_axis=0, concat_axis=0, tiled=True)  17.5 us
    ppermute x12, starting transfers between devices, move(): return lax.ppermute(x, 'frame', pairs)  12.3 us
    unnamed x40, local copies, waits for them, and re-layouts  11.2 us
    ppermute x1, waiting for transfers between devices, to_quad(): return lax.ppermute(x, 'quad', [(d, (d + s) % nq) for d in range(nq)])  8.3 us
    ppermute x1, waiting for transfers between devices, local(): total = lax.ppermute(total, ('frame', 'quad'), final)  5.27 us
    ppermute x4, starting transfers between devices, from_quad(): return lax.ppermute(x, 'quad', [((d + s) % nq, d) for d in range(nq)])  4.06 us
  transfers between devices with their start and end apart: 19, of which 10 were waited for; matrix products, arithmetic and copies ran while one was open for 2% of the time, Pallas kernels for 16%

commit v1 on v0

--- a/solution.py
+++ b/solution.py
@@ -377,8 +377,10 @@
     extra = jnp.where(iota((8, width), 0) == 0, extra, 0.0)
     for r in range(stage):
         z = (geo[2] + r) & (stage - 1)
-        rows_out = jnp.concatenate([blocks[k, z] for k in range(4)] + [extra], axis=0)
+        rows_out = jnp.concatenate([blocks[0, z], blocks[1, z], extra], axis=0)
         outs[r][...] = rows_out.astype(BF16)
+        rows_out = jnp.concatenate([blocks[2, z], blocks[3, z]], axis=0)
+        outs[stage + r][...] = rows_out.astype(BF16)
 
 
 def middle_kernel(dims, *refs):
@@ -546,7 +548,8 @@
         [geo] + all_terms + [motion_weights],
         3,
     )
-    last_terms = [move(t, flipped(1)) for t in pair_terms[:1]]
+    pair_terms[0] = after(pair_terms[0], back_send)
+    last_terms = [move(pair_terms[0], flipped(1))]
 
     stage, block = nf // 4, half // nf
     sums, gain_sum, late_left = run(
@@ -566,9 +569,9 @@
     parts_w = run(
         second_weight_kernel,
         "weight_terms_last_tokens",
-        [sds(4 * block + 8, width)] * stage,
+        [sds(2 * block + 8, width)] * stage + [sds(2 * block, width)] * stage,
         [geo, sums, gain_sum, late_left, quarter, table, gain2] + late_terms,
-        2,
+        0.01,
         scratch=[pltpu.VMEM((4, stage, block, width), F32)],
     )
 
@@ -585,21 +588,22 @@
         6,
         big,
     )
-    total = parts_w[stage - 1]
+    totals = [parts_w[stage - 1], parts_w[2 * stage - 1]]
     for step in range(1, stage):
-        if step == stage - 2:
-            total = after(total, back_recv)
-        moved = move(total, ring)
-        if step == stage - 1:
-            moved = after(moved, grad_hidden)
-        total = add(moved, parts_w[stage - 1 - step])
+        for i in range(2):
+            if step == stage - 2:
+                totals[i] = after(totals[i], back_recv)
+            moved = move(totals[i], ring)
+            if step == stage - 1:
+                moved = after(moved, grad_hidden)
+            totals[i] = add(moved, parts_w[(i + 1) * stage - 1 - step])
     final = []
     for g in range(nf):
         for q in range(nq):
             j = quarter_of(g % 4) * stage + g // 4
             final.append((g * nq + q, nf * q + j))
-    grad_hidden = after(grad_hidden, total)
-    total = lax.ppermute(total, ("frame", "quad"), final)
+    grad_hidden = after(grad_hidden, *totals)
+    totals = [lax.ppermute(t, ("frame", "quad"), final) for t in totals]
     (input_grad,) = run(
         tail_kernel,
         "spatial_backward",
@@ -610,9 +614,10 @@
     )
     everyone = nf * nq
     factor = 1.0 / math.sqrt(everyone * fr * pq)
-    weight_grad = total[: 4 * block].reshape(4, block, width).astype(F32) * factor
+    weight_grad = jnp.concatenate([totals[0][: 2 * block], totals[1]], axis=0)
+    weight_grad = weight_grad.reshape(4, block, width).astype(F32) * factor
     place = ((frame * nq + quad) % stage) * block
-    gain_grad = lax.dynamic_slice(total[4 * block], (place,), (block,)).astype(F32) * factor
+    gain_grad = lax.dynamic_slice(totals[0][2 * block], (place,), (block,)).astype(F32) * factor
     return block_output, input_grad, weight_grad, gain_grad
 
 

time: 118 us -> 112 us (0.949)
  the two profiles are of different devices: /device:TPU:1 before, /device:TPU:7 now
where the time goes in v1:
time: 112 us; the launch traced here: 111 us
  waiting for transfers between devices  32.9 us (29%)
  starting transfers between devices  29.3 us (26%)
  Pallas kernels  22.4 us (20%)
  blocking collectives  17 us (15%)
  local copies, waits for them, and re-layouts  6.7 us (6%)
  other arithmetic  1.87 us (2%)
    pallas_call x12, Pallas kernels, call(): pl.pallas_call(kernel, out_shape=outs, in_specs=in_specs, out_specs=[pl.B...  22.4 us
    ppermute x15, waiting for transfers between devices, move(): return lax.ppermute(x, 'frame', pairs)  17.3 us
    all_to_all x1, blocking collectives, swap(): return lax.all_to_all(x, 'frame', split_axis=0, concat_axis=0, tiled=True)  17 us
    ppermute x2, starting transfers between devices, local(): totals = [lax.ppermute(t, ('frame', 'quad'), final) for t in totals]  9.96 us
    ppermute x15, starting transfers between devices, move(): return lax.ppermute(x, 'frame', pairs)  9.08 us
    ppermute x1, waiting for transfers between devices, to_quad(): return lax.ppermute(x, 'quad', [(d, (d + s) % nq) for d in range(nq)])  8.76 us
    unnamed x34, local copies, waits for them, and re-layouts  6.68 us
    all_to_all x1, starting transfers between devices, swap(): return lax.all_to_all(x, 'frame', split_axis=0, concat_axis=0, tiled=True)  6.04 us
  transfers between devices with their start and end apart: 23, of which 12 were waited for; matrix products, arithmetic and copies ran while one was open for 1% of the time, Pallas kernels for 17%

profile of v1, /device:TPU:7, one launch (start us, length us, event | category | flops | bytes accessed | tf_op | source)
XLA Modules:
  0.0 111.3 jit_solution(17923299072065668831)
XLA Ops:
  1.3 2.9 %copy-done = bf16[4,1280,640]{2,1,0:T(8,128)(2,1)S(1)} copy-done((bf16[4,1280,640]{2,1,0:T(8,128)(2,1)S(1)}, bf16[4,1280,640]{2,1,0:T(8,128)(2,1)}, u32[]{:S(2)}) %copy-start) | copy-done | bytes 6553624
  7.9 3.4 %spatial_forward.1 = (bf16[128,3200]{1,0:T(8,128)(2,1)S(1)}, bf16[16,8,640]{2,1,0:T(8,128)(2,1)S(1)}) custom-call(s32[3]{0:T(128)S(1)} %pad_add_fusion.refs_0_.geo.quad_ref, bf16[4,16,1280]{2,1,0:T(8,128)(2,1)S(1)} %copy-done.6, bf16[4,16,1280]{2,1,0:T(8,128)(2,1)S(1)} %collective-permute-done.refs_2_, f32[1280]{0:T(1024)S(1)} %copy-done.10, ...), custom_call_target="tpu_custom_call" | custom-call | flops 3000000000 | bytes 1048576 | tf_op jit(solution)/shard_map/spatial_forward/pallas_call | solution.py:430
  12.2 17.0 %all_to_all.10.received = bf16[16,16,640]{2,1,0:T(8,128)(2,1)S(1)} all-to-all(bf16[16,16,640]{2,1,0:T(8,128)(2,1)S(1)} %join_sent.1), channel_id=1, replica_groups=mesh['frame'=16,'quad'=2] {'frame'}, dimensions={0} | all-to-all | bytes 655360 | tf_op jit(solution)/shard_map/all_to_all | solution.py:481
  29.2 1.5 %motion_projection.1 = (f32[64,2560]{1,0:T(8,128)S(1)}, bf16[64,2560]{1,0:T(8,128)(2,1)S(1)}) custom-call(s32[3]{0:T(128)S(1)} %pad_add_fusion.refs_0_.geo.quad_ref, bf16[16,16,640]{2,1,0:T(8,128)(2,1)S(1)} %all_to_all.10.received, bf16[4,640,640]{2,1,0:T(8,128)(2,1)S(1)} %copy-done.5), custom_call_target="tpu_custom_call" | custom-call | flops 1500000000 | bytes 1048576 | tf_op jit(solution)/shard_map/motion_projection/pallas_call | solution.py:430
  31.7 8.8 %collective-permute-done.2.refs_1_ = bf16[64,2560]{1,0:T(8,128)(2,1)S(1)} collective-permute-done((bf16[64,2560]{1,0:T(8,128)(2,1)S(1)}, bf16[64,2560]{1,0:T(8,128)(2,1)S(1)}, u32[]{:S(2)}, u32[]{:S(2)}) %collective-permute-start.2) | collective-permute-done | bytes 327712 | tf_op jit(solution)/shard_map/ppermute | solution.py:478
  42.8 1.8 %collective-permute-start.8 = (bf16[64,2560]{1,0:T(8,128)(2,1)S(1)}, bf16[64,2560]{1,0:T(8,128)(2,1)S(1)}, u32[]{:S(2)}, u32[]{:S(2)}) collective-permute-start(bf16[64,2560]{1,0:T(8,128)(2,1)S(1)} %temporal_attention.1.refs_0_.refs_6_), channel_id=1, source_target_pairs={{0,2},{2,0},{4,6},{6,4},{8,10},{10,8},{12,14},{14,12},{16,18},{18,... | collective-permute-start | bytes 983048 | tf_op jit(solution)/shard_map/ppermute | solution.py:488
  44.6 1.6 %positional_table.1.refs_5_.pos = f32[64,1280]{1,0:T(8,128)S(1)} custom-call(s32[3]{0:T(128)S(1)} %pad_add_fusion.refs_0_.geo.quad_ref), custom_call_target="tpu_custom_call" | custom-call | flops 1500000000 | bytes 1048576 | tf_op jit(solution)/shard_map/positional_table/pallas_call | solution.py:430
  47.5 2.9 %collective-permute-done.3.refs_1_.refs_7_ = bf16[64,2560]{1,0:T(8,128)(2,1)S(1)} collective-permute-done((bf16[64,2560]{1,0:T(8,128)(2,1)S(1)}, bf16[64,2560]{1,0:T(8,128)(2,1)S(1)}, u32[]{:S(2)}, u32[]{:S(2)}) %collective-permute-start.3) | collective-permute-done | bytes 327712 | tf_op jit(solution)/shard_map/ppermute | solution.py:475
  50.4 2.5 %temporal_back_projection.1 = (bf16[16,16,640]{2,1,0:T(8,128)(2,1)}, bf16[3,160,640]{2,1,0:T(8,128)(2,1)S(1)}) custom-call(s32[3]{0:T(128)S(1)} %pad_add_fusion.refs_0_.geo.quad_ref, bf16[64,2560]{1,0:T(8,128)(2,1)S(1)} %temporal_attention.1.refs_0_.refs_6_, bf16[64,2560]{1,0:T(8,128)(2,1)S(1)} %collective-permute-done.3.refs_1_.refs_7_, ...), custom_call_target="tpu_custom_call" | custom-call | flops 3000000000 | bytes 1048576 | tf_op jit(solution)/shard_map/temporal_back_projection/pallas_call | solution.py:430
  52.9 1.3 %collective-permute-start.11 = (bf16[64,2560]{1,0:T(8,128)(2,1)S(1)}, bf16[64,2560]{1,0:T(8,128)(2,1)}, u32[]{:S(2)}, u32[]{:S(2)}) collective-permute-start(bf16[64,2560]{1,0:T(8,128)(2,1)S(1)} %collective-permute-done.10.refs_10_), channel_id=1, source_target_pairs={{0,2},{2,0},{4,6},{6,4},{8,10},{10,8},{12,14},{14,12},{16,18},{18,... | collective-permute-start | bytes 983048 | tf_op jit(solution)/shard_map/ppermute | solution.py:488
  56.7 3.1 %collective-permute-done.6.refs_2_ = bf16[2,128,160]{2,1,0:T(8,128)(2,1)S(1)} collective-permute-done((bf16[2,128,160]{2,1,0:T(8,128)(2,1)S(1)}, bf16[2,128,160]{2,1,0:T(8,128)(2,1)S(1)}, u32[]{:S(2)}, u32[]{:S(2)}) %collective-permute-start.6) | collective-permute-done | bytes 81952 | tf_op jit(solution)/shard_map/ppermute | solution.py:488
  60.1 6.0 %all-to-all-start.1 = ((bf16[16,16,640]{2,1,0:T(8,128)(2,1)}), bf16[16,16,640]{2,1,0:T(8,128)(2,1)S(1)}, u32[]{:S(2)}, u32[]{:S(2)}) async-start(bf16[16,16,640]{2,1,0:T(8,128)(2,1)} %get-tuple-element.46), calls=%async_computation.1 | async-start | bytes 655360 | tf_op jit(solution)/shard_map/all_to_all | solution.py:481
  67.1 2.2 %weight_terms_first_tokens.1 = (f32[4,4,40,640]{3,2,1,0:T(8,128)S(1)}, f32[1,160]{1,0:T(1,128)S(1)}, bf16[2,128,160]{2,1,0:T(8,128)(2,1)S(1)}) custom-call(s32[3]{0:T(128)S(1)} %pad_add_fusion.refs_0_.geo.quad_ref, bf16[2,128,160]{2,1,0:T(8,128)(2,1)S(1)} %copy-done.12, bf16[2,128,160]{2,1,0:T(8,128)(2,1)S(1)} %collective-permute-done.5.refs_1_, ...), custom_call_target="tpu_custom_call" | custom-call | flops 3000000000 | bytes 1048576 | tf_op jit(solution)/shard_map/weight_terms_first_tokens/pallas_call | solution.py:430
  69.4 2.8 %collective-permute-start.13 = (bf16[64,2560]{1,0:T(8,128)(2,1)S(1)}, bf16[64,2560]{1,0:T(8,128)(2,1)S(1)}, u32[]{:S(2)}, u32[]{:S(2)}) collective-permute-start(bf16[64,2560]{1,0:T(8,128)(2,1)S(1)} %collective-permute-done.12.refs_0_), channel_id=1, source_target_pairs={{0,2},{2,0},{4,6},{6,4},{8,10},{10,8},{12,14},{14,12},{16,18},{18,... | collective-permute-start | bytes 983048 | tf_op jit(solution)/shard_map/ppermute | solution.py:488
  73.5 1.5 %weight_terms_last_tokens.1 = (bf16[88,640]{1,0:T(8,128)(2,1)S(1)}, bf16[88,640]{1,0:T(8,128)(2,1)S(1)}, bf16[88,640]{1,0:T(8,128)(2,1)S(1)}, bf16[88,640]{1,0:T...) custom-call(s32[3]{0:T(128)S(1)} %pad_add_fusion.refs_0_.geo.quad_re, ...), custom_call_target="tpu_custom_call" | custom-call | flops 10000000 | bytes 1048576 | tf_op jit(solution)/shard_map/weight_terms_last_tokens/pallas_call | solution.py:430
  77.6 3.2 %collective-permute-done.17 = bf16[80,640]{1,0:T(8,128)(2,1)S(1)} collective-permute-done((bf16[80,640]{1,0:T(8,128)(2,1)S(1)}, bf16[80,640]{1,0:T(8,128)(2,1)S(1)}, u32[]{:S(2)}, u32[]{:S(2)}) %collective-permute-start.17) | collective-permute-done | bytes 102432 | tf_op jit(solution)/shard_map/ppermute | solution.py:488
  81.0 2.9 %collective-permute-done.14 = bf16[88,640]{1,0:T(8,128)(2,1)S(1)} collective-permute-done((bf16[88,640]{1,0:T(8,128)(2,1)S(1)}, bf16[88,640]{1,0:T(8,128)(2,1)S(1)}, u32[]{:S(2)}, u32[]{:S(2)}) %collective-permute-start.14) | collective-permute-done | bytes 112672 | tf_op jit(solution)/shard_map/ppermute | solution.py:488
  83.9 2.3 %collective-permute-done.18 = bf16[80,640]{1,0:T(8,128)(2,1)S(1)} collective-permute-done((bf16[80,640]{1,0:T(8,128)(2,1)S(1)}, bf16[80,640]{1,0:T(8,128)(2,1)S(1)}, u32[]{:S(2)}, u32[]{:S(2)}) %collective-permute-start.18) | collective-permute-done | bytes 102432 | tf_op jit(solution)/shard_map/ppermute | solution.py:488
  86.4 3.4 %collective-permute-done.15 = bf16[88,640]{1,0:T(8,128)(2,1)S(1)} collective-permute-done((bf16[88,640]{1,0:T(8,128)(2,1)S(1)}, bf16[88,640]{1,0:T(8,128)(2,1)S(1)}, u32[]{:S(2)}, u32[]{:S(2)}) %collective-permute-start.15) | collective-permute-done | bytes 112672 | tf_op jit(solution)/shard_map/ppermute | solution.py:488
  91.3 1.7 %block_output_hidden_gradient.1 = (bf16[4,16,1280]{2,1,0:T(8,128)(2,1)}, bf16[128,1280]{1,0:T(8,128)(2,1)S(1)}) custom-call(s32[3]{0:T(128)S(1)} %pad_add_fusion.refs_0_.geo.quad_ref, bf16[16,16,640]{2,1,0:T(8,128)(2,1)S(1)} %all-to-all-done.1.refs_1_, bf16[16,16,640]{2,1,0:T(8,128)(2,1)S(1)} %collective-permute-done.4.refs_2_, ...), custom_call_target="tpu_custom_call" | custom-call | flops 6000000000 | bytes 1048576 | tf_op jit(solution)/shard_map/block_output_hidden_gradient/pallas_call | solution.py:430
  93.0 8.0 %collective-permute-start.21 = (bf16[80,640]{1,0:T(8,128)(2,1)S(1)}, bf16[80,640]{1,0:T(8,128)(2,1)S(1)}, u32[]{:S(2)}, u32[]{:S(2)}) collective-permute-start(bf16[80,640]{1,0:T(8,128)(2,1)S(1)} %add_convert_fusion.3), channel_id=1, source_target_pairs={{0,0},{1,16},{2,8},{3,24},{4,4},{5,20},{6,12},{7,28},{8,1},{9,17},... | collective-permute-start | bytes 307208 | tf_op jit(solution)/shard_map/ppermute | solution.py:606
  101.1 1.9 %collective-permute-start.20 = (bf16[88,640]{1,0:T(8,128)(2,1)S(1)}, bf16[88,640]{1,0:T(8,128)(2,1)S(1)}, u32[]{:S(2)}, u32[]{:S(2)}) collective-permute-start(bf16[88,640]{1,0:T(8,128)(2,1)S(1)} %add_convert_fusion), channel_id=1, source_target_pairs={{0,0},{1,16},{2,8},{3,24},{4,4},{5,20},{6,12},{7,28},{8,1},{9,17},... | collective-permute-start | bytes 337928 | tf_op jit(solution)/shard_map/ppermute | solution.py:606
  103.0 4.1 %spatial_backward.1 = bf16[4,16,1280]{2,1,0:T(8,128)(2,1)} custom-call(bf16[128,1280]{1,0:T(8,128)(2,1)S(1)} %get-tuple-element.71.grad_hidden, bf16[4,16,1280]{2,1,0:T(8,128)(2,1)S(1)} %copy-done.7, bf16[128,3200]{1,0:T(8,128)(2,1)S(1)} %copy-done.14, f32[1280]{0:T(1024)S(1)} %copy-done.10, bf16[4,1280,640]{2,1,0:T(8,128)(2,1)S(1)} %bitcast.7), custom_call_target="tpu_custom_call" | custom-call | flops 3500000000 | bytes 1048576 | tf_op jit(solution)/shard_map/spatial_backward/pallas_call | solution.py:430
  107.1 2.7 %collective-permute-done.20 = bf16[88,640]{1,0:T(8,128)(2,1)S(1)} collective-permute-done((bf16[88,640]{1,0:T(8,128)(2,1)S(1)}, bf16[88,640]{1,0:T(8,128)(2,1)S(1)}, u32[]{:S(2)}, u32[]{:S(2)}) %collective-permute-start.20) | collective-permute-done | bytes 112672 | tf_op jit(solution)/shard_map/ppermute | solution.py:606
  (84 shorter events, 20.5 us)
Async XLA Ops:
  0.6 5.3 %collective-permute-start = (bf16[4,16,1280]{2,1,0:T(8,128)(2,1)}, bf16[4,16,1280]{2,1,0:T(8,128)(2,1)S(1)}, u32[]{:S(2)}, u32[]{:S(2)}) collective-permute-start(bf16[4,16,1280]{2,1,0:T(8,128)(2,1)} %xs.1), channel_id=1, source_target_pairs={{1,0},{0,1},{3,2},{2,3},{5,4},{4,5},{7,6},{6,7},{9,8},{8,9},{11,10... | collective-permute-start | bytes 491528 | tf_op jit(solution)/shard_map/ppermute | solution.py:475
  5.8 23.5 %copy-start.5 = (bf16[4,640,640]{2,1,0:T(8,128)(2,1)S(1)}, bf16[4,640,640]{2,1,0:T(8,128)(2,1)}, u32[]{:S(2)}) copy-start(bf16[4,640,640]{2,1,0:T(8,128)(2,1)} %refs_2_.1) | copy-start | bytes 9830404
  6.0 5.4 %collective-permute-start.1 = (bf16[4,16,1280]{2,1,0:T(8,128)(2,1)S(1)}, bf16[4,16,1280]{2,1,0:T(8,128)(2,1)S(1)}, u32[]{:S(2)}, u32[]{:S(2)}) collective-permute-start(bf16[4,16,1280]{2,1,0:T(8,128)(2,1)S(1)} %copy-done.2), channel_id=1, source_target_pairs={{1,0},{0,1},{3,2},{2,3},{5,4},{4,5},{7,6},{6,7},{9,8},{8,9},{11,10... | collective-permute-start | bytes 491528 | tf_op jit(solution)/shard_map/ppermute | solution.py:475
  30.7 9.7 %collective-permute-start.2 = (bf16[64,2560]{1,0:T(8,128)(2,1)S(1)}, bf16[64,2560]{1,0:T(8,128)(2,1)S(1)}, u32[]{:S(2)}, u32[]{:S(2)}) collective-permute-start(bf16[64,2560]{1,0:T(8,128)(2,1)S(1)} %get-tuple-element.41), channel_id=1, source_target_pairs={{0,1},{1,0},{2,3},{3,2},{4,5},{5,4},{6,7},{7,6},{8,9},{9,8},{10,11... | collective-permute-start | bytes 983048 | tf_op jit(solution)/shard_map/ppermute | solution.py:478
  41.5 8.9 %collective-permute-start.3 = (bf16[64,2560]{1,0:T(8,128)(2,1)S(1)}, bf16[64,2560]{1,0:T(8,128)(2,1)S(1)}, u32[]{:S(2)}, u32[]{:S(2)}) collective-permute-start(bf16[64,2560]{1,0:T(8,128)(2,1)S(1)} %temporal_attention.1.refs_0_.refs_6_), channel_id=1, source_target_pairs={{1,0},{0,1},{3,2},{2,3},{5,4},{4,5},{7,6},{6,7},{9,8},{8,9},{11,10... | collective-permute-start | bytes 983048 | tf_op jit(solution)/shard_map/ppermute | solution.py:475
  42.5 10.4 %collective-permute-start.10 = (bf16[64,2560]{1,0:T(8,128)(2,1)S(1)}, bf16[64,2560]{1,0:T(8,128)(2,1)S(1)}, u32[]{:S(2)}, u32[]{:S(2)}) collective-permute-start(bf16[64,2560]{1,0:T(8,128)(2,1)S(1)} %temporal_attention.1.refs_0_.refs_6_), channel_id=1, source_target_pairs={{0,4},{2,6},{4,0},{6,2},{8,12},{10,14},{12,8},{14,10},{16,20},{18,... | collective-permute-start | bytes 983048 | tf_op jit(solution)/shard_map/ppermute | solution.py:488
  42.8 23.4 %collective-permute-start.8 = (bf16[64,2560]{1,0:T(8,128)(2,1)S(1)}, bf16[64,2560]{1,0:T(8,128)(2,1)S(1)}, u32[]{:S(2)}, u32[]{:S(2)}) collective-permute-start(bf16[64,2560]{1,0:T(8,128)(2,1)S(1)} %temporal_attention.1.refs_0_.refs_6_), channel_id=1, source_target_pairs={{0,2},{2,0},{4,6},{6,4},{8,10},{10,8},{12,14},{14,12},{16,18},{18,... | collective-permute-start | bytes 983048 | tf_op jit(solution)/shard_map/ppermute | solution.py:488
  52.9 13.3 %collective-permute-start.11 = (bf16[64,2560]{1,0:T(8,128)(2,1)S(1)}, bf16[64,2560]{1,0:T(8,128)(2,1)}, u32[]{:S(2)}, u32[]{:S(2)}) collective-permute-start(bf16[64,2560]{1,0:T(8,128)(2,1)S(1)} %collective-permute-done.10.refs_10_), channel_id=1, source_target_pairs={{0,2},{2,0},{4,6},{6,4},{8,10},{10,8},{12,14},{14,12},{16,18},{18,... | collective-permute-start | bytes 983048 | tf_op jit(solution)/shard_map/ppermute | solution.py:488
  54.3 11.9 %collective-permute-start.9 = (bf16[64,2560]{1,0:T(8,128)(2,1)S(1)}, bf16[64,2560]{1,0:T(8,128)(2,1)}, u32[]{:S(2)}, u32[]{:S(2)}) collective-permute-start(bf16[64,2560]{1,0:T(8,128)(2,1)S(1)} %collective-permute-done.3.refs_1_.refs_7_), channel_id=1, source_target_pairs={{0,2},{2,0},{4,6},{6,4},{8,10},{10,8},{12,14},{14,12},{16,18},{18,... | collective-permute-start | bytes 983048 | tf_op jit(solution)/shard_map/ppermute | solution.py:488
  54.3 1.8 %collective-permute-start.5 = (bf16[2,128,160]{2,1,0:T(8,128)(2,1)S(1)}, bf16[2,128,160]{2,1,0:T(8,128)(2,1)S(1)}, u32[]{:S(2)}, u32[]{:S(2)}) collective-permute-start(bf16[2,128,160]{2,1,0:T(8,128)(2,1)S(1)} %get-tuple-element.50), channel_id=1, source_target_pairs={{0,2},{2,0},{4,6},{6,4},{8,10},{10,8},{12,14},{14,12},{16,18},{18,... | collective-permute-start | bytes 245768 | tf_op jit(solution)/shard_map/ppermute | solution.py:488
  54.8 5.0 %collective-permute-start.6 = (bf16[2,128,160]{2,1,0:T(8,128)(2,1)S(1)}, bf16[2,128,160]{2,1,0:T(8,128)(2,1)S(1)}, u32[]{:S(2)}, u32[]{:S(2)}) collective-permute-start(bf16[2,128,160]{2,1,0:T(8,128)(2,1)S(1)} %get-tuple-element.51), channel_id=1, source_target_pairs={{0,4},{2,6},{4,0},{6,2},{8,12},{10,14},{12,8},{14,10},{16,20},{18,... | collective-permute-start | bytes 245768 | tf_op jit(solution)/shard_map/ppermute | solution.py:488
  56.2 10.0 %collective-permute-start.7 = (bf16[2,128,160]{2,1,0:T(8,128)(2,1)S(1)}, bf16[2,128,160]{2,1,0:T(8,128)(2,1)S(1)}, u32[]{:S(2)}, u32[]{:S(2)}) collective-permute-start(bf16[2,128,160]{2,1,0:T(8,128)(2,1)S(1)} %get-tuple-element.52), channel_id=1, source_target_pairs={{0,6},{2,4},{4,2},{6,0},{8,14},{10,12},{12,10},{14,8},{16,22},{18,... | collective-permute-start | bytes 245768 | tf_op jit(solution)/shard_map/ppermute | solution.py:488
  59.8 9.6 %collective-permute-start.12 = (bf16[64,2560]{1,0:T(8,128)(2,1)S(1)}, bf16[64,2560]{1,0:T(8,128)(2,1)S(1)}, u32[]{:S(2)}, u32[]{:S(2)}) collective-permute-start(bf16[64,2560]{1,0:T(8,128)(2,1)S(1)} %collective-permute-done.3.refs_1_.refs_7_), channel_id=1, source_target_pairs={{0,4},{2,6},{4,0},{6,2},{8,12},{10,14},{12,8},{14,10},{16,20},{18,... | collective-permute-start | bytes 983048 | tf_op jit(solution)/shard_map/ppermute | solution.py:488
  60.1 15.9 %all-to-all-start.1 = ((bf16[16,16,640]{2,1,0:T(8,128)(2,1)}), bf16[16,16,640]{2,1,0:T(8,128)(2,1)S(1)}, u32[]{:S(2)}, u32[]{:S(2)}) async-start(bf16[16,16,640]{2,1,0:T(8,128)(2,1)} %get-tuple-element.46), calls=%async_computation.1 | async-start | bytes 655360 | tf_op jit(solution)/shard_map/all_to_all | solution.py:481
  69.4 4.1 %collective-permute-start.13 = (bf16[64,2560]{1,0:T(8,128)(2,1)S(1)}, bf16[64,2560]{1,0:T(8,128)(2,1)S(1)}, u32[]{:S(2)}, u32[]{:S(2)}) collective-permute-start(bf16[64,2560]{1,0:T(8,128)(2,1)S(1)} %collective-permute-done.12.refs_0_), channel_id=1, source_target_pairs={{0,2},{2,0},{4,6},{6,4},{8,10},{10,8},{12,14},{14,12},{16,18},{18,... | collective-permute-start | bytes 983048 | tf_op jit(solution)/shard_map/ppermute | solution.py:488
  74.9 5.9 %collective-permute-start.17 = (bf16[80,640]{1,0:T(8,128)(2,1)S(1)}, bf16[80,640]{1,0:T(8,128)(2,1)S(1)}, u32[]{:S(2)}, u32[]{:S(2)}) collective-permute-start(bf16[80,640]{1,0:T(8,128)(2,1)S(1)} %get-tuple-element.65), channel_id=1, source_target_pairs={{0,8},{2,10},{4,12},{6,14},{8,16},{10,18},{12,20},{14,22},{16,24},... | collective-permute-start | bytes 307208 | tf_op jit(solution)/shard_map/ppermute | solution.py:488
  76.0 14.1 %collective-permute-start.4 = (bf16[16,16,640]{2,1,0:T(8,128)(2,1)S(1)}, bf16[16,16,640]{2,1,0:T(8,128)(2,1)S(1)}, u32[]{:S(2)}, u32[]{:S(2)}) collective-permute-start(bf16[16,16,640]{2,1,0:T(8,128)(2,1)S(1)} %all-to-all-done.1.refs_1_), channel_id=1, source_target_pairs={{1,0},{0,1},{3,2},{2,3},{5,4},{4,5},{7,6},{6,7},{9,8},{8,9},{11,10... | collective-permute-start | bytes 983048 | tf_op jit(solution)/shard_map/ppermute | solution.py:475
  76.9 6.9 %collective-permute-start.14 = (bf16[88,640]{1,0:T(8,128)(2,1)S(1)}, bf16[88,640]{1,0:T(8,128)(2,1)S(1)}, u32[]{:S(2)}, u32[]{:S(2)}) collective-permute-start(bf16[88,640]{1,0:T(8,128)(2,1)S(1)} %get-tuple-element.59), channel_id=1, source_target_pairs={{0,8},{2,10},{4,12},{6,14},{8,16},{10,18},{12,20},{14,22},{16,24},... | collective-permute-start | bytes 337928 | tf_op jit(solution)/shard_map/ppermute | solution.py:488
  80.9 5.4 %collective-permute-start.18 = (bf16[80,640]{1,0:T(8,128)(2,1)S(1)}, bf16[80,640]{1,0:T(8,128)(2,1)S(1)}, u32[]{:S(2)}, u32[]{:S(2)}) collective-permute-start(bf16[80,640]{1,0:T(8,128)(2,1)S(1)} %add_convert_fusion.5), channel_id=1, source_target_pairs={{0,8},{2,10},{4,12},{6,14},{8,16},{10,18},{12,20},{14,22},{16,24},... | collective-permute-start | bytes 307208 | tf_op jit(solution)/shard_map/ppermute | solution.py:488
  83.9 5.9 %collective-permute-start.15 = (bf16[88,640]{1,0:T(8,128)(2,1)S(1)}, bf16[88,640]{1,0:T(8,128)(2,1)S(1)}, u32[]{:S(2)}, u32[]{:S(2)}) collective-permute-start(bf16[88,640]{1,0:T(8,128)(2,1)S(1)} %add_convert_fusion.2), channel_id=1, source_target_pairs={{0,8},{2,10},{4,12},{6,14},{8,16},{10,18},{12,20},{14,22},{16,24},... | collective-permute-start | bytes 337928 | tf_op jit(solution)/shard_map/ppermute | solution.py:488
  86.3 6.6 %collective-permute-start.19 = (bf16[80,640]{1,0:T(8,128)(2,1)S(1)}, bf16[80,640]{1,0:T(8,128)(2,1)S(1)}, u32[]{:S(2)}, u32[]{:S(2)}) collective-permute-start(bf16[80,640]{1,0:T(8,128)(2,1)S(1)} %add_convert_fusion.4), channel_id=1, source_target_pairs={{0,8},{2,10},{4,12},{6,14},{8,16},{10,18},{12,20},{14,22},{16,24},... | collective-permute-start | bytes 307208 | tf_op jit(solution)/shard_map/ppermute | solution.py:488
  89.8 11.2 %collective-permute-start.16 = (bf16[88,640]{1,0:T(8,128)(2,1)S(1)}, bf16[88,640]{1,0:T(8,128)(2,1)S(1)}, u32[]{:S(2)}, u32[]{:S(2)}) collective-permute-start(bf16[88,640]{1,0:T(8,128)(2,1)S(1)} %add_convert_fusion.1), channel_id=1, source_target_pairs={{0,8},{2,10},{4,12},{6,14},{8,16},{10,18},{12,20},{14,22},{16,24},... | collective-permute-start | bytes 337928 | tf_op jit(solution)/shard_map/ppermute | solution.py:488
  93.0 17.5 %collective-permute-start.21 = (bf16[80,640]{1,0:T(8,128)(2,1)S(1)}, bf16[80,640]{1,0:T(8,128)(2,1)S(1)}, u32[]{:S(2)}, u32[]{:S(2)}) collective-permute-start(bf16[80,640]{1,0:T(8,128)(2,1)S(1)} %add_convert_fusion.3), channel_id=1, source_target_pairs={{0,0},{1,16},{2,8},{3,24},{4,4},{5,20},{6,12},{7,28},{8,1},{9,17},... | collective-permute-start | bytes 307208 | tf_op jit(solution)/shard_map/ppermute | solution.py:606
  101.1 8.8 %collective-permute-start.20 = (bf16[88,640]{1,0:T(8,128)(2,1)S(1)}, bf16[88,640]{1,0:T(8,128)(2,1)S(1)}, u32[]{:S(2)}, u32[]{:S(2)}) collective-permute-start(bf16[88,640]{1,0:T(8,128)(2,1)S(1)} %add_convert_fusion), channel_id=1, source_target_pairs={{0,0},{1,16},{2,8},{3,24},{4,4},{5,20},{6,12},{7,28},{8,1},{9,17},... | collective-permute-start | bytes 337928 | tf_op jit(solution)/shard_map/ppermute | solution.py:606
  (16 other events, 145.5 us)

commit v2 on v1

--- a/solution.py
+++ b/solution.py
@@ -435,7 +435,9 @@
             scratch_shapes=list(scratch),
             compiler_params=pltpu.CompilerParams(vmem_limit_bytes=vmem * 1024 * 1024),
             cost_estimate=pl.CostEstimate(
-                flops=int(micros * 1e9), bytes_accessed=2**20, transcendentals=0
+                flops=int(micros * 1e9),
+                bytes_accessed=2**20 if micros > 0.1 else 2**12,
+                transcendentals=0,
             ),
             name=name,
         )(*args)
@@ -546,7 +548,7 @@
         "temporal_back_projection",
         [sds(nf, 2 * nq * fr, half), sds(3, half // 4, width)],
         [geo] + all_terms + [motion_weights],
-        3,
+        0.01,
     )
     pair_terms[0] = after(pair_terms[0], back_send)
     last_terms = [move(pair_terms[0], flipped(1))]
@@ -562,7 +564,7 @@
         ],
         [geo] + factors + [quarter, table] + all_terms + core_terms
         + pair_terms[:1] + last_terms,
-        3,
+        0.01,
     )
     late_terms = [after(t, back_send, sums) for t in pair_terms[1:]]
     late_terms += [move(t, flipped(1)) for t in late_terms]

time: 112 us -> 119 us (1.062)
  the two profiles are of different devices: /device:TPU:7 before, /device:TPU:1 now
where the time goes in v2:
time: 119 us; the launch traced here: 117 us
  waiting for transfers between devices  35.1 us (29%)
  starting transfers between devices  29.9 us (25%)
  Pallas kernels  23 us (19%)
  blocking collectives  17.5 us (15%)
  local copies, waits for them, and re-layouts  8.25 us (7%)
  other arithmetic  1.87 us (2%)
    ppermute x15, waiting for transfers between devices, move(): return lax.ppermute(x, 'frame', pairs)  25.1 us
    pallas_call x12, Pallas kernels, call(): pl.pallas_call(kernel, out_shape=outs, in_specs=in_specs, out_specs=[pl.B...  23 us
    all_to_all x1, blocking collectives, swap(): return lax.all_to_all(x, 'frame', split_axis=0, concat_axis=0, tiled=True)  17.5 us
    ppermute x15, starting transfers between devices, move(): return lax.ppermute(x, 'frame', pairs)  12.6 us
    ppermute x2, starting transfers between devices, local(): totals = [lax.ppermute(t, ('frame', 'quad'), final) for t in totals]  9.39 us
    ppermute x1, waiting for transfers between devices, to_quad(): return lax.ppermute(x, 'quad', [(d, (d + s) % nq) for d in range(nq)])  8.3 us
    unnamed x38, local copies, waits for them, and re-layouts  8.24 us
    ppermute x4, starting transfers between devices, from_quad(): return lax.ppermute(x, 'quad', [((d + s) % nq, d) for d in range(nq)])  3.76 us
  transfers between devices with their start and end apart: 23, of which 9 were waited for; matrix products, arithmetic and copies ran while one was open for 1% of the time, Pallas kernels for 17%

profile of v2, /device:TPU:1, one launch (start us, length us, event | category | flops | bytes accessed | tf_op | source)
XLA Modules:
  0.0 116.6 jit_solution(11789324851868619177)
XLA Ops:
  0.6 2.1 %collective-permute-start = (bf16[4,16,1280]{2,1,0:T(8,128)(2,1)}, bf16[4,16,1280]{2,1,0:T(8,128)(2,1)S(1)}, u32[]{:S(2)}, u32[]{:S(2)}) collective-permute-start(bf16[4,16,1280]{2,1,0:T(8,128)(2,1)} %xs.1), channel_id=1, source_target_pairs={{1,0},{0,1},{3,2},{2,3},{5,4},{4,5},{7,6},{6,7},{9,8},{8,9},{11,10... | collective-permute-start | bytes 491528 | tf_op jit(solution)/shard_map/ppermute | solution.py:477
  3.1 2.9 %copy-done = bf16[4,1280,640]{2,1,0:T(8,128)(2,1)S(1)} copy-done((bf16[4,1280,640]{2,1,0:T(8,128)(2,1)S(1)}, bf16[4,1280,640]{2,1,0:T(8,128)(2,1)}, u32[]{:S(2)}) %copy-start) | copy-done | bytes 6553624
  8.0 1.7 %copy-done.1 = bf16[4,1280,640]{2,1,0:T(8,128)(2,1)S(1)} copy-done((bf16[4,1280,640]{2,1,0:T(8,128)(2,1)S(1)}, bf16[4,1280,640]{2,1,0:T(8,128)(2,1)}, u32[]{:S(2)}) %copy-start.1) | copy-done | bytes 6553624
  9.8 3.4 %spatial_forward.1 = (bf16[128,3200]{1,0:T(8,128)(2,1)S(1)}, bf16[16,8,640]{2,1,0:T(8,128)(2,1)S(1)}) custom-call(s32[3]{0:T(128)S(1)} %pad_add_fusion.refs_0_.geo.quad_ref, bf16[4,16,1280]{2,1,0:T(8,128)(2,1)S(1)} %copy-done.8, bf16[4,16,1280]{2,1,0:T(8,128)(2,1)S(1)} %collective-permute-done.refs_2_, f32[1280]{0:T(1024)S(1)} %copy-done.14, ...), custom_call_target="tpu_custom_call" | custom-call | flops 3000000000 | bytes 1048576 | tf_op jit(solution)/shard_map/spatial_forward/pallas_call | solution.py:430
  14.0 17.5 %all_to_all.10.received = bf16[16,16,640]{2,1,0:T(8,128)(2,1)S(1)} all-to-all(bf16[16,16,640]{2,1,0:T(8,128)(2,1)S(1)} %join_sent.1), channel_id=1, replica_groups=mesh['frame'=16,'quad'=2] {'frame'}, dimensions={0} | all-to-all | bytes 655360 | tf_op jit(solution)/shard_map/all_to_all | solution.py:483
  33.7 8.3 %collective-permute-done.2.refs_1_ = bf16[64,2560]{1,0:T(8,128)(2,1)S(1)} collective-permute-done((bf16[64,2560]{1,0:T(8,128)(2,1)S(1)}, bf16[64,2560]{1,0:T(8,128)(2,1)S(1)}, u32[]{:S(2)}, u32[]{:S(2)}) %collective-permute-start.2) | collective-permute-done | bytes 327712 | tf_op jit(solution)/shard_map/ppermute | solution.py:480
  45.9 1.9 %cut_factors.1 = (bf16[2,128,160]{2,1,0:T(8,128)(2,1)S(1)}, bf16[2,128,160]{2,1,0:T(8,128)(2,1)}, bf16[2,128,160]{2,1,0:T(8,128)(2,1)S(1)}, bf16[2,128,160]{2,1,0:T(8,128)(2,1)S(1)}) custom-call(s32[3]{0:T(128)S(1)} %pad_add_fusion.refs_0_.geo.quad_ref, bf16[16,16,640]{2,1,0:T(8,128)(2,1)S(1)} %all_to_all.10.received), custom_call_target="tpu_custom_call" | custom-call | flops 500000000 | bytes 1048576 | tf_op jit(solution)/shard_map/cut_factors/pallas_call | solution.py:430
  47.8 1.6 %positional_table.1.refs_5_.pos = f32[64,1280]{1,0:T(8,128)S(1)} custom-call(s32[3]{0:T(128)S(1)} %pad_add_fusion.refs_0_.geo.quad_ref), custom_call_target="tpu_custom_call" | custom-call | flops 1500000000 | bytes 1048576 | tf_op jit(solution)/shard_map/positional_table/pallas_call | solution.py:430
  49.4 1.7 %collective-permute-done.3.refs_1_.refs_7_ = bf16[64,2560]{1,0:T(8,128)(2,1)S(1)} collective-permute-done((bf16[64,2560]{1,0:T(8,128)(2,1)S(1)}, bf16[64,2560]{1,0:T(8,128)(2,1)S(1)}, u32[]{:S(2)}, u32[]{:S(2)}) %collective-permute-start.3) | collective-permute-done | bytes 327712 | tf_op jit(solution)/shard_map/ppermute | solution.py:477
  51.1 2.5 %temporal_back_projection.1 = (bf16[16,16,640]{2,1,0:T(8,128)(2,1)}, bf16[3,160,640]{2,1,0:T(8,128)(2,1)S(1)}) custom-call(s32[3]{0:T(128)S(1)} %pad_add_fusion.refs_0_.geo.quad_ref, bf16[64,2560]{1,0:T(8,128)(2,1)S(1)} %temporal_attention.1.refs_0_.refs_6_, bf16[64,2560]{1,0:T(8,128)(2,1)S(1)} %collective-permute-done.3.refs_1_.refs_7_, ...), custom_call_target="tpu_custom_call" | custom-call | flops 10000000 | bytes 4096 | tf_op jit(solution)/shard_map/temporal_back_projection/pallas_call | solution.py:430
  53.6 2.2 %collective-permute-start.11 = (bf16[64,2560]{1,0:T(8,128)(2,1)S(1)}, bf16[64,2560]{1,0:T(8,128)(2,1)S(1)}, u32[]{:S(2)}, u32[]{:S(2)}) collective-permute-start(bf16[64,2560]{1,0:T(8,128)(2,1)S(1)} %collective-permute-done.10.refs_10_), channel_id=1, source_target_pairs={{0,2},{2,0},{4,6},{6,4},{8,10},{10,8},{12,14},{14,12},{16,18},{18,... | collective-permute-start | bytes 983048 | tf_op jit(solution)/shard_map/ppermute | solution.py:490
  57.8 3.4 %all-to-all-start.1 = ((bf16[16,16,640]{2,1,0:T(8,128)(2,1)}), bf16[16,16,640]{2,1,0:T(8,128)(2,1)S(1)}, u32[]{:S(2)}, u32[]{:S(2)}) async-start(bf16[16,16,640]{2,1,0:T(8,128)(2,1)} %get-tuple-element.46), calls=%async_computation.1 | async-start | bytes 655360 | tf_op jit(solution)/shard_map/all_to_all | solution.py:483
  63.2 7.1 %collective-permute-done.6.refs_2_ = bf16[2,128,160]{2,1,0:T(8,128)(2,1)S(1)} collective-permute-done((bf16[2,128,160]{2,1,0:T(8,128)(2,1)}, bf16[2,128,160]{2,1,0:T(8,128)(2,1)S(1)}, u32[]{:S(2)}, u32[]{:S(2)}) %collective-permute-start.6) | collective-permute-done | bytes 81952 | tf_op jit(solution)/shard_map/ppermute | solution.py:490
  70.2 3.1 %collective-permute-start.7 = (bf16[2,128,160]{2,1,0:T(8,128)(2,1)}, bf16[2,128,160]{2,1,0:T(8,128)(2,1)S(1)}, u32[]{:S(2)}, u32[]{:S(2)}) collective-permute-start(bf16[2,128,160]{2,1,0:T(8,128)(2,1)} %copy-done.12), channel_id=1, source_target_pairs={{0,6},{2,4},{4,2},{6,0},{8,14},{10,12},{12,10},{14,8},{16,22},{18,... | collective-permute-start | bytes 245768 | tf_op jit(solution)/shard_map/ppermute | solution.py:490
  73.3 3.7 %collective-permute-done.7.refs_3_ = bf16[2,128,160]{2,1,0:T(8,128)(2,1)S(1)} collective-permute-done((bf16[2,128,160]{2,1,0:T(8,128)(2,1)}, bf16[2,128,160]{2,1,0:T(8,128)(2,1)S(1)}, u32[]{:S(2)}, u32[]{:S(2)}) %collective-permute-start.7) | collective-permute-done | bytes 81952 | tf_op jit(solution)/shard_map/ppermute | solution.py:490
  77.9 2.2 %weight_terms_first_tokens.1 = (f32[4,4,40,640]{3,2,1,0:T(8,128)S(1)}, f32[1,160]{1,0:T(1,128)S(1)}, bf16[2,128,160]{2,1,0:T(8,128)(2,1)S(1)}) custom-call(s32[3]{0:T(128)S(1)} %pad_add_fusion.refs_0_.geo.quad_ref, bf16[2,128,160]{2,1,0:T(8,128)(2,1)S(1)} %get-tuple-element.43.refs_0_, bf16[2,128,160]{2,1,0:T(8,128)(2,1)S(1)} %copy-done.6, ...), custom_call_target="tpu_custom_call" | custom-call | flops 10000000 | bytes 4096 | tf_op jit(solution)/shard_map/weight_terms_first_tokens/pallas_call | solution.py:430
  85.2 4.3 %collective-permute-done.17 = bf16[80,640]{1,0:T(8,128)(2,1)S(1)} collective-permute-done((bf16[80,640]{1,0:T(8,128)(2,1)S(1)}, bf16[80,640]{1,0:T(8,128)(2,1)S(1)}, u32[]{:S(2)}, u32[]{:S(2)}) %collective-permute-start.17) | collective-permute-done | bytes 102432 | tf_op jit(solution)/shard_map/ppermute | solution.py:490
  89.6 1.8 %collective-permute-done.14 = bf16[88,640]{1,0:T(8,128)(2,1)S(1)} collective-permute-done((bf16[88,640]{1,0:T(8,128)(2,1)S(1)}, bf16[88,640]{1,0:T(8,128)(2,1)S(1)}, u32[]{:S(2)}, u32[]{:S(2)}) %collective-permute-start.14) | collective-permute-done | bytes 112672 | tf_op jit(solution)/shard_map/ppermute | solution.py:490
  91.5 3.3 %collective-permute-done.18 = bf16[80,640]{1,0:T(8,128)(2,1)S(1)} collective-permute-done((bf16[80,640]{1,0:T(8,128)(2,1)S(1)}, bf16[80,640]{1,0:T(8,128)(2,1)S(1)}, u32[]{:S(2)}, u32[]{:S(2)}) %collective-permute-start.18) | collective-permute-done | bytes 102432 | tf_op jit(solution)/shard_map/ppermute | solution.py:490
  95.0 3.5 %collective-permute-done.15 = bf16[88,640]{1,0:T(8,128)(2,1)S(1)} collective-permute-done((bf16[88,640]{1,0:T(8,128)(2,1)S(1)}, bf16[88,640]{1,0:T(8,128)(2,1)S(1)}, u32[]{:S(2)}, u32[]{:S(2)}) %collective-permute-start.15) | collective-permute-done | bytes 112672 | tf_op jit(solution)/shard_map/ppermute | solution.py:490
  99.9 1.7 %block_output_hidden_gradient.1 = (bf16[4,16,1280]{2,1,0:T(8,128)(2,1)}, bf16[128,1280]{1,0:T(8,128)(2,1)S(1)}) custom-call(s32[3]{0:T(128)S(1)} %pad_add_fusion.refs_0_.geo.quad_ref, bf16[16,16,640]{2,1,0:T(8,128)(2,1)S(1)} %all-to-all-done.1.refs_1_, bf16[16,16,640]{2,1,0:T(8,128)(2,1)S(1)} %collective-permute-done.4.refs_2_, ...), custom_call_target="tpu_custom_call" | custom-call | flops 6000000000 | bytes 1048576 | tf_op jit(solution)/shard_map/block_output_hidden_gradient/pallas_call | solution.py:430
  101.6 4.0 %collective-permute-start.21 = (bf16[80,640]{1,0:T(8,128)(2,1)S(1)}, bf16[80,640]{1,0:T(8,128)(2,1)S(1)}, u32[]{:S(2)}, u32[]{:S(2)}) collective-permute-start(bf16[80,640]{1,0:T(8,128)(2,1)S(1)} %add_convert_fusion.3), channel_id=1, source_target_pairs={{0,0},{1,16},{2,8},{3,24},{4,4},{5,20},{6,12},{7,28},{8,1},{9,17},... | collective-permute-start | bytes 307208 | tf_op jit(solution)/shard_map/ppermute | solution.py:608
  105.7 5.4 %collective-permute-start.20 = (bf16[88,640]{1,0:T(8,128)(2,1)S(1)}, bf16[88,640]{1,0:T(8,128)(2,1)S(1)}, u32[]{:S(2)}, u32[]{:S(2)}) collective-permute-start(bf16[88,640]{1,0:T(8,128)(2,1)S(1)} %add_convert_fusion), channel_id=1, source_target_pairs={{0,0},{1,16},{2,8},{3,24},{4,4},{5,20},{6,12},{7,28},{8,1},{9,17},... | collective-permute-start | bytes 337928 | tf_op jit(solution)/shard_map/ppermute | solution.py:608
  111.1 4.1 %spatial_backward.1 = bf16[4,16,1280]{2,1,0:T(8,128)(2,1)} custom-call(bf16[128,1280]{1,0:T(8,128)(2,1)S(1)} %get-tuple-element.71.grad_hidden, bf16[4,16,1280]{2,1,0:T(8,128)(2,1)S(1)} %copy-done.9, bf16[128,3200]{1,0:T(8,128)(2,1)S(1)} %copy-done.16, f32[1280]{0:T(1024)S(1)} %copy-done.14, bf16[4,1280,640]{2,1,0:T(8,128)(2,1)S(1)} %bitcast.7), custom_call_target="tpu_custom_call" | custom-call | flops 3500000000 | bytes 1048576 | tf_op jit(solution)/shard_map/spatial_backward/pallas_call | solution.py:430
  (88 shorter events, 22.3 us)
Async XLA Ops:
  0.6 7.0 %collective-permute-start = (bf16[4,16,1280]{2,1,0:T(8,128)(2,1)}, bf16[4,16,1280]{2,1,0:T(8,128)(2,1)S(1)}, u32[]{:S(2)}, u32[]{:S(2)}) collective-permute-start(bf16[4,16,1280]{2,1,0:T(8,128)(2,1)} %xs.1), channel_id=1, source_target_pairs={{1,0},{0,1},{3,2},{2,3},{5,4},{4,5},{7,6},{6,7},{9,8},{8,9},{11,10... | collective-permute-start | bytes 491528 | tf_op jit(solution)/shard_map/ppermute | solution.py:477
  7.6 23.9 %copy-start.2 = (bf16[4,640,640]{2,1,0:T(8,128)(2,1)S(1)}, bf16[4,640,640]{2,1,0:T(8,128)(2,1)}, u32[]{:S(2)}) copy-start(bf16[4,640,640]{2,1,0:T(8,128)(2,1)} %refs_2_.1) | copy-start | bytes 9830404
  7.6 5.6 %collective-permute-start.1 = (bf16[4,16,1280]{2,1,0:T(8,128)(2,1)S(1)}, bf16[4,16,1280]{2,1,0:T(8,128)(2,1)S(1)}, u32[]{:S(2)}, u32[]{:S(2)}) collective-permute-start(bf16[4,16,1280]{2,1,0:T(8,128)(2,1)S(1)} %copy-done.3), channel_id=1, source_target_pairs={{1,0},{0,1},{3,2},{2,3},{5,4},{4,5},{7,6},{6,7},{9,8},{8,9},{11,10... | collective-permute-start | bytes 491528 | tf_op jit(solution)/shard_map/ppermute | solution.py:477
  33.0 9.0 %collective-permute-start.2 = (bf16[64,2560]{1,0:T(8,128)(2,1)S(1)}, bf16[64,2560]{1,0:T(8,128)(2,1)S(1)}, u32[]{:S(2)}, u32[]{:S(2)}) collective-permute-start(bf16[64,2560]{1,0:T(8,128)(2,1)S(1)} %get-tuple-element.41), channel_id=1, source_target_pairs={{0,1},{1,0},{2,3},{3,2},{4,5},{5,4},{6,7},{7,6},{8,9},{9,8},{10,11... | collective-permute-start | bytes 983048 | tf_op jit(solution)/shard_map/ppermute | solution.py:480
  43.1 8.0 %collective-permute-start.3 = (bf16[64,2560]{1,0:T(8,128)(2,1)S(1)}, bf16[64,2560]{1,0:T(8,128)(2,1)S(1)}, u32[]{:S(2)}, u32[]{:S(2)}) collective-permute-start(bf16[64,2560]{1,0:T(8,128)(2,1)S(1)} %temporal_attention.1.refs_0_.refs_6_), channel_id=1, source_target_pairs={{1,0},{0,1},{3,2},{2,3},{5,4},{4,5},{7,6},{6,7},{9,8},{8,9},{11,10... | collective-permute-start | bytes 983048 | tf_op jit(solution)/shard_map/ppermute | solution.py:477
  43.7 9.9 %collective-permute-start.10 = (bf16[64,2560]{1,0:T(8,128)(2,1)S(1)}, bf16[64,2560]{1,0:T(8,128)(2,1)S(1)}, u32[]{:S(2)}, u32[]{:S(2)}) collective-permute-start(bf16[64,2560]{1,0:T(8,128)(2,1)S(1)} %temporal_attention.1.refs_0_.refs_6_), channel_id=1, source_target_pairs={{0,4},{2,6},{4,0},{6,2},{8,12},{10,14},{12,8},{14,10},{16,20},{18,... | collective-permute-start | bytes 983048 | tf_op jit(solution)/shard_map/ppermute | solution.py:490
  44.9 32.1 %collective-permute-start.8 = (bf16[64,2560]{1,0:T(8,128)(2,1)S(1)}, bf16[64,2560]{1,0:T(8,128)(2,1)S(1)}, u32[]{:S(2)}, u32[]{:S(2)}) collective-permute-start(bf16[64,2560]{1,0:T(8,128)(2,1)S(1)} %temporal_attention.1.refs_0_.refs_6_), channel_id=1, source_target_pairs={{0,2},{2,0},{4,6},{6,4},{8,10},{10,8},{12,14},{14,12},{16,18},{18,... | collective-permute-start | bytes 983048 | tf_op jit(solution)/shard_map/ppermute | solution.py:490
  53.6 23.3 %collective-permute-start.11 = (bf16[64,2560]{1,0:T(8,128)(2,1)S(1)}, bf16[64,2560]{1,0:T(8,128)(2,1)S(1)}, u32[]{:S(2)}, u32[]{:S(2)}) collective-permute-start(bf16[64,2560]{1,0:T(8,128)(2,1)S(1)} %collective-permute-done.10.refs_10_), channel_id=1, source_target_pairs={{0,2},{2,0},{4,6},{6,4},{8,10},{10,8},{12,14},{14,12},{16,18},{18,... | collective-permute-start | bytes 983048 | tf_op jit(solution)/shard_map/ppermute | solution.py:490
  55.8 21.2 %collective-permute-start.9 = (bf16[64,2560]{1,0:T(8,128)(2,1)S(1)}, bf16[64,2560]{1,0:T(8,128)(2,1)}, u32[]{:S(2)}, u32[]{:S(2)}) collective-permute-start(bf16[64,2560]{1,0:T(8,128)(2,1)S(1)} %collective-permute-done.3.refs_1_.refs_7_), channel_id=1, source_target_pairs={{0,2},{2,0},{4,6},{6,4},{8,10},{10,8},{12,14},{14,12},{16,18},{18,... | collective-permute-start | bytes 983048 | tf_op jit(solution)/shard_map/ppermute | solution.py:490
  55.8 24.3 %collective-permute-start.12 = (bf16[64,2560]{1,0:T(8,128)(2,1)S(1)}, bf16[64,2560]{1,0:T(8,128)(2,1)S(1)}, u32[]{:S(2)}, u32[]{:S(2)}) collective-permute-start(bf16[64,2560]{1,0:T(8,128)(2,1)S(1)} %collective-permute-done.3.refs_1_.refs_7_), channel_id=1, source_target_pairs={{0,4},{2,6},{4,0},{6,2},{8,12},{10,14},{12,8},{14,10},{16,20},{18,... | collective-permute-start | bytes 983048 | tf_op jit(solution)/shard_map/ppermute | solution.py:490
  57.0 4.2 %collective-permute-start.5 = (bf16[2,128,160]{2,1,0:T(8,128)(2,1)}, bf16[2,128,160]{2,1,0:T(8,128)(2,1)S(1)}, u32[]{:S(2)}, u32[]{:S(2)}) collective-permute-start(bf16[2,128,160]{2,1,0:T(8,128)(2,1)} %get-tuple-element.50), channel_id=1, source_target_pairs={{0,2},{2,0},{4,6},{6,4},{8,10},{10,8},{12,14},{14,12},{16,18},{18,... | collective-permute-start | bytes 245768 | tf_op jit(solution)/shard_map/ppermute | solution.py:490
  57.8 26.7 %all-to-all-start.1 = ((bf16[16,16,640]{2,1,0:T(8,128)(2,1)}), bf16[16,16,640]{2,1,0:T(8,128)(2,1)S(1)}, u32[]{:S(2)}, u32[]{:S(2)}) async-start(bf16[16,16,640]{2,1,0:T(8,128)(2,1)} %get-tuple-element.46), calls=%async_computation.1 | async-start | bytes 655360 | tf_op jit(solution)/shard_map/all_to_all | solution.py:483
  61.9 8.3 %collective-permute-start.6 = (bf16[2,128,160]{2,1,0:T(8,128)(2,1)}, bf16[2,128,160]{2,1,0:T(8,128)(2,1)S(1)}, u32[]{:S(2)}, u32[]{:S(2)}) collective-permute-start(bf16[2,128,160]{2,1,0:T(8,128)(2,1)} %copy-done.13), channel_id=1, source_target_pairs={{0,4},{2,6},{4,0},{6,2},{8,12},{10,14},{12,8},{14,10},{16,20},{18,... | collective-permute-start | bytes 245768 | tf_op jit(solution)/shard_map/ppermute | solution.py:490
  70.2 6.7 %collective-permute-start.7 = (bf16[2,128,160]{2,1,0:T(8,128)(2,1)}, bf16[2,128,160]{2,1,0:T(8,128)(2,1)S(1)}, u32[]{:S(2)}, u32[]{:S(2)}) collective-permute-start(bf16[2,128,160]{2,1,0:T(8,128)(2,1)} %copy-done.12), channel_id=1, source_target_pairs={{0,6},{2,4},{4,2},{6,0},{8,14},{10,12},{12,10},{14,8},{16,22},{18,... | collective-permute-start | bytes 245768 | tf_op jit(solution)/shard_map/ppermute | solution.py:490
  80.1 1.7 %collective-permute-start.13 = (bf16[64,2560]{1,0:T(8,128)(2,1)S(1)}, bf16[64,2560]{1,0:T(8,128)(2,1)S(1)}, u32[]{:S(2)}, u32[]{:S(2)}) collective-permute-start(bf16[64,2560]{1,0:T(8,128)(2,1)S(1)} %collective-permute-done.12.refs_0_), channel_id=1, source_target_pairs={{0,2},{2,0},{4,6},{6,4},{8,10},{10,8},{12,14},{14,12},{16,18},{18,... | collective-permute-start | bytes 983048 | tf_op jit(solution)/shard_map/ppermute | solution.py:490
  83.3 6.2 %collective-permute-start.17 = (bf16[80,640]{1,0:T(8,128)(2,1)S(1)}, bf16[80,640]{1,0:T(8,128)(2,1)S(1)}, u32[]{:S(2)}, u32[]{:S(2)}) collective-permute-start(bf16[80,640]{1,0:T(8,128)(2,1)S(1)} %get-tuple-element.65), channel_id=1, source_target_pairs={{0,8},{2,10},{4,12},{6,14},{8,16},{10,18},{12,20},{14,22},{16,24},... | collective-permute-start | bytes 307208 | tf_op jit(solution)/shard_map/ppermute | solution.py:490
  84.5 14.2 %collective-permute-start.4 = (bf16[16,16,640]{2,1,0:T(8,128)(2,1)S(1)}, bf16[16,16,640]{2,1,0:T(8,128)(2,1)S(1)}, u32[]{:S(2)}, u32[]{:S(2)}) collective-permute-start(bf16[16,16,640]{2,1,0:T(8,128)(2,1)S(1)} %all-to-all-done.1.refs_1_), channel_id=1, source_target_pairs={{1,0},{0,1},{3,2},{2,3},{5,4},{4,5},{7,6},{6,7},{9,8},{8,9},{11,10... | collective-permute-start | bytes 983048 | tf_op jit(solution)/shard_map/ppermute | solution.py:477
  85.1 6.3 %collective-permute-start.14 = (bf16[88,640]{1,0:T(8,128)(2,1)S(1)}, bf16[88,640]{1,0:T(8,128)(2,1)S(1)}, u32[]{:S(2)}, u32[]{:S(2)}) collective-permute-start(bf16[88,640]{1,0:T(8,128)(2,1)S(1)} %get-tuple-element.59), channel_id=1, source_target_pairs={{0,8},{2,10},{4,12},{6,14},{8,16},{10,18},{12,20},{14,22},{16,24},... | collective-permute-start | bytes 337928 | tf_op jit(solution)/shard_map/ppermute | solution.py:490
  89.5 5.4 %collective-permute-start.18 = (bf16[80,640]{1,0:T(8,128)(2,1)S(1)}, bf16[80,640]{1,0:T(8,128)(2,1)S(1)}, u32[]{:S(2)}, u32[]{:S(2)}) collective-permute-start(bf16[80,640]{1,0:T(8,128)(2,1)S(1)} %add_convert_fusion.5), channel_id=1, source_target_pairs={{0,8},{2,10},{4,12},{6,14},{8,16},{10,18},{12,20},{14,22},{16,24},... | collective-permute-start | bytes 307208 | tf_op jit(solution)/shard_map/ppermute | solution.py:490
  91.4 7.0 %collective-permute-start.15 = (bf16[88,640]{1,0:T(8,128)(2,1)S(1)}, bf16[88,640]{1,0:T(8,128)(2,1)S(1)}, u32[]{:S(2)}, u32[]{:S(2)}) collective-permute-start(bf16[88,640]{1,0:T(8,128)(2,1)S(1)} %add_convert_fusion.2), channel_id=1, source_target_pairs={{0,8},{2,10},{4,12},{6,14},{8,16},{10,18},{12,20},{14,22},{16,24},... | collective-permute-start | bytes 337928 | tf_op jit(solution)/shard_map/ppermute | solution.py:490
  94.9 6.6 %collective-permute-start.19 = (bf16[80,640]{1,0:T(8,128)(2,1)S(1)}, bf16[80,640]{1,0:T(8,128)(2,1)S(1)}, u32[]{:S(2)}, u32[]{:S(2)}) collective-permute-start(bf16[80,640]{1,0:T(8,128)(2,1)S(1)} %add_convert_fusion.4), channel_id=1, source_target_pairs={{0,8},{2,10},{4,12},{6,14},{8,16},{10,18},{12,20},{14,22},{16,24},... | collective-permute-start | bytes 307208 | tf_op jit(solution)/shard_map/ppermute | solution.py:490
  98.4 7.2 %collective-permute-start.16 = (bf16[88,640]{1,0:T(8,128)(2,1)S(1)}, bf16[88,640]{1,0:T(8,128)(2,1)S(1)}, u32[]{:S(2)}, u32[]{:S(2)}) collective-permute-start(bf16[88,640]{1,0:T(8,128)(2,1)S(1)} %add_convert_fusion.1), channel_id=1, source_target_pairs={{0,8},{2,10},{4,12},{6,14},{8,16},{10,18},{12,20},{14,22},{16,24},... | collective-permute-start | bytes 337928 | tf_op jit(solution)/shard_map/ppermute | solution.py:490
  101.6 14.2 %collective-permute-start.21 = (bf16[80,640]{1,0:T(8,128)(2,1)S(1)}, bf16[80,640]{1,0:T(8,128)(2,1)S(1)}, u32[]{:S(2)}, u32[]{:S(2)}) collective-permute-start(bf16[80,640]{1,0:T(8,128)(2,1)S(1)} %add_convert_fusion.3), channel_id=1, source_target_pairs={{0,0},{1,16},{2,8},{3,24},{4,4},{5,20},{6,12},{7,28},{8,1},{9,17},... | collective-permute-start | bytes 307208 | tf_op jit(solution)/shard_map/ppermute | solution.py:608
  105.7 9.5 %collective-permute-start.20 = (bf16[88,640]{1,0:T(8,128)(2,1)S(1)}, bf16[88,640]{1,0:T(8,128)(2,1)S(1)}, u32[]{:S(2)}, u32[]{:S(2)}) collective-permute-start(bf16[88,640]{1,0:T(8,128)(2,1)S(1)} %add_convert_fusion), channel_id=1, source_target_pairs={{0,0},{1,16},{2,8},{3,24},{4,4},{5,20},{6,12},{7,28},{8,1},{9,17},... | collective-permute-start | bytes 337928 | tf_op jit(solution)/shard_map/ppermute | solution.py:608
  (18 other events, 157.3 us)

commit v3 on v2

--- a/solution.py
+++ b/solution.py
@@ -523,15 +523,17 @@
         [geo, received, motion_weights],
         1.5,
     )
-    parts = [parts[0]] + [to_quad(p, s + 1) for s, p in enumerate(parts[1:])]
-    (terms,) = run(temporal_kernel, "temporal_attention", [sds(tokens, 4 * width)], parts, 2)
     factors = run(
         cut_kernel,
         "cut_factors",
         [sds(2, rows, half // 4)] * 4,
-        [geo, after(received, terms)],
+        [geo, after(received, parts[0])],
         0.5,
     )
+    factors = [factors[0]] + [move(factors[d], flipped(d)) for d in range(1, 4)]
+    parts = [after(parts[0], factors[0])] + [to_quad(p, s + 1) for s, p in enumerate(parts[1:])]
+    (terms,) = run(temporal_kernel, "temporal_attention", [sds(tokens, 4 * width)], parts, 2)
+    terms = after(terms, *factors)
     (table,) = run(
         table_kernel,
         "positional_table",
@@ -539,10 +541,9 @@
         [after(geo, terms)],
         1.5,
     )
-    all_terms = [terms] + [after(from_quad(terms, s), factors[0], table) for s in range(1, nq)]
+    all_terms = [terms] + [after(from_quad(terms, s), table) for s in range(1, nq)]
     pair_terms = [move(t, flipped(2)) for t in all_terms]
     core_terms = [move(t, flipped(1)) for t in all_terms]
-    factors = [factors[0]] + [move(factors[d], flipped(d)) for d in range(1, 4)]
     back_send, quarter = run(
         back_kernel,
         "temporal_back_projection",

time: 119 us -> 108 us (0.908)
  the two profiles are of different devices: /device:TPU:1 before, /device:TPU:7 now
where the time goes in v3:
time: 108 us
  starting transfers between devices  28.1 us (26%)
  waiting for transfers between devices  27 us (25%)
  Pallas kernels  22.4 us (21%)
  blocking collectives  17 us (16%)
  local copies, waits for them, and re-layouts  10.5 us (10%)
  other arithmetic  1.87 us (2%)
    pallas_call x12, Pallas kernels, call(): pl.pallas_call(kernel, out_shape=outs, in_specs=in_specs, out_specs=[pl.B...  22.4 us
    all_to_all x1, blocking collectives, swap(): return lax.all_to_all(x, 'frame', split_axis=0, concat_axis=0, tiled=True)  17 us
    ppermute x15, waiting for transfers between devices, move(): return lax.ppermute(x, 'frame', pairs)  14.3 us
    unnamed x42, local copies, waits for them, and re-layouts  10.4 us
    ppermute x2, starting transfers between devices, local(): totals = [lax.ppermute(t, ('frame', 'quad'), final) for t in totals]  9.83 us
    ppermute x15, starting transfers between devices, move(): return lax.ppermute(x, 'frame', pairs)  8.9 us
    ppermute x1, waiting for transfers between devices, to_quad(): return lax.ppermute(x, 'quad', [(d, (d + s) % nq) for d in range(nq)])  5.31 us
    all_to_all x1, starting transfers between devices, swap(): return lax.all_to_all(x, 'frame', split_axis=0, concat_axis=0, tiled=True)  5.21 us
  transfers between devices with their start and end apart: 23, of which 10 were waited for; matrix products, arithmetic and copies ran while one was open for 1% of the time, Pallas kernels for 19%

profile of v3, /device:TPU:7, one launch (start us, length us, event | category | flops | bytes accessed | tf_op | source)
XLA Modules:
  0.0 107.8 jit_solution(15569828394540421030)
XLA Ops:
  1.3 2.9 %copy-done = bf16[4,1280,640]{2,1,0:T(8,128)(2,1)S(1)} copy-done((bf16[4,1280,640]{2,1,0:T(8,128)(2,1)S(1)}, bf16[4,1280,640]{2,1,0:T(8,128)(2,1)}, u32[]{:S(2)}) %copy-start) | copy-done | bytes 6553624
  7.9 3.4 %spatial_forward.1 = (bf16[128,3200]{1,0:T(8,128)(2,1)S(1)}, bf16[16,8,640]{2,1,0:T(8,128)(2,1)S(1)}) custom-call(s32[3]{0:T(128)S(1)} %pad_add_fusion.refs_0_.geo.quad_ref, bf16[4,16,1280]{2,1,0:T(8,128)(2,1)S(1)} %copy-done.12, bf16[4,16,1280]{2,1,0:T(8,128)(2,1)S(1)} %collective-permute-done.refs_2_, f32[1280]{0:T(1024)S(1)} %copy-done.16, ...), custom_call_target="tpu_custom_call" | custom-call | flops 3000000000 | bytes 1048576 | tf_op jit(solution)/shard_map/spatial_forward/pallas_call | solution.py:430
  12.2 17.0 %all_to_all.10.received = bf16[16,16,640]{2,1,0:T(8,128)(2,1)S(1)} all-to-all(bf16[16,16,640]{2,1,0:T(8,128)(2,1)S(1)} %join_sent.1), channel_id=1, replica_groups=mesh['frame'=16,'quad'=2] {'frame'}, dimensions={0} | all-to-all | bytes 655360 | tf_op jit(solution)/shard_map/all_to_all | solution.py:483
  29.2 1.5 %motion_projection.1 = (f32[64,2560]{1,0:T(8,128)S(1)}, bf16[64,2560]{1,0:T(8,128)(2,1)S(1)}) custom-call(s32[3]{0:T(128)S(1)} %pad_add_fusion.refs_0_.geo.quad_ref, bf16[16,16,640]{2,1,0:T(8,128)(2,1)S(1)} %all_to_all.10.received, bf16[4,640,640]{2,1,0:T(8,128)(2,1)S(1)} %copy-done.2), custom_call_target="tpu_custom_call" | custom-call | flops 1500000000 | bytes 1048576 | tf_op jit(solution)/shard_map/motion_projection/pallas_call | solution.py:430
  33.0 1.7 %collective-permute-start.4 = (bf16[2,128,160]{2,1,0:T(8,128)(2,1)S(1)}, bf16[2,128,160]{2,1,0:T(8,128)(2,1)S(1)}, u32[]{:S(2)}, u32[]{:S(2)}) collective-permute-start(bf16[2,128,160]{2,1,0:T(8,128)(2,1)S(1)} %get-tuple-element.48), channel_id=1, source_target_pairs={{0,4},{2,6},{4,0},{6,2},{8,12},{10,14},{12,8},{14,10},{16,20},{18,... | collective-permute-start | bytes 245768 | tf_op jit(solution)/shard_map/ppermute | solution.py:490
  35.1 5.3 %collective-permute-done.2.refs_1_ = bf16[64,2560]{1,0:T(8,128)(2,1)S(1)} collective-permute-done((bf16[64,2560]{1,0:T(8,128)(2,1)S(1)}, bf16[64,2560]{1,0:T(8,128)(2,1)S(1)}, u32[]{:S(2)}, u32[]{:S(2)}) %collective-permute-start.2) | collective-permute-done | bytes 327712 | tf_op jit(solution)/shard_map/ppermute | solution.py:480
  44.7 1.8 %collective-permute-start.8 = (bf16[64,2560]{1,0:T(8,128)(2,1)S(1)}, bf16[64,2560]{1,0:T(8,128)(2,1)S(1)}, u32[]{:S(2)}, u32[]{:S(2)}) collective-permute-start(bf16[64,2560]{1,0:T(8,128)(2,1)S(1)} %temporal_attention.1.refs_0_.refs_6_), channel_id=1, source_target_pairs={{0,2},{2,0},{4,6},{6,4},{8,10},{10,8},{12,14},{14,12},{16,18},{18,... | collective-permute-start | bytes 983048 | tf_op jit(solution)/shard_map/ppermute | solution.py:490
  46.5 1.6 %positional_table.1.refs_5_.pos = f32[64,1280]{1,0:T(8,128)S(1)} custom-call(s32[3]{0:T(128)S(1)} %pad_add_fusion.refs_0_.geo.quad_ref), custom_call_target="tpu_custom_call" | custom-call | flops 1500000000 | bytes 1048576 | tf_op jit(solution)/shard_map/positional_table/pallas_call | solution.py:430
  48.2 4.2 %collective-permute-done.6.refs_1_.refs_7_ = bf16[64,2560]{1,0:T(8,128)(2,1)S(1)} collective-permute-done((bf16[64,2560]{1,0:T(8,128)(2,1)S(1)}, bf16[64,2560]{1,0:T(8,128)(2,1)S(1)}, u32[]{:S(2)}, u32[]{:S(2)}) %collective-permute-start.6) | collective-permute-done | bytes 327712 | tf_op jit(solution)/shard_map/ppermute | solution.py:477
  52.3 2.5 %temporal_back_projection.1 = (bf16[16,16,640]{2,1,0:T(8,128)(2,1)}, bf16[3,160,640]{2,1,0:T(8,128)(2,1)S(1)}) custom-call(s32[3]{0:T(128)S(1)} %pad_add_fusion.refs_0_.geo.quad_ref, bf16[64,2560]{1,0:T(8,128)(2,1)S(1)} %temporal_attention.1.refs_0_.refs_6_, bf16[64,2560]{1,0:T(8,128)(2,1)S(1)} %collective-permute-done.6.refs_1_.refs_7_, ...), custom_call_target="tpu_custom_call" | custom-call | flops 10000000 | bytes 4096 | tf_op jit(solution)/shard_map/temporal_back_projection/pallas_call | solution.py:430
  54.9 1.3 %collective-permute-start.11 = (bf16[64,2560]{1,0:T(8,128)(2,1)S(1)}, bf16[64,2560]{1,0:T(8,128)(2,1)S(1)}, u32[]{:S(2)}, u32[]{:S(2)}) collective-permute-start(bf16[64,2560]{1,0:T(8,128)(2,1)S(1)} %collective-permute-done.10.refs_10_), channel_id=1, source_target_pairs={{0,2},{2,0},{4,6},{6,4},{8,10},{10,8},{12,14},{14,12},{16,18},{18,... | collective-permute-start | bytes 983048 | tf_op jit(solution)/shard_map/ppermute | solution.py:490
  56.5 5.2 %all-to-all-start.1 = ((bf16[16,16,640]{2,1,0:T(8,128)(2,1)}), bf16[16,16,640]{2,1,0:T(8,128)(2,1)S(1)}, u32[]{:S(2)}, u32[]{:S(2)}) async-start(bf16[16,16,640]{2,1,0:T(8,128)(2,1)} %get-tuple-element.53), calls=%async_computation.1 | async-start | bytes 655360 | tf_op jit(solution)/shard_map/all_to_all | solution.py:483
  64.4 2.2 %weight_terms_first_tokens.1 = (f32[4,4,40,640]{3,2,1,0:T(8,128)S(1)}, f32[1,160]{1,0:T(1,128)S(1)}, bf16[2,128,160]{2,1,0:T(8,128)(2,1)S(1)}) custom-call(s32[3]{0:T(128)S(1)} %pad_add_fusion.refs_0_.geo.quad_ref, bf16[2,128,160]{2,1,0:T(8,128)(2,1)S(1)} %get-tuple-element.44.refs_0_, bf16[2,128,160]{2,1,0:T(8,128)(2,1)S(1)} %copy-done.6, ...), custom_call_target="tpu_custom_call" | custom-call | flops 10000000 | bytes 4096 | tf_op jit(solution)/shard_map/weight_terms_first_tokens/pallas_call | solution.py:430
  66.7 1.8 %collective-permute-start.13 = (bf16[64,2560]{1,0:T(8,128)(2,1)S(1)}, bf16[64,2560]{1,0:T(8,128)(2,1)S(1)}, u32[]{:S(2)}, u32[]{:S(2)}) collective-permute-start(bf16[64,2560]{1,0:T(8,128)(2,1)S(1)} %collective-permute-done.12.refs_0_), channel_id=1, source_target_pairs={{0,2},{2,0},{4,6},{6,4},{8,10},{10,8},{12,14},{14,12},{16,18},{18,... | collective-permute-start | bytes 983048 | tf_op jit(solution)/shard_map/ppermute | solution.py:490
  69.7 1.5 %weight_terms_last_tokens.1 = (bf16[88,640]{1,0:T(8,128)(2,1)S(1)}, bf16[88,640]{1,0:T(8,128)(2,1)S(1)}, bf16[88,640]{1,0:T(8,128)(2,1)S(1)}, bf16[88,640]{1,0:T...) custom-call(s32[3]{0:T(128)S(1)} %pad_add_fusion.refs_0_.geo.quad_re, ...), custom_call_target="tpu_custom_call" | custom-call | flops 10000000 | bytes 4096 | tf_op jit(solution)/shard_map/weight_terms_last_tokens/pallas_call | solution.py:430
  73.2 3.9 %collective-permute-done.17 = bf16[80,640]{1,0:T(8,128)(2,1)S(1)} collective-permute-done((bf16[80,640]{1,0:T(8,128)(2,1)S(1)}, bf16[80,640]{1,0:T(8,128)(2,1)S(1)}, u32[]{:S(2)}, u32[]{:S(2)}) %collective-permute-start.17) | collective-permute-done | bytes 102432 | tf_op jit(solution)/shard_map/ppermute | solution.py:490
  77.2 2.3 %collective-permute-done.14 = bf16[88,640]{1,0:T(8,128)(2,1)S(1)} collective-permute-done((bf16[88,640]{1,0:T(8,128)(2,1)S(1)}, bf16[88,640]{1,0:T(8,128)(2,1)S(1)}, u32[]{:S(2)}, u32[]{:S(2)}) %collective-permute-start.14) | collective-permute-done | bytes 112672 | tf_op jit(solution)/shard_map/ppermute | solution.py:490
  79.6 2.9 %collective-permute-done.18 = bf16[80,640]{1,0:T(8,128)(2,1)S(1)} collective-permute-done((bf16[80,640]{1,0:T(8,128)(2,1)S(1)}, bf16[80,640]{1,0:T(8,128)(2,1)S(1)}, u32[]{:S(2)}, u32[]{:S(2)}) %collective-permute-start.18) | collective-permute-done | bytes 102432 | tf_op jit(solution)/shard_map/ppermute | solution.py:490
  82.6 3.9 %collective-permute-done.15 = bf16[88,640]{1,0:T(8,128)(2,1)S(1)} collective-permute-done((bf16[88,640]{1,0:T(8,128)(2,1)S(1)}, bf16[88,640]{1,0:T(8,128)(2,1)S(1)}, u32[]{:S(2)}, u32[]{:S(2)}) %collective-permute-start.15) | collective-permute-done | bytes 112672 | tf_op jit(solution)/shard_map/ppermute | solution.py:490
  88.0 1.7 %block_output_hidden_gradient.1 = (bf16[4,16,1280]{2,1,0:T(8,128)(2,1)}, bf16[128,1280]{1,0:T(8,128)(2,1)S(1)}) custom-call(s32[3]{0:T(128)S(1)} %pad_add_fusion.refs_0_.geo.quad_ref, bf16[16,16,640]{2,1,0:T(8,128)(2,1)S(1)} %all-to-all-done.1.refs_1_, bf16[16,16,640]{2,1,0:T(8,128)(2,1)S(1)} %collective-permute-done.7.refs_2_, ...), custom_call_target="tpu_custom_call" | custom-call | flops 6000000000 | bytes 1048576 | tf_op jit(solution)/shard_map/block_output_hidden_gradient/pallas_call | solution.py:430
  89.7 7.9 %collective-permute-start.21 = (bf16[80,640]{1,0:T(8,128)(2,1)S(1)}, bf16[80,640]{1,0:T(8,128)(2,1)S(1)}, u32[]{:S(2)}, u32[]{:S(2)}) collective-permute-start(bf16[80,640]{1,0:T(8,128)(2,1)S(1)} %add_convert_fusion.3), channel_id=1, source_target_pairs={{0,0},{1,16},{2,8},{3,24},{4,4},{5,20},{6,12},{7,28},{8,1},{9,17},... | collective-permute-start | bytes 307208 | tf_op jit(solution)/shard_map/ppermute | solution.py:609
  97.6 1.9 %collective-permute-start.20 = (bf16[88,640]{1,0:T(8,128)(2,1)S(1)}, bf16[88,640]{1,0:T(8,128)(2,1)S(1)}, u32[]{:S(2)}, u32[]{:S(2)}) collective-permute-start(bf16[88,640]{1,0:T(8,128)(2,1)S(1)} %add_convert_fusion), channel_id=1, source_target_pairs={{0,0},{1,16},{2,8},{3,24},{4,4},{5,20},{6,12},{7,28},{8,1},{9,17},... | collective-permute-start | bytes 337928 | tf_op jit(solution)/shard_map/ppermute | solution.py:609
  99.6 4.1 %spatial_backward.1 = bf16[4,16,1280]{2,1,0:T(8,128)(2,1)} custom-call(bf16[128,1280]{1,0:T(8,128)(2,1)S(1)} %get-tuple-element.75.grad_hidden, bf16[4,16,1280]{2,1,0:T(8,128)(2,1)S(1)} %copy-done.13, bf16[128,3200]{1,0:T(8,128)(2,1)S(1)} %copy-done.18, f32[1280]{0:T(1024)S(1)} %copy-done.16, bf16[4,1280,640]{2,1,0:T(8,128)(2,1)S(1)} %bitcast.7), custom_call_target="tpu_custom_call" | custom-call | flops 3500000000 | bytes 1048576 | tf_op jit(solution)/shard_map/spatial_backward/pallas_call | solution.py:430
  103.7 2.7 %collective-permute-done.20 = bf16[88,640]{1,0:T(8,128)(2,1)S(1)} collective-permute-done((bf16[88,640]{1,0:T(8,128)(2,1)S(1)}, bf16[88,640]{1,0:T(8,128)(2,1)S(1)}, u32[]{:S(2)}, u32[]{:S(2)}) %collective-permute-start.20) | collective-permute-done | bytes 112672 | tf_op jit(solution)/shard_map/ppermute | solution.py:609
  (92 shorter events, 21.5 us)
Async XLA Ops:
  0.6 5.3 %collective-permute-start = (bf16[4,16,1280]{2,1,0:T(8,128)(2,1)}, bf16[4,16,1280]{2,1,0:T(8,128)(2,1)S(1)}, u32[]{:S(2)}, u32[]{:S(2)}) collective-permute-start(bf16[4,16,1280]{2,1,0:T(8,128)(2,1)} %xs.1), channel_id=1, source_target_pairs={{1,0},{0,1},{3,2},{2,3},{5,4},{4,5},{7,6},{6,7},{9,8},{8,9},{11,10... | collective-permute-start | bytes 491528 | tf_op jit(solution)/shard_map/ppermute | solution.py:477
  5.8 23.5 %copy-start.2 = (bf16[4,640,640]{2,1,0:T(8,128)(2,1)S(1)}, bf16[4,640,640]{2,1,0:T(8,128)(2,1)}, u32[]{:S(2)}) copy-start(bf16[4,640,640]{2,1,0:T(8,128)(2,1)} %refs_2_.1) | copy-start | bytes 9830404
  6.0 5.4 %collective-permute-start.1 = (bf16[4,16,1280]{2,1,0:T(8,128)(2,1)S(1)}, bf16[4,16,1280]{2,1,0:T(8,128)(2,1)S(1)}, u32[]{:S(2)}, u32[]{:S(2)}) collective-permute-start(bf16[4,16,1280]{2,1,0:T(8,128)(2,1)S(1)} %copy-done.3), channel_id=1, source_target_pairs={{1,0},{0,1},{3,2},{2,3},{5,4},{4,5},{7,6},{6,7},{9,8},{8,9},{11,10... | collective-permute-start | bytes 491528 | tf_op jit(solution)/shard_map/ppermute | solution.py:477
  30.7 9.7 %collective-permute-start.2 = (bf16[64,2560]{1,0:T(8,128)(2,1)S(1)}, bf16[64,2560]{1,0:T(8,128)(2,1)S(1)}, u32[]{:S(2)}, u32[]{:S(2)}) collective-permute-start(bf16[64,2560]{1,0:T(8,128)(2,1)S(1)} %get-tuple-element.46), channel_id=1, source_target_pairs={{0,1},{1,0},{2,3},{3,2},{4,5},{5,4},{6,7},{7,6},{8,9},{9,8},{10,11... | collective-permute-start | bytes 983048 | tf_op jit(solution)/shard_map/ppermute | solution.py:480
  33.0 8.6 %collective-permute-start.3 = (bf16[2,128,160]{2,1,0:T(8,128)(2,1)S(1)}, bf16[2,128,160]{2,1,0:T(8,128)(2,1)S(1)}, u32[]{:S(2)}, u32[]{:S(2)}) collective-permute-start(bf16[2,128,160]{2,1,0:T(8,128)(2,1)S(1)} %get-tuple-element.47), channel_id=1, source_target_pairs={{0,2},{2,0},{4,6},{6,4},{8,10},{10,8},{12,14},{14,12},{16,18},{18,... | collective-permute-start | bytes 245768 | tf_op jit(solution)/shard_map/ppermute | solution.py:490
  33.0 9.2 %collective-permute-start.4 = (bf16[2,128,160]{2,1,0:T(8,128)(2,1)S(1)}, bf16[2,128,160]{2,1,0:T(8,128)(2,1)S(1)}, u32[]{:S(2)}, u32[]{:S(2)}) collective-permute-start(bf16[2,128,160]{2,1,0:T(8,128)(2,1)S(1)} %get-tuple-element.48), channel_id=1, source_target_pairs={{0,4},{2,6},{4,0},{6,2},{8,12},{10,14},{12,8},{14,10},{16,20},{18,... | collective-permute-start | bytes 245768 | tf_op jit(solution)/shard_map/ppermute | solution.py:490
  34.7 8.1 %collective-permute-start.5 = (bf16[2,128,160]{2,1,0:T(8,128)(2,1)S(1)}, bf16[2,128,160]{2,1,0:T(8,128)(2,1)S(1)}, u32[]{:S(2)}, u32[]{:S(2)}) collective-permute-start(bf16[2,128,160]{2,1,0:T(8,128)(2,1)S(1)} %get-tuple-element.49), channel_id=1, source_target_pairs={{0,6},{2,4},{4,2},{6,0},{8,14},{10,12},{12,10},{14,8},{16,22},{18,... | collective-permute-start | bytes 245768 | tf_op jit(solution)/shard_map/ppermute | solution.py:490
  43.5 8.8 %collective-permute-start.6 = (bf16[64,2560]{1,0:T(8,128)(2,1)S(1)}, bf16[64,2560]{1,0:T(8,128)(2,1)S(1)}, u32[]{:S(2)}, u32[]{:S(2)}) collective-permute-start(bf16[64,2560]{1,0:T(8,128)(2,1)S(1)} %temporal_attention.1.refs_0_.refs_6_), channel_id=1, source_target_pairs={{1,0},{0,1},{3,2},{2,3},{5,4},{4,5},{7,6},{6,7},{9,8},{8,9},{11,10... | collective-permute-start | bytes 983048 | tf_op jit(solution)/shard_map/ppermute | solution.py:477
  44.4 10.4 %collective-permute-start.10 = (bf16[64,2560]{1,0:T(8,128)(2,1)S(1)}, bf16[64,2560]{1,0:T(8,128)(2,1)S(1)}, u32[]{:S(2)}, u32[]{:S(2)}) collective-permute-start(bf16[64,2560]{1,0:T(8,128)(2,1)S(1)} %temporal_attention.1.refs_0_.refs_6_), channel_id=1, source_target_pairs={{0,4},{2,6},{4,0},{6,2},{8,12},{10,14},{12,8},{14,10},{16,20},{18,... | collective-permute-start | bytes 983048 | tf_op jit(solution)/shard_map/ppermute | solution.py:490
  44.7 17.0 %collective-permute-start.8 = (bf16[64,2560]{1,0:T(8,128)(2,1)S(1)}, bf16[64,2560]{1,0:T(8,128)(2,1)S(1)}, u32[]{:S(2)}, u32[]{:S(2)}) collective-permute-start(bf16[64,2560]{1,0:T(8,128)(2,1)S(1)} %temporal_attention.1.refs_0_.refs_6_), channel_id=1, source_target_pairs={{0,2},{2,0},{4,6},{6,4},{8,10},{10,8},{12,14},{14,12},{16,18},{18,... | collective-permute-start | bytes 983048 | tf_op jit(solution)/shard_map/ppermute | solution.py:490
  54.9 6.9 %collective-permute-start.11 = (bf16[64,2560]{1,0:T(8,128)(2,1)S(1)}, bf16[64,2560]{1,0:T(8,128)(2,1)S(1)}, u32[]{:S(2)}, u32[]{:S(2)}) collective-permute-start(bf16[64,2560]{1,0:T(8,128)(2,1)S(1)} %collective-permute-done.10.refs_10_), channel_id=1, source_target_pairs={{0,2},{2,0},{4,6},{6,4},{8,10},{10,8},{12,14},{14,12},{16,18},{18,... | collective-permute-start | bytes 983048 | tf_op jit(solution)/shard_map/ppermute | solution.py:490
  56.2 5.5 %collective-permute-start.9 = (bf16[64,2560]{1,0:T(8,128)(2,1)S(1)}, bf16[64,2560]{1,0:T(8,128)(2,1)}, u32[]{:S(2)}, u32[]{:S(2)}) collective-permute-start(bf16[64,2560]{1,0:T(8,128)(2,1)S(1)} %collective-permute-done.6.refs_1_.refs_7_), channel_id=1, source_target_pairs={{0,2},{2,0},{4,6},{6,4},{8,10},{10,8},{12,14},{14,12},{16,18},{18,... | collective-permute-start | bytes 983048 | tf_op jit(solution)/shard_map/ppermute | solution.py:490
  56.2 10.5 %collective-permute-start.12 = (bf16[64,2560]{1,0:T(8,128)(2,1)S(1)}, bf16[64,2560]{1,0:T(8,128)(2,1)S(1)}, u32[]{:S(2)}, u32[]{:S(2)}) collective-permute-start(bf16[64,2560]{1,0:T(8,128)(2,1)S(1)} %collective-permute-done.6.refs_1_.refs_7_), channel_id=1, source_target_pairs={{0,4},{2,6},{4,0},{6,2},{8,12},{10,14},{12,8},{14,10},{16,20},{18,... | collective-permute-start | bytes 983048 | tf_op jit(solution)/shard_map/ppermute | solution.py:490
  56.5 15.1 %all-to-all-start.1 = ((bf16[16,16,640]{2,1,0:T(8,128)(2,1)}), bf16[16,16,640]{2,1,0:T(8,128)(2,1)S(1)}, u32[]{:S(2)}, u32[]{:S(2)}) async-start(bf16[16,16,640]{2,1,0:T(8,128)(2,1)} %get-tuple-element.53), calls=%async_computation.1 | async-start | bytes 655360 | tf_op jit(solution)/shard_map/all_to_all | solution.py:483
  66.7 3.0 %collective-permute-start.13 = (bf16[64,2560]{1,0:T(8,128)(2,1)S(1)}, bf16[64,2560]{1,0:T(8,128)(2,1)S(1)}, u32[]{:S(2)}, u32[]{:S(2)}) collective-permute-start(bf16[64,2560]{1,0:T(8,128)(2,1)S(1)} %collective-permute-done.12.refs_0_), channel_id=1, source_target_pairs={{0,2},{2,0},{4,6},{6,4},{8,10},{10,8},{12,14},{14,12},{16,18},{18,... | collective-permute-start | bytes 983048 | tf_op jit(solution)/shard_map/ppermute | solution.py:490
  71.2 5.9 %collective-permute-start.17 = (bf16[80,640]{1,0:T(8,128)(2,1)S(1)}, bf16[80,640]{1,0:T(8,128)(2,1)S(1)}, u32[]{:S(2)}, u32[]{:S(2)}) collective-permute-start(bf16[80,640]{1,0:T(8,128)(2,1)S(1)} %get-tuple-element.69), channel_id=1, source_target_pairs={{0,8},{2,10},{4,12},{6,14},{8,16},{10,18},{12,20},{14,22},{16,24},... | collective-permute-start | bytes 307208 | tf_op jit(solution)/shard_map/ppermute | solution.py:490
  71.6 15.2 %collective-permute-start.7 = (bf16[16,16,640]{2,1,0:T(8,128)(2,1)S(1)}, bf16[16,16,640]{2,1,0:T(8,128)(2,1)S(1)}, u32[]{:S(2)}, u32[]{:S(2)}) collective-permute-start(bf16[16,16,640]{2,1,0:T(8,128)(2,1)S(1)} %all-to-all-done.1.refs_1_), channel_id=1, source_target_pairs={{1,0},{0,1},{3,2},{2,3},{5,4},{4,5},{7,6},{6,7},{9,8},{8,9},{11,10... | collective-permute-start | bytes 983048 | tf_op jit(solution)/shard_map/ppermute | solution.py:477
  72.5 7.1 %collective-permute-start.14 = (bf16[88,640]{1,0:T(8,128)(2,1)S(1)}, bf16[88,640]{1,0:T(8,128)(2,1)S(1)}, u32[]{:S(2)}, u32[]{:S(2)}) collective-permute-start(bf16[88,640]{1,0:T(8,128)(2,1)S(1)} %get-tuple-element.63), channel_id=1, source_target_pairs={{0,8},{2,10},{4,12},{6,14},{8,16},{10,18},{12,20},{14,22},{16,24},... | collective-permute-start | bytes 337928 | tf_op jit(solution)/shard_map/ppermute | solution.py:490
  77.2 5.4 %collective-permute-start.18 = (bf16[80,640]{1,0:T(8,128)(2,1)S(1)}, bf16[80,640]{1,0:T(8,128)(2,1)S(1)}, u32[]{:S(2)}, u32[]{:S(2)}) collective-permute-start(bf16[80,640]{1,0:T(8,128)(2,1)S(1)} %add_convert_fusion.5), channel_id=1, source_target_pairs={{0,8},{2,10},{4,12},{6,14},{8,16},{10,18},{12,20},{14,22},{16,24},... | collective-permute-start | bytes 307208 | tf_op jit(solution)/shard_map/ppermute | solution.py:490
  79.6 6.9 %collective-permute-start.15 = (bf16[88,640]{1,0:T(8,128)(2,1)S(1)}, bf16[88,640]{1,0:T(8,128)(2,1)S(1)}, u32[]{:S(2)}, u32[]{:S(2)}) collective-permute-start(bf16[88,640]{1,0:T(8,128)(2,1)S(1)} %add_convert_fusion.2), channel_id=1, source_target_pairs={{0,8},{2,10},{4,12},{6,14},{8,16},{10,18},{12,20},{14,22},{16,24},... | collective-permute-start | bytes 337928 | tf_op jit(solution)/shard_map/ppermute | solution.py:490
  82.6 7.1 %collective-permute-start.19 = (bf16[80,640]{1,0:T(8,128)(2,1)S(1)}, bf16[80,640]{1,0:T(8,128)(2,1)S(1)}, u32[]{:S(2)}, u32[]{:S(2)}) collective-permute-start(bf16[80,640]{1,0:T(8,128)(2,1)S(1)} %add_convert_fusion.4), channel_id=1, source_target_pairs={{0,8},{2,10},{4,12},{6,14},{8,16},{10,18},{12,20},{14,22},{16,24},... | collective-permute-start | bytes 307208 | tf_op jit(solution)/shard_map/ppermute | solution.py:490
  86.5 11.0 %collective-permute-start.16 = (bf16[88,640]{1,0:T(8,128)(2,1)S(1)}, bf16[88,640]{1,0:T(8,128)(2,1)S(1)}, u32[]{:S(2)}, u32[]{:S(2)}) collective-permute-start(bf16[88,640]{1,0:T(8,128)(2,1)S(1)} %add_convert_fusion.1), channel_id=1, source_target_pairs={{0,8},{2,10},{4,12},{6,14},{8,16},{10,18},{12,20},{14,22},{16,24},... | collective-permute-start | bytes 337928 | tf_op jit(solution)/shard_map/ppermute | solution.py:490
  89.7 17.4 %collective-permute-start.21 = (bf16[80,640]{1,0:T(8,128)(2,1)S(1)}, bf16[80,640]{1,0:T(8,128)(2,1)S(1)}, u32[]{:S(2)}, u32[]{:S(2)}) collective-permute-start(bf16[80,640]{1,0:T(8,128)(2,1)S(1)} %add_convert_fusion.3), channel_id=1, source_target_pairs={{0,0},{1,16},{2,8},{3,24},{4,4},{5,20},{6,12},{7,28},{8,1},{9,17},... | collective-permute-start | bytes 307208 | tf_op jit(solution)/shard_map/ppermute | solution.py:609
  97.6 8.8 %collective-permute-start.20 = (bf16[88,640]{1,0:T(8,128)(2,1)S(1)}, bf16[88,640]{1,0:T(8,128)(2,1)S(1)}, u32[]{:S(2)}, u32[]{:S(2)}) collective-permute-start(bf16[88,640]{1,0:T(8,128)(2,1)S(1)} %add_convert_fusion), channel_id=1, source_target_pairs={{0,0},{1,16},{2,8},{3,24},{4,4},{5,20},{6,12},{7,28},{8,1},{9,17},... | collective-permute-start | bytes 337928 | tf_op jit(solution)/shard_map/ppermute | solution.py:609
  (20 other events, 145.5 us)

commit v4 on v3

--- a/solution.py
+++ b/solution.py
@@ -276,12 +276,20 @@
             outs[d][i] = quarter_lanes(rows, quarter_of(geo[1] ^ d)).astype(BF16)
 
 
-def table_kernel(dims, geo, out):
+def table_kernel(dims, geo, *refs):
+    nq, nf, fr, pq = dims
+    factors, (out, early_out, late_out) = refs[:4], refs[4:]
     shape = out.shape
     lane = iota(shape, 1)
     freq = jnp.exp((lane >> 1).astype(F32) * (-2.0 * math.log(10000.0) / shape[1]))
     turn = (lane & 1).astype(F32) * (0.5 * math.pi)
     out[...] = jnp.sin(iota(shape, 0).astype(F32) * freq + turn)
+    tokens = nf * fr
+    for i in range(2):
+        early = [factors[0][i], factors[1][i], factors[2][i, :tokens], factors[3][i, :tokens]]
+        early_out[i] = jnp.concatenate(early, axis=0)
+        late = [factors[2][i, tokens:], factors[3][i, tokens:]]
+        late_out[i] = jnp.concatenate(late, axis=0)
 
 
 def temporal_kernel(dims, *refs):
@@ -344,19 +352,11 @@
     return products, jnp.sum(grad * (normed.astype(F32) - table), axis=0, keepdims=True)
 
 
-def first_weight_kernel(dims, geo, *refs):
-    nq, nf, fr, pq = dims
-    factors, (weights, pos), refs = refs[:4], refs[4:6], refs[6:]
-    terms, (blocks, gain_out, late_out) = refs[: 2 * nq + 2], refs[2 * nq + 2 :]
+def first_weight_kernel(dims, geo, left, weights, pos, *refs):
+    nq, nf, fr, pq = dims
+    terms, (blocks, gain_out) = refs[: 2 * nq + 2], refs[2 * nq + 2 :]
     _, stage, block, _ = blocks.shape
-    tokens = nf * fr
-    left = []
-    for i in range(2):
-        early = [factors[0][i], factors[1][i], factors[2][i, :tokens], factors[3][i, :tokens]]
-        left.append(jnp.concatenate(early, axis=0))
-        late = [factors[2][i, tokens:], factors[3][i, tokens:]]
-        late_out[i] = jnp.concatenate(late, axis=0)
-    products, gain_out[...] = weight_sums(geo, nq, *left, weights, pos, terms)
+    products, gain_out[...] = weight_sums(geo, nq, left[0], left[1], weights, pos, terms)
     for k in range(4):
         for z in range(stage):
             blocks[k, z] = products[k][z * block : (z + 1) * block]
@@ -533,12 +533,15 @@
     factors = [factors[0]] + [move(factors[d], flipped(d)) for d in range(1, 4)]
     parts = [after(parts[0], factors[0])] + [to_quad(p, s + 1) for s, p in enumerate(parts[1:])]
     (terms,) = run(temporal_kernel, "temporal_attention", [sds(tokens, 4 * width)], parts, 2)
-    terms = after(terms, *factors)
-    (table,) = run(
+    table, early_left, late_left = run(
         table_kernel,
-        "positional_table",
-        [sds(tokens, channels, dtype=F32)],
-        [after(geo, terms)],
+        "positional_table_factors",
+        [
+            sds(tokens, channels, dtype=F32),
+            sds(2, (2 * nq + 2) * tokens, half // 4),
+            sds(2, 2 * (nq - 1) * tokens, half // 4),
+        ],
+        [after(geo, terms)] + factors,
         1.5,
     )
     all_terms = [terms] + [after(from_quad(terms, s), table) for s in range(1, nq)]
@@ -555,15 +558,14 @@
     last_terms = [move(pair_terms[0], flipped(1))]
 
     stage, block = nf // 4, half // nf
-    sums, gain_sum, late_left = run(
+    sums, gain_sum = run(
         first_weight_kernel,
         "weight_terms_first_tokens",
         [
             sds(4, stage, block, width, dtype=F32),
             sds(1, half // 4, dtype=F32),
-            sds(2, 2 * (nq - 1) * tokens, half // 4),
         ],
-        [geo] + factors + [quarter, table] + all_terms + core_terms
+        [geo, early_left, quarter, table] + all_terms + core_terms
         + pair_terms[:1] + last_terms,
         0.01,
     )
@@ -596,9 +598,9 @@
         for i in range(2):
             if step == stage - 2:
                 totals[i] = after(totals[i], back_recv)
+            if i == 1:
+                totals[i] = after(totals[i], totals[0])
             moved = move(totals[i], ring)
-            if step == stage - 1:
-                moved = after(moved, grad_hidden)
             totals[i] = add(moved, parts_w[(i + 1) * stage - 1 - step])
     final = []
     for g in range(nf):

time: 108 us -> 127 us (1.18)
  the two profiles are of different devices: /device:TPU:7 before, /device:TPU:5 now
where the time goes in v4:
time: 127 us
  waiting for transfers between devices  44.2 us (35%)
  starting transfers between devices  27.2 us (21%)
  Pallas kernels  23 us (18%)
  blocking collectives  18 us (14%)
  local copies, waits for them, and re-layouts  7.79 us (6%)
  other arithmetic  5.61 us (4%)
    ppermute x15, waiting for transfers between devices, move(): return lax.ppermute(x, 'frame', pairs)  34.1 us
    pallas_call x12, Pallas kernels, call(): pl.pallas_call(kernel, out_shape=outs, in_specs=in_specs, out_specs=[pl.B...  23 us
    all_to_all x1, blocking collectives, swap(): return lax.all_to_all(x, 'frame', split_axis=0, concat_axis=0, tiled=True)  18 us
    ppermute x2, starting transfers between devices, local(): totals = [lax.ppermute(t, ('frame', 'quad'), final) for t in totals]  10.6 us
    ppermute x15, starting transfers between devices, move(): return lax.ppermute(x, 'frame', pairs)  9.19 us
    unnamed x42, local copies, waits for them, and re-layouts  7.78 us
    ppermute x1, waiting for transfers between devices, to_quad(): return lax.ppermute(x, 'quad', [(d, (d + s) % nq) for d in range(nq)])  6.72 us
    convert_element_type x6, other arithmetic, add(): return (a.astype(F32) + b.astype(F32)).astype(BF16)  3.92 us
  transfers between devices with their start and end apart: 23, of which 13 were waited for; matrix products, arithmetic and copies ran while one was open for 3% of the time, Pallas kernels for 16%

profile of v4, /device:TPU:5, one launch (start us, length us, event | category | flops | bytes accessed | tf_op | source)
XLA Modules:
  0.0 126.8 jit_solution(13159281501673604147)
XLA Ops:
  1.1 2.9 %copy-done = bf16[4,1280,640]{2,1,0:T(8,128)(2,1)S(1)} copy-done((bf16[4,1280,640]{2,1,0:T(8,128)(2,1)S(1)}, bf16[4,1280,640]{2,1,0:T(8,128)(2,1)}, u32[]{:S(2)}) %copy-start) | copy-done | bytes 6553624
  7.7 3.4 %spatial_forward.1 = (bf16[128,3200]{1,0:T(8,128)(2,1)S(1)}, bf16[16,8,640]{2,1,0:T(8,128)(2,1)S(1)}) custom-call(s32[3]{0:T(128)S(1)} %pad_add_fusion.refs_0_.geo.quad_ref, bf16[4,16,1280]{2,1,0:T(8,128)(2,1)S(1)} %copy-done.12, bf16[4,16,1280]{2,1,0:T(8,128)(2,1)S(1)} %collective-permute-done.refs_2_, f32[1280]{0:T(1024)S(1)} %copy-done.16, ...), custom_call_target="tpu_custom_call" | custom-call | flops 3000000000 | bytes 1048576 | tf_op jit(solution)/shard_map/spatial_forward/pallas_call | solution.py:430
  12.0 18.0 %all_to_all.10.received = bf16[16,16,640]{2,1,0:T(8,128)(2,1)S(1)} all-to-all(bf16[16,16,640]{2,1,0:T(8,128)(2,1)S(1)} %join_sent.1), channel_id=1, replica_groups=mesh['frame'=16,'quad'=2] {'frame'}, dimensions={0} | all-to-all | bytes 655360 | tf_op jit(solution)/shard_map/all_to_all | solution.py:483
  30.0 1.5 %motion_projection.1 = (f32[64,2560]{1,0:T(8,128)S(1)}, bf16[64,2560]{1,0:T(8,128)(2,1)S(1)}) custom-call(s32[3]{0:T(128)S(1)} %pad_add_fusion.refs_0_.geo.quad_ref, bf16[16,16,640]{2,1,0:T(8,128)(2,1)S(1)} %all_to_all.10.received, bf16[4,640,640]{2,1,0:T(8,128)(2,1)S(1)} %copy-done.2), custom_call_target="tpu_custom_call" | custom-call | flops 1500000000 | bytes 1048576 | tf_op jit(solution)/shard_map/motion_projection/pallas_call | solution.py:430
  32.5 1.3 %cut_factors.1 = (bf16[2,128,160]{2,1,0:T(8,128)(2,1)S(1)}, bf16[2,128,160]{2,1,0:T(8,128)(2,1)S(1)}, bf16[2,128,160]{2,1,0:T(8,128)(2,1)S(1)}, bf16[2,128,160]{2,1,0:T(8,128)(2,1)S(1)}) custom-call(s32[3]{0:T(128)S(1)} %pad_add_fusion.refs_0_.geo.quad_ref, bf16[16,16,640]{2,1,0:T(8,128)(2,1)S(1)} %all_to_all.10.received), custom_call_target="tpu_custom_call" | custom-call | flops 500000000 | bytes 1048576 | tf_op jit(solution)/shard_map/cut_factors/pallas_call | solution.py:430
  33.8 6.7 %collective-permute-done.2.refs_1_ = bf16[64,2560]{1,0:T(8,128)(2,1)S(1)} collective-permute-done((bf16[64,2560]{1,0:T(8,128)(2,1)S(1)}, bf16[64,2560]{1,0:T(8,128)(2,1)S(1)}, u32[]{:S(2)}, u32[]{:S(2)}) %collective-permute-start.2) | collective-permute-done | bytes 327712 | tf_op jit(solution)/shard_map/ppermute | solution.py:480
  46.6 6.4 %collective-permute-done.5.refs_2_ = bf16[2,128,160]{2,1,0:T(8,128)(2,1)S(1)} collective-permute-done((bf16[2,128,160]{2,1,0:T(8,128)(2,1)S(1)}, bf16[2,128,160]{2,1,0:T(8,128)(2,1)S(1)}, u32[]{:S(2)}, u32[]{:S(2)}) %collective-permute-start.5) | collective-permute-done | bytes 81952 | tf_op jit(solution)/shard_map/ppermute | solution.py:490
  53.0 4.6 %collective-permute-done.6.refs_3_ = bf16[2,128,160]{2,1,0:T(8,128)(2,1)S(1)} collective-permute-done((bf16[2,128,160]{2,1,0:T(8,128)(2,1)S(1)}, bf16[2,128,160]{2,1,0:T(8,128)(2,1)S(1)}, u32[]{:S(2)}, u32[]{:S(2)}) %collective-permute-start.6) | collective-permute-done | bytes 81952 | tf_op jit(solution)/shard_map/ppermute | solution.py:490
  57.6 1.7 %positional_table_factors.1 = (f32[64,1280]{1,0:T(8,128)S(1)}, bf16[2,384,160]{2,1,0:T(8,128)(2,1)S(1)}, bf16[2,128,160]{2,1,0:T(8,128)(2,1)S(1)}) custom-call(s32[3]{0:T(128)S(1)} %pad_add_fusion.refs_0_.geo.quad_ref, bf16[2,128,160]{2,1,0:T(8,128)(2,1)S(1)} %get-tuple-element.46.refs_0_, bf16[2,128,160]{2,1,0:T(8,128)(2,1)S(1)} %collective-permute-done.4.refs_1_, ...), custom_call_target="tpu_custom_call" | custom-call | flops 1500000000 | bytes 1048576 | tf_op jit(solution)/shard_map/positional_table_factors/pallas_call | solution.py:430
  59.3 2.5 %temporal_back_projection.1 = (bf16[16,16,640]{2,1,0:T(8,128)(2,1)}, bf16[3,160,640]{2,1,0:T(8,128)(2,1)S(1)}) custom-call(s32[3]{0:T(128)S(1)} %pad_add_fusion.refs_0_.geo.quad_ref, bf16[64,2560]{1,0:T(8,128)(2,1)S(1)} %temporal_attention.1.refs_0_, bf16[64,2560]{1,0:T(8,128)(2,1)S(1)} %collective-permute-done.3.refs_1_, bf16[4,640,640]{2,1,0:T(8,128)(2,1)S(1)} %copy-done.2), custom_call_target="tpu_custom_call" | custom-call | flops 10000000 | bytes 4096 | tf_op jit(solution)/shard_map/temporal_back_projection/pallas_call | solution.py:430
  63.9 1.7 %weight_terms_first_tokens.1 = (f32[4,4,40,640]{3,2,1,0:T(8,128)S(1)}, f32[1,160]{1,0:T(1,128)S(1)}) custom-call(s32[3]{0:T(128)S(1)} %pad_add_fusion.refs_0_.geo.quad_ref, bf16[2,384,160]{2,1,0:T(8,128)(2,1)S(1)} %get-tuple-element.59.left, bf16[3,160,640]{2,1,0:T(8,128)(2,1)S(1)} %get-tuple-element.60.weights, f32[64,1280]{1,0:T(8,128)S(1)} %get-tuple-element.53.pos, ...), custom_call_target="tpu_custom_call" | custom-call | flops 10000000 | bytes 4096 | tf_op jit(solution)/shard_map/weight_terms_first_tokens/pallas_call | solution.py:430
  65.6 6.0 %collective-permute-done.12.refs_0_ = bf16[64,2560]{1,0:T(8,128)(2,1)S(1)} collective-permute-done((bf16[64,2560]{1,0:T(8,128)(2,1)S(1)}, bf16[64,2560]{1,0:T(8,128)(2,1)S(1)}, u32[]{:S(2)}, u32[]{:S(2)}) %collective-permute-start.12) | collective-permute-done | bytes 327712 | tf_op jit(solution)/shard_map/ppermute | solution.py:490
  72.4 3.6 %all-to-all-start.1 = ((bf16[16,16,640]{2,1,0:T(8,128)(2,1)}), bf16[16,16,640]{2,1,0:T(8,128)(2,1)S(1)}, u32[]{:S(2)}, u32[]{:S(2)}) async-start(bf16[16,16,640]{2,1,0:T(8,128)(2,1)} %get-tuple-element.55), calls=%async_computation.1 | async-start | bytes 655360 | tf_op jit(solution)/shard_map/all_to_all | solution.py:483
  76.0 2.6 %weight_terms_last_tokens.1 = (bf16[88,640]{1,0:T(8,128)(2,1)S(1)}, bf16[88,640]{1,0:T(8,128)(2,1)S(1)}, bf16[88,640]{1,0:T(8,128)(2,1)S(1)}, bf16[88,640]{1,0:T...) custom-call(s32[3]{0:T(128)S(1)} %pad_add_fusion.refs_0_.geo.quad_re, ...), custom_call_target="tpu_custom_call" | custom-call | flops 10000000 | bytes 4096 | tf_op jit(solution)/shard_map/weight_terms_last_tokens/pallas_call | solution.py:430
  79.9 1.4 %collective-permute-start.14 = (bf16[88,640]{1,0:T(8,128)(2,1)S(1)}, bf16[88,640]{1,0:T(8,128)(2,1)S(1)}, u32[]{:S(2)}, u32[]{:S(2)}) collective-permute-start(bf16[88,640]{1,0:T(8,128)(2,1)S(1)} %get-tuple-element.66), channel_id=1, source_target_pairs={{0,8},{2,10},{4,12},{6,14},{8,16},{10,18},{12,20},{14,22},{16,24},... | collective-permute-start | bytes 337928 | tf_op jit(solution)/shard_map/ppermute | solution.py:490
  81.3 6.7 %collective-permute-done.14 = bf16[88,640]{1,0:T(8,128)(2,1)S(1)} collective-permute-done((bf16[88,640]{1,0:T(8,128)(2,1)S(1)}, bf16[88,640]{1,0:T(8,128)(2,1)S(1)}, u32[]{:S(2)}, u32[]{:S(2)}) %collective-permute-start.14) | collective-permute-done | bytes 112672 | tf_op jit(solution)/shard_map/ppermute | solution.py:490
  89.9 3.7 %collective-permute-done.17 = bf16[80,640]{1,0:T(8,128)(2,1)S(1)} collective-permute-done((bf16[80,640]{1,0:T(8,128)(2,1)}, bf16[80,640]{1,0:T(8,128)(2,1)S(1)}, u32[]{:S(2)}, u32[]{:S(2)}) %collective-permute-start.17) | collective-permute-done | bytes 102432 | tf_op jit(solution)/shard_map/ppermute | solution.py:490
  94.5 1.5 %collective-permute-done.15 = bf16[88,640]{1,0:T(8,128)(2,1)S(1)} collective-permute-done((bf16[88,640]{1,0:T(8,128)(2,1)S(1)}, bf16[88,640]{1,0:T(8,128)(2,1)S(1)}, u32[]{:S(2)}, u32[]{:S(2)}) %collective-permute-start.15) | collective-permute-done | bytes 112672 | tf_op jit(solution)/shard_map/ppermute | solution.py:490
  97.8 4.6 %collective-permute-done.18 = bf16[80,640]{1,0:T(8,128)(2,1)S(1)} collective-permute-done((bf16[80,640]{1,0:T(8,128)(2,1)S(1)}, bf16[80,640]{1,0:T(8,128)(2,1)S(1)}, u32[]{:S(2)}, u32[]{:S(2)}) %collective-permute-start.18) | collective-permute-done | bytes 102432 | tf_op jit(solution)/shard_map/ppermute | solution.py:490
  106.9 1.7 %block_output_hidden_gradient.1 = (bf16[4,16,1280]{2,1,0:T(8,128)(2,1)}, bf16[128,1280]{1,0:T(8,128)(2,1)S(1)}) custom-call(s32[3]{0:T(128)S(1)} %pad_add_fusion.refs_0_.geo.quad_ref, bf16[16,16,640]{2,1,0:T(8,128)(2,1)S(1)} %all-to-all-done.1.refs_1_, bf16[16,16,640]{2,1,0:T(8,128)(2,1)S(1)} %collective-permute-done.7.refs_2_, ...), custom_call_target="tpu_custom_call" | custom-call | flops 6000000000 | bytes 1048576 | tf_op jit(solution)/shard_map/block_output_hidden_gradient/pallas_call | solution.py:430
  108.6 8.7 %collective-permute-start.20 = (bf16[88,640]{1,0:T(8,128)(2,1)S(1)}, bf16[88,640]{1,0:T(8,128)(2,1)S(1)}, u32[]{:S(2)}, u32[]{:S(2)}) collective-permute-start(bf16[88,640]{1,0:T(8,128)(2,1)S(1)} %add_convert_fusion), channel_id=1, source_target_pairs={{0,0},{1,16},{2,8},{3,24},{4,4},{5,20},{6,12},{7,28},{8,1},{9,17},... | collective-permute-start | bytes 337928 | tf_op jit(solution)/shard_map/ppermute | solution.py:611
  117.3 1.9 %collective-permute-start.21 = (bf16[80,640]{1,0:T(8,128)(2,1)S(1)}, bf16[80,640]{1,0:T(8,128)(2,1)S(1)}, u32[]{:S(2)}, u32[]{:S(2)}) collective-permute-start(bf16[80,640]{1,0:T(8,128)(2,1)S(1)} %add_convert_fusion.3), channel_id=1, source_target_pairs={{0,0},{1,16},{2,8},{3,24},{4,4},{5,20},{6,12},{7,28},{8,1},{9,17},... | collective-permute-start | bytes 307208 | tf_op jit(solution)/shard_map/ppermute | solution.py:611
  119.3 4.1 %spatial_backward.1 = bf16[4,16,1280]{2,1,0:T(8,128)(2,1)} custom-call(bf16[128,1280]{1,0:T(8,128)(2,1)S(1)} %get-tuple-element.79.grad_hidden, bf16[4,16,1280]{2,1,0:T(8,128)(2,1)S(1)} %copy-done.13, bf16[128,3200]{1,0:T(8,128)(2,1)S(1)} %copy-done.18, f32[1280]{0:T(1024)S(1)} %copy-done.16, bf16[4,1280,640]{2,1,0:T(8,128)(2,1)S(1)} %bitcast.7), custom_call_target="tpu_custom_call" | custom-call | flops 3500000000 | bytes 1048576 | tf_op jit(solution)/shard_map/spatial_backward/pallas_call | solution.py:430
  124.0 2.0 %collective-permute-done.21 = bf16[80,640]{1,0:T(8,128)(2,1)S(1)} collective-permute-done((bf16[80,640]{1,0:T(8,128)(2,1)S(1)}, bf16[80,640]{1,0:T(8,128)(2,1)S(1)}, u32[]{:S(2)}, u32[]{:S(2)}) %collective-permute-start.21) | collective-permute-done | bytes 102432 | tf_op jit(solution)/shard_map/ppermute | solution.py:611
  (92 shorter events, 26.7 us)
Async XLA Ops:
  0.6 5.3 %collective-permute-start = (bf16[4,16,1280]{2,1,0:T(8,128)(2,1)}, bf16[4,16,1280]{2,1,0:T(8,128)(2,1)S(1)}, u32[]{:S(2)}, u32[]{:S(2)}) collective-permute-start(bf16[4,16,1280]{2,1,0:T(8,128)(2,1)} %xs.1), channel_id=1, source_target_pairs={{1,0},{0,1},{3,2},{2,3},{5,4},{4,5},{7,6},{6,7},{9,8},{8,9},{11,10... | collective-permute-start | bytes 491528 | tf_op jit(solution)/shard_map/ppermute | solution.py:477
  6.0 5.2 %collective-permute-start.1 = (bf16[4,16,1280]{2,1,0:T(8,128)(2,1)S(1)}, bf16[4,16,1280]{2,1,0:T(8,128)(2,1)S(1)}, u32[]{:S(2)}, u32[]{:S(2)}) collective-permute-start(bf16[4,16,1280]{2,1,0:T(8,128)(2,1)S(1)} %copy-done.3), channel_id=1, source_target_pairs={{1,0},{0,1},{3,2},{2,3},{5,4},{4,5},{7,6},{6,7},{9,8},{8,9},{11,10... | collective-permute-start | bytes 491528 | tf_op jit(solution)/shard_map/ppermute | solution.py:477
  31.5 9.0 %collective-permute-start.2 = (bf16[64,2560]{1,0:T(8,128)(2,1)S(1)}, bf16[64,2560]{1,0:T(8,128)(2,1)S(1)}, u32[]{:S(2)}, u32[]{:S(2)}) collective-permute-start(bf16[64,2560]{1,0:T(8,128)(2,1)S(1)} %get-tuple-element.48), channel_id=1, source_target_pairs={{0,1},{1,0},{2,3},{3,2},{4,5},{5,4},{6,7},{7,6},{8,9},{9,8},{10,11... | collective-permute-start | bytes 983048 | tf_op jit(solution)/shard_map/ppermute | solution.py:480
  41.6 17.7 %collective-permute-start.3 = (bf16[64,2560]{1,0:T(8,128)(2,1)S(1)}, bf16[64,2560]{1,0:T(8,128)(2,1)S(1)}, u32[]{:S(2)}, u32[]{:S(2)}) collective-permute-start(bf16[64,2560]{1,0:T(8,128)(2,1)S(1)} %temporal_attention.1.refs_0_), channel_id=1, source_target_pairs={{1,0},{0,1},{3,2},{2,3},{5,4},{4,5},{7,6},{6,7},{9,8},{8,9},{11,10... | collective-permute-start | bytes 983048 | tf_op jit(solution)/shard_map/ppermute | solution.py:477
  42.5 19.2 %collective-permute-start.10 = (bf16[64,2560]{1,0:T(8,128)(2,1)S(1)}, bf16[64,2560]{1,0:T(8,128)(2,1)S(1)}, u32[]{:S(2)}, u32[]{:S(2)}) collective-permute-start(bf16[64,2560]{1,0:T(8,128)(2,1)S(1)} %temporal_attention.1.refs_0_), channel_id=1, source_target_pairs={{0,4},{2,6},{4,0},{6,2},{8,12},{10,14},{12,8},{14,10},{16,20},{18,... | collective-permute-start | bytes 983048 | tf_op jit(solution)/shard_map/ppermute | solution.py:490
  43.7 2.7 %collective-permute-start.4 = (bf16[2,128,160]{2,1,0:T(8,128)(2,1)S(1)}, bf16[2,128,160]{2,1,0:T(8,128)(2,1)S(1)}, u32[]{:S(2)}, u32[]{:S(2)}) collective-permute-start(bf16[2,128,160]{2,1,0:T(8,128)(2,1)S(1)} %get-tuple-element.50), channel_id=1, source_target_pairs={{0,2},{2,0},{4,6},{6,4},{8,10},{10,8},{12,14},{14,12},{16,18},{18,... | collective-permute-start | bytes 245768 | tf_op jit(solution)/shard_map/ppermute | solution.py:490
  44.8 8.3 %collective-permute-start.5 = (bf16[2,128,160]{2,1,0:T(8,128)(2,1)S(1)}, bf16[2,128,160]{2,1,0:T(8,128)(2,1)S(1)}, u32[]{:S(2)}, u32[]{:S(2)}) collective-permute-start(bf16[2,128,160]{2,1,0:T(8,128)(2,1)S(1)} %get-tuple-element.51), channel_id=1, source_target_pairs={{0,4},{2,6},{4,0},{6,2},{8,12},{10,14},{12,8},{14,10},{16,20},{18,... | collective-permute-start | bytes 245768 | tf_op jit(solution)/shard_map/ppermute | solution.py:490
  45.8 11.8 %collective-permute-start.6 = (bf16[2,128,160]{2,1,0:T(8,128)(2,1)S(1)}, bf16[2,128,160]{2,1,0:T(8,128)(2,1)S(1)}, u32[]{:S(2)}, u32[]{:S(2)}) collective-permute-start(bf16[2,128,160]{2,1,0:T(8,128)(2,1)S(1)} %get-tuple-element.52), channel_id=1, source_target_pairs={{0,6},{2,4},{4,2},{6,0},{8,14},{10,12},{12,10},{14,8},{16,22},{18,... | collective-permute-start | bytes 245768 | tf_op jit(solution)/shard_map/ppermute | solution.py:490
  46.4 17.1 %collective-permute-start.8 = (bf16[64,2560]{1,0:T(8,128)(2,1)S(1)}, bf16[64,2560]{1,0:T(8,128)(2,1)S(1)}, u32[]{:S(2)}, u32[]{:S(2)}) collective-permute-start(bf16[64,2560]{1,0:T(8,128)(2,1)S(1)} %temporal_attention.1.refs_0_), channel_id=1, source_target_pairs={{0,2},{2,0},{4,6},{6,4},{8,10},{10,8},{12,14},{14,12},{16,18},{18,... | collective-permute-start | bytes 983048 | tf_op jit(solution)/shard_map/ppermute | solution.py:490
  61.8 1.7 %collective-permute-start.11 = (bf16[64,2560]{1,0:T(8,128)(2,1)S(1)}, bf16[64,2560]{1,0:T(8,128)(2,1)S(1)}, u32[]{:S(2)}, u32[]{:S(2)}) collective-permute-start(bf16[64,2560]{1,0:T(8,128)(2,1)S(1)} %collective-permute-done.10.refs_4_), channel_id=1, source_target_pairs={{0,2},{2,0},{4,6},{6,4},{8,10},{10,8},{12,14},{14,12},{16,18},{18,... | collective-permute-start | bytes 983048 | tf_op jit(solution)/shard_map/ppermute | solution.py:490
  61.8 2.1 %collective-permute-start.9 = (bf16[64,2560]{1,0:T(8,128)(2,1)S(1)}, bf16[64,2560]{1,0:T(8,128)(2,1)S(1)}, u32[]{:S(2)}, u32[]{:S(2)}) collective-permute-start(bf16[64,2560]{1,0:T(8,128)(2,1)S(1)} %collective-permute-done.3.refs_1_), channel_id=1, source_target_pairs={{0,2},{2,0},{4,6},{6,4},{8,10},{10,8},{12,14},{14,12},{16,18},{18,... | collective-permute-start | bytes 983048 | tf_op jit(solution)/shard_map/ppermute | solution.py:490
  62.3 9.3 %collective-permute-start.12 = (bf16[64,2560]{1,0:T(8,128)(2,1)S(1)}, bf16[64,2560]{1,0:T(8,128)(2,1)S(1)}, u32[]{:S(2)}, u32[]{:S(2)}) collective-permute-start(bf16[64,2560]{1,0:T(8,128)(2,1)S(1)} %collective-permute-done.3.refs_1_), channel_id=1, source_target_pairs={{0,4},{2,6},{4,0},{6,2},{8,12},{10,14},{12,8},{14,10},{16,20},{18,... | collective-permute-start | bytes 983048 | tf_op jit(solution)/shard_map/ppermute | solution.py:490
  65.6 39.2 %copy-start.4 = (bf16[4,16,1280]{2,1,0:T(8,128)(2,1)S(1)}, bf16[4,16,1280]{2,1,0:T(8,128)(2,1)}, u32[]{:S(2)}) copy-start(bf16[4,16,1280]{2,1,0:T(8,128)(2,1)} %refs_3_.3) | copy-start | bytes 491524
  71.6 4.4 %collective-permute-start.13 = (bf16[64,2560]{1,0:T(8,128)(2,1)S(1)}, bf16[64,2560]{1,0:T(8,128)(2,1)}, u32[]{:S(2)}, u32[]{:S(2)}) collective-permute-start(bf16[64,2560]{1,0:T(8,128)(2,1)S(1)} %collective-permute-done.12.refs_0_), channel_id=1, source_target_pairs={{0,2},{2,0},{4,6},{6,4},{8,10},{10,8},{12,14},{14,12},{16,18},{18,... | collective-permute-start | bytes 983048 | tf_op jit(solution)/shard_map/ppermute | solution.py:490
  72.4 16.5 %all-to-all-start.1 = ((bf16[16,16,640]{2,1,0:T(8,128)(2,1)}), bf16[16,16,640]{2,1,0:T(8,128)(2,1)S(1)}, u32[]{:S(2)}, u32[]{:S(2)}) async-start(bf16[16,16,640]{2,1,0:T(8,128)(2,1)} %get-tuple-element.55), calls=%async_computation.1 | async-start | bytes 655360 | tf_op jit(solution)/shard_map/all_to_all | solution.py:483
  79.9 8.0 %collective-permute-start.14 = (bf16[88,640]{1,0:T(8,128)(2,1)S(1)}, bf16[88,640]{1,0:T(8,128)(2,1)S(1)}, u32[]{:S(2)}, u32[]{:S(2)}) collective-permute-start(bf16[88,640]{1,0:T(8,128)(2,1)S(1)} %get-tuple-element.66), channel_id=1, source_target_pairs={{0,8},{2,10},{4,12},{6,14},{8,16},{10,18},{12,20},{14,22},{16,24},... | collective-permute-start | bytes 337928 | tf_op jit(solution)/shard_map/ppermute | solution.py:490
  88.0 5.6 %collective-permute-start.17 = (bf16[80,640]{1,0:T(8,128)(2,1)}, bf16[80,640]{1,0:T(8,128)(2,1)S(1)}, u32[]{:S(2)}, u32[]{:S(2)}) collective-permute-start(bf16[80,640]{1,0:T(8,128)(2,1)} %get-tuple-element.72), channel_id=1, source_target_pairs={{0,8},{2,10},{4,12},{6,14},{8,16},{10,18},{12,20},{14,22},{16,24},... | collective-permute-start | bytes 307208 | tf_op jit(solution)/shard_map/ppermute | solution.py:490
  89.0 7.0 %collective-permute-start.15 = (bf16[88,640]{1,0:T(8,128)(2,1)S(1)}, bf16[88,640]{1,0:T(8,128)(2,1)S(1)}, u32[]{:S(2)}, u32[]{:S(2)}) collective-permute-start(bf16[88,640]{1,0:T(8,128)(2,1)S(1)} %add_convert_fusion.2), channel_id=1, source_target_pairs={{0,8},{2,10},{4,12},{6,14},{8,16},{10,18},{12,20},{14,22},{16,24},... | collective-permute-start | bytes 337928 | tf_op jit(solution)/shard_map/ppermute | solution.py:490
  97.1 5.4 %collective-permute-start.18 = (bf16[80,640]{1,0:T(8,128)(2,1)S(1)}, bf16[80,640]{1,0:T(8,128)(2,1)S(1)}, u32[]{:S(2)}, u32[]{:S(2)}) collective-permute-start(bf16[80,640]{1,0:T(8,128)(2,1)S(1)} %add_convert_fusion.5), channel_id=1, source_target_pairs={{0,8},{2,10},{4,12},{6,14},{8,16},{10,18},{12,20},{14,22},{16,24},... | collective-permute-start | bytes 307208 | tf_op jit(solution)/shard_map/ppermute | solution.py:490
  97.2 7.7 %collective-permute-start.7 = (bf16[16,16,640]{2,1,0:T(8,128)(2,1)S(1)}, bf16[16,16,640]{2,1,0:T(8,128)(2,1)S(1)}, u32[]{:S(2)}, u32[]{:S(2)}) collective-permute-start(bf16[16,16,640]{2,1,0:T(8,128)(2,1)S(1)} %all-to-all-done.1.refs_1_), channel_id=1, source_target_pairs={{1,0},{0,1},{3,2},{2,3},{5,4},{4,5},{7,6},{6,7},{9,8},{8,9},{11,10... | collective-permute-start | bytes 983048 | tf_op jit(solution)/shard_map/ppermute | solution.py:477
  97.8 5.8 %collective-permute-start.16 = (bf16[88,640]{1,0:T(8,128)(2,1)S(1)}, bf16[88,640]{1,0:T(8,128)(2,1)S(1)}, u32[]{:S(2)}, u32[]{:S(2)}) collective-permute-start(bf16[88,640]{1,0:T(8,128)(2,1)S(1)} %add_convert_fusion.1), channel_id=1, source_target_pairs={{0,8},{2,10},{4,12},{6,14},{8,16},{10,18},{12,20},{14,22},{16,24},... | collective-permute-start | bytes 337928 | tf_op jit(solution)/shard_map/ppermute | solution.py:490
  104.6 12.7 %collective-permute-start.19 = (bf16[80,640]{1,0:T(8,128)(2,1)S(1)}, bf16[80,640]{1,0:T(8,128)(2,1)S(1)}, u32[]{:S(2)}, u32[]{:S(2)}) collective-permute-start(bf16[80,640]{1,0:T(8,128)(2,1)S(1)} %add_convert_fusion.4), channel_id=1, source_target_pairs={{0,8},{2,10},{4,12},{6,14},{8,16},{10,18},{12,20},{14,22},{16,24},... | collective-permute-start | bytes 307208 | tf_op jit(solution)/shard_map/ppermute | solution.py:490
  108.6 14.8 %collective-permute-start.20 = (bf16[88,640]{1,0:T(8,128)(2,1)S(1)}, bf16[88,640]{1,0:T(8,128)(2,1)S(1)}, u32[]{:S(2)}, u32[]{:S(2)}) collective-permute-start(bf16[88,640]{1,0:T(8,128)(2,1)S(1)} %add_convert_fusion), channel_id=1, source_target_pairs={{0,0},{1,16},{2,8},{3,24},{4,4},{5,20},{6,12},{7,28},{8,1},{9,17},... | collective-permute-start | bytes 337928 | tf_op jit(solution)/shard_map/ppermute | solution.py:611
  117.3 8.7 %collective-permute-start.21 = (bf16[80,640]{1,0:T(8,128)(2,1)S(1)}, bf16[80,640]{1,0:T(8,128)(2,1)S(1)}, u32[]{:S(2)}, u32[]{:S(2)}) collective-permute-start(bf16[80,640]{1,0:T(8,128)(2,1)S(1)} %add_convert_fusion.3), channel_id=1, source_target_pairs={{0,0},{1,16},{2,8},{3,24},{4,4},{5,20},{6,12},{7,28},{8,1},{9,17},... | collective-permute-start | bytes 307208 | tf_op jit(solution)/shard_map/ppermute | solution.py:611
  (20 other events, 166.3 us)

commit v5 on v4

--- a/solution.py
+++ b/solution.py
@@ -533,6 +533,7 @@
     factors = [factors[0]] + [move(factors[d], flipped(d)) for d in range(1, 4)]
     parts = [after(parts[0], factors[0])] + [to_quad(p, s + 1) for s, p in enumerate(parts[1:])]
     (terms,) = run(temporal_kernel, "temporal_attention", [sds(tokens, 4 * width)], parts, 2)
+    terms = after(terms, *factors)
     table, early_left, late_left = run(
         table_kernel,
         "positional_table_factors",
@@ -585,6 +586,14 @@
 
     back_recv = swap(back_send)
     backs = [back_recv] + [from_quad(back_recv, s) for s in range(1, nq)]
+    totals = [parts_w[stage - 1], parts_w[2 * stage - 1]]
+    for step in range(1, stage):
+        for i in range(2):
+            if step == stage - 2:
+                totals[i] = after(totals[i], back_recv)
+            moved = move(totals[i], ring)
+            totals[i] = add(moved, parts_w[(i + 1) * stage - 1 - step])
+    backs[0] = after(backs[0], *totals)
     block_output, grad_hidden = run(
         middle_kernel,
         "block_output_hidden_gradient",
@@ -593,21 +602,11 @@
         6,
         big,
     )
-    totals = [parts_w[stage - 1], parts_w[2 * stage - 1]]
-    for step in range(1, stage):
-        for i in range(2):
-            if step == stage - 2:
-                totals[i] = after(totals[i], back_recv)
-            if i == 1:
-                totals[i] = after(totals[i], totals[0])
-            moved = move(totals[i], ring)
-            totals[i] = add(moved, parts_w[(i + 1) * stage - 1 - step])
     final = []
     for g in range(nf):
         for q in range(nq):
             j = quarter_of(g % 4) * stage + g // 4
             final.append((g * nq + q, nf * q + j))
-    grad_hidden = after(grad_hidden, *totals)
     totals = [lax.ppermute(t, ("frame", "quad"), final) for t in totals]
     (input_grad,) = run(
         tail_kernel,

time: 127 us -> 109 us (0.86)
  the two profiles are of different devices: /device:TPU:5 before, /device:TPU:1 now
where the time goes in v5:
time: 109 us; the launch traced here: 108 us
  starting transfers between devices  30.8 us (28%)
  waiting for transfers between devices  28 us (26%)
  Pallas kernels  22.4 us (21%)
  blocking collectives  17.5 us (16%)
  local copies, waits for them, and re-layouts  6.7 us (6%)
  other arithmetic  1.87 us (2%)
    pallas_call x12, Pallas kernels, call(): pl.pallas_call(kernel, out_shape=outs, in_specs=in_specs, out_specs=[pl.B...  22.4 us
    ppermute x15, waiting for transfers between devices, move(): return lax.ppermute(x, 'frame', pairs)  18.2 us
    all_to_all x1, blocking collectives, swap(): return lax.all_to_all(x, 'frame', split_axis=0, concat_axis=0, tiled=True)  17.5 us
    ppermute x2, starting transfers between devices, local(): totals = [lax.ppermute(t, ('frame', 'quad'), final) for t in totals]  11.8 us
    ppermute x15, starting transfers between devices, move(): return lax.ppermute(x, 'frame', pairs)  9.83 us
    unnamed x30, local copies, waits for them, and re-layouts  6.69 us
    ppermute x4, waiting for transfers between devices, from_quad(): return lax.ppermute(x, 'quad', [((d + s) % nq, d) for d in range(nq)])  4.62 us
    ppermute x1, waiting for transfers between devices, to_quad(): return lax.ppermute(x, 'quad', [(d, (d + s) % nq) for d in range(nq)])  4.6 us
  transfers between devices with their start and end apart: 23, of which 11 were waited for; matrix products, arithmetic and copies ran while one was open for 1% of the time, Pallas kernels for 19%

profile of v5, /device:TPU:1, one launch (start us, length us, event | category | flops | bytes accessed | tf_op | source)
XLA Modules:
  0.0 108.3 jit_solution(11508455226783069006)
XLA Ops:
  0.6 2.1 %collective-permute-start = (bf16[4,16,1280]{2,1,0:T(8,128)(2,1)}, bf16[4,16,1280]{2,1,0:T(8,128)(2,1)S(1)}, u32[]{:S(2)}, u32[]{:S(2)}) collective-permute-start(bf16[4,16,1280]{2,1,0:T(8,128)(2,1)} %xs.1), channel_id=1, source_target_pairs={{1,0},{0,1},{3,2},{2,3},{5,4},{4,5},{7,6},{6,7},{9,8},{8,9},{11,10... | collective-permute-start | bytes 491528 | tf_op jit(solution)/shard_map/ppermute | solution.py:477
  3.1 2.9 %copy-done = bf16[4,1280,640]{2,1,0:T(8,128)(2,1)S(1)} copy-done((bf16[4,1280,640]{2,1,0:T(8,128)(2,1)S(1)}, bf16[4,1280,640]{2,1,0:T(8,128)(2,1)}, u32[]{:S(2)}) %copy-start) | copy-done | bytes 6553624
  8.0 1.7 %copy-done.1 = bf16[4,1280,640]{2,1,0:T(8,128)(2,1)S(1)} copy-done((bf16[4,1280,640]{2,1,0:T(8,128)(2,1)S(1)}, bf16[4,1280,640]{2,1,0:T(8,128)(2,1)}, u32[]{:S(2)}) %copy-start.1) | copy-done | bytes 6553624
  9.8 3.4 %spatial_forward.1 = (bf16[128,3200]{1,0:T(8,128)(2,1)S(1)}, bf16[16,8,640]{2,1,0:T(8,128)(2,1)S(1)}) custom-call(s32[3]{0:T(128)S(1)} %pad_add_fusion.refs_0_.geo.quad_ref, bf16[4,16,1280]{2,1,0:T(8,128)(2,1)S(1)} %copy-done.6, bf16[4,16,1280]{2,1,0:T(8,128)(2,1)S(1)} %collective-permute-done.refs_2_, f32[1280]{0:T(1024)S(1)} %copy-done.10, ...), custom_call_target="tpu_custom_call" | custom-call | flops 3000000000 | bytes 1048576 | tf_op jit(solution)/shard_map/spatial_forward/pallas_call | solution.py:430
  14.0 17.5 %all_to_all.10.received = bf16[16,16,640]{2,1,0:T(8,128)(2,1)S(1)} all-to-all(bf16[16,16,640]{2,1,0:T(8,128)(2,1)S(1)} %join_sent.1), channel_id=1, replica_groups=mesh['frame'=16,'quad'=2] {'frame'}, dimensions={0} | all-to-all | bytes 655360 | tf_op jit(solution)/shard_map/all_to_all | solution.py:483
  35.7 1.7 %collective-permute-start.5 = (bf16[2,128,160]{2,1,0:T(8,128)(2,1)S(1)}, bf16[2,128,160]{2,1,0:T(8,128)(2,1)S(1)}, u32[]{:S(2)}, u32[]{:S(2)}) collective-permute-start(bf16[2,128,160]{2,1,0:T(8,128)(2,1)S(1)} %get-tuple-element.49), channel_id=1, source_target_pairs={{0,6},{2,4},{4,2},{6,0},{8,14},{10,12},{12,10},{14,8},{16,22},{18,... | collective-permute-start | bytes 245768 | tf_op jit(solution)/shard_map/ppermute | solution.py:490
  37.4 4.6 %collective-permute-done.2.refs_1_ = bf16[64,2560]{1,0:T(8,128)(2,1)S(1)} collective-permute-done((bf16[64,2560]{1,0:T(8,128)(2,1)S(1)}, bf16[64,2560]{1,0:T(8,128)(2,1)S(1)}, u32[]{:S(2)}, u32[]{:S(2)}) %collective-permute-start.2) | collective-permute-done | bytes 327712 | tf_op jit(solution)/shard_map/ppermute | solution.py:480
  46.0 1.7 %positional_table_factors.1 = (f32[64,1280]{1,0:T(8,128)S(1)}, bf16[2,384,160]{2,1,0:T(8,128)(2,1)S(1)}, bf16[2,128,160]{2,1,0:T(8,128)(2,1)S(1)}) custom-call(s32[3]{0:T(128)S(1)} %pad_add_fusion.refs_0_.geo.quad_ref, bf16[2,128,160]{2,1,0:T(8,128)(2,1)S(1)} %get-tuple-element.44.refs_0_, bf16[2,128,160]{2,1,0:T(8,128)(2,1)S(1)} %collective-permute-done.3.refs_1_, ...), custom_call_target="tpu_custom_call" | custom-call | flops 1500000000 | bytes 1048576 | tf_op jit(solution)/shard_map/positional_table_factors/pallas_call | solution.py:430
  47.6 4.6 %collective-permute-done.6.refs_1_ = bf16[64,2560]{1,0:T(8,128)(2,1)S(1)} collective-permute-done((bf16[64,2560]{1,0:T(8,128)(2,1)S(1)}, bf16[64,2560]{1,0:T(8,128)(2,1)S(1)}, u32[]{:S(2)}, u32[]{:S(2)}) %collective-permute-start.6) | collective-permute-done | bytes 327712 | tf_op jit(solution)/shard_map/ppermute | solution.py:477
  52.2 2.5 %temporal_back_projection.1 = (bf16[16,16,640]{2,1,0:T(8,128)(2,1)}, bf16[3,160,640]{2,1,0:T(8,128)(2,1)S(1)}) custom-call(s32[3]{0:T(128)S(1)} %pad_add_fusion.refs_0_.geo.quad_ref, bf16[64,2560]{1,0:T(8,128)(2,1)S(1)} %temporal_attention.1.refs_0_, bf16[64,2560]{1,0:T(8,128)(2,1)S(1)} %collective-permute-done.6.refs_1_, bf16[4,640,640]{2,1,0:T(8,128)(2,1)S(1)} %copy-done.2), custom_call_target="tpu_custom_call" | custom-call | flops 10000000 | bytes 4096 | tf_op jit(solution)/shard_map/temporal_back_projection/pallas_call | solution.py:430
  54.8 1.6 %collective-permute-start.10 = (bf16[64,2560]{1,0:T(8,128)(2,1)S(1)}, bf16[64,2560]{1,0:T(8,128)(2,1)}, u32[]{:S(2)}, u32[]{:S(2)}) collective-permute-start(bf16[64,2560]{1,0:T(8,128)(2,1)S(1)} %collective-permute-done.9.refs_4_), channel_id=1, source_target_pairs={{0,2},{2,0},{4,6},{6,4},{8,10},{10,8},{12,14},{14,12},{16,18},{18,... | collective-permute-start | bytes 983048 | tf_op jit(solution)/shard_map/ppermute | solution.py:490
  57.0 4.1 %all-to-all-start.1 = ((bf16[16,16,640]{2,1,0:T(8,128)(2,1)}), bf16[16,16,640]{2,1,0:T(8,128)(2,1)S(1)}, u32[]{:S(2)}, u32[]{:S(2)}) async-start(bf16[16,16,640]{2,1,0:T(8,128)(2,1)} %get-tuple-element.54), calls=%async_computation.1 | async-start | bytes 655360 | tf_op jit(solution)/shard_map/all_to_all | solution.py:483
  61.1 2.2 %weight_terms_first_tokens.1 = (f32[4,4,40,640]{3,2,1,0:T(8,128)S(1)}, f32[1,160]{1,0:T(1,128)S(1)}) custom-call(s32[3]{0:T(128)S(1)} %pad_add_fusion.refs_0_.geo.quad_ref, bf16[2,384,160]{2,1,0:T(8,128)(2,1)S(1)} %get-tuple-element.55.left, bf16[3,160,640]{2,1,0:T(8,128)(2,1)S(1)} %get-tuple-element.56.weights, f32[64,1280]{1,0:T(8,128)S(1)} %get-tuple-element.52.pos, ...), custom_call_target="tpu_custom_call" | custom-call | flops 10000000 | bytes 4096 | tf_op jit(solution)/shard_map/weight_terms_first_tokens/pallas_call | solution.py:430
  63.4 2.1 %collective-permute-done.11.refs_0_ = bf16[64,2560]{1,0:T(8,128)(2,1)S(1)} collective-permute-done((bf16[64,2560]{1,0:T(8,128)(2,1)S(1)}, bf16[64,2560]{1,0:T(8,128)(2,1)S(1)}, u32[]{:S(2)}, u32[]{:S(2)}) %collective-permute-start.11) | collective-permute-done | bytes 327712 | tf_op jit(solution)/shard_map/ppermute | solution.py:490
  65.5 2.7 %collective-permute-start.12 = (bf16[64,2560]{1,0:T(8,128)(2,1)S(1)}, bf16[64,2560]{1,0:T(8,128)(2,1)S(1)}, u32[]{:S(2)}, u32[]{:S(2)}) collective-permute-start(bf16[64,2560]{1,0:T(8,128)(2,1)S(1)} %collective-permute-done.11.refs_0_), channel_id=1, source_target_pairs={{0,2},{2,0},{4,6},{6,4},{8,10},{10,8},{12,14},{14,12},{16,18},{18,... | collective-permute-start | bytes 983048 | tf_op jit(solution)/shard_map/ppermute | solution.py:490
  73.3 3.6 %collective-permute-done.16 = bf16[80,640]{1,0:T(8,128)(2,1)S(1)} collective-permute-done((bf16[80,640]{1,0:T(8,128)(2,1)S(1)}, bf16[80,640]{1,0:T(8,128)(2,1)S(1)}, u32[]{:S(2)}, u32[]{:S(2)}) %collective-permute-start.16) | collective-permute-done | bytes 102432 | tf_op jit(solution)/shard_map/ppermute | solution.py:490
  77.0 2.5 %collective-permute-done.13 = bf16[88,640]{1,0:T(8,128)(2,1)S(1)} collective-permute-done((bf16[88,640]{1,0:T(8,128)(2,1)S(1)}, bf16[88,640]{1,0:T(8,128)(2,1)S(1)}, u32[]{:S(2)}, u32[]{:S(2)}) %collective-permute-start.13) | collective-permute-done | bytes 112672 | tf_op jit(solution)/shard_map/ppermute | solution.py:490
  79.6 2.7 %collective-permute-done.17 = bf16[80,640]{1,0:T(8,128)(2,1)S(1)} collective-permute-done((bf16[80,640]{1,0:T(8,128)(2,1)S(1)}, bf16[80,640]{1,0:T(8,128)(2,1)S(1)}, u32[]{:S(2)}, u32[]{:S(2)}) %collective-permute-start.17) | collective-permute-done | bytes 102432 | tf_op jit(solution)/shard_map/ppermute | solution.py:490
  82.4 3.9 %collective-permute-done.14 = bf16[88,640]{1,0:T(8,128)(2,1)S(1)} collective-permute-done((bf16[88,640]{1,0:T(8,128)(2,1)S(1)}, bf16[88,640]{1,0:T(8,128)(2,1)S(1)}, u32[]{:S(2)}, u32[]{:S(2)}) %collective-permute-start.14) | collective-permute-done | bytes 112672 | tf_op jit(solution)/shard_map/ppermute | solution.py:490
  86.4 1.6 %collective-permute-done.18 = bf16[80,640]{1,0:T(8,128)(2,1)S(1)} collective-permute-done((bf16[80,640]{1,0:T(8,128)(2,1)S(1)}, bf16[80,640]{1,0:T(8,128)(2,1)S(1)}, u32[]{:S(2)}, u32[]{:S(2)}) %collective-permute-start.18) | collective-permute-done | bytes 102432 | tf_op jit(solution)/shard_map/ppermute | solution.py:490
  88.0 5.2 %collective-permute-start.21 = (bf16[80,640]{1,0:T(8,128)(2,1)S(1)}, bf16[80,640]{1,0:T(8,128)(2,1)S(1)}, u32[]{:S(2)}, u32[]{:S(2)}) collective-permute-start(bf16[80,640]{1,0:T(8,128)(2,1)S(1)} %add_convert_fusion.3), channel_id=1, source_target_pairs={{0,0},{1,16},{2,8},{3,24},{4,4},{5,20},{6,12},{7,28},{8,1},{9,17},... | collective-permute-start | bytes 307208 | tf_op jit(solution)/shard_map/ppermute | solution.py:610
  93.3 6.6 %collective-permute-start.20 = (bf16[88,640]{1,0:T(8,128)(2,1)S(1)}, bf16[88,640]{1,0:T(8,128)(2,1)S(1)}, u32[]{:S(2)}, u32[]{:S(2)}) collective-permute-start(bf16[88,640]{1,0:T(8,128)(2,1)S(1)} %add_convert_fusion), channel_id=1, source_target_pairs={{0,0},{1,16},{2,8},{3,24},{4,4},{5,20},{6,12},{7,28},{8,1},{9,17},... | collective-permute-start | bytes 337928 | tf_op jit(solution)/shard_map/ppermute | solution.py:610
  101.1 1.7 %block_output_hidden_gradient.1 = (bf16[4,16,1280]{2,1,0:T(8,128)(2,1)}, bf16[128,1280]{1,0:T(8,128)(2,1)S(1)}) custom-call(s32[3]{0:T(128)S(1)} %pad_add_fusion.refs_0_.geo.quad_ref, bf16[16,16,640]{2,1,0:T(8,128)(2,1)S(1)} %all-to-all-done.1.refs_1_, bf16[16,16,640]{2,1,0:T(8,128)(2,1)S(1)} %collective-permute-done.19.refs_2_, ...), custom_call_target="tpu_custom_call" | custom-call | flops 6000000000 | bytes 1048576 | tf_op jit(solution)/shard_map/block_output_hidden_gradient/pallas_call | solution.py:430
  102.8 4.1 %spatial_backward.1 = bf16[4,16,1280]{2,1,0:T(8,128)(2,1)} custom-call(bf16[128,1280]{1,0:T(8,128)(2,1)S(1)} %get-tuple-element.75.grad_hidden, bf16[4,16,1280]{2,1,0:T(8,128)(2,1)S(1)} %copy-done.7, bf16[128,3200]{1,0:T(8,128)(2,1)S(1)} %copy-done.12, f32[1280]{0:T(1024)S(1)} %copy-done.10, bf16[4,1280,640]{2,1,0:T(8,128)(2,1)S(1)} %bitcast.7), custom_call_target="tpu_custom_call" | custom-call | flops 3500000000 | bytes 1048576 | tf_op jit(solution)/shard_map/spatial_backward/pallas_call | solution.py:430
  (80 shorter events, 20.1 us)
Async XLA Ops:
  0.6 7.0 %collective-permute-start = (bf16[4,16,1280]{2,1,0:T(8,128)(2,1)}, bf16[4,16,1280]{2,1,0:T(8,128)(2,1)S(1)}, u32[]{:S(2)}, u32[]{:S(2)}) collective-permute-start(bf16[4,16,1280]{2,1,0:T(8,128)(2,1)} %xs.1), channel_id=1, source_target_pairs={{1,0},{0,1},{3,2},{2,3},{5,4},{4,5},{7,6},{6,7},{9,8},{8,9},{11,10... | collective-permute-start | bytes 491528 | tf_op jit(solution)/shard_map/ppermute | solution.py:477
  7.6 5.6 %collective-permute-start.1 = (bf16[4,16,1280]{2,1,0:T(8,128)(2,1)S(1)}, bf16[4,16,1280]{2,1,0:T(8,128)(2,1)S(1)}, u32[]{:S(2)}, u32[]{:S(2)}) collective-permute-start(bf16[4,16,1280]{2,1,0:T(8,128)(2,1)S(1)} %copy-done.3), channel_id=1, source_target_pairs={{1,0},{0,1},{3,2},{2,3},{5,4},{4,5},{7,6},{6,7},{9,8},{8,9},{11,10... | collective-permute-start | bytes 491528 | tf_op jit(solution)/shard_map/ppermute | solution.py:477
  33.0 9.0 %collective-permute-start.2 = (bf16[64,2560]{1,0:T(8,128)(2,1)S(1)}, bf16[64,2560]{1,0:T(8,128)(2,1)S(1)}, u32[]{:S(2)}, u32[]{:S(2)}) collective-permute-start(bf16[64,2560]{1,0:T(8,128)(2,1)S(1)} %get-tuple-element.46), channel_id=1, source_target_pairs={{0,1},{1,0},{2,3},{3,2},{4,5},{5,4},{6,7},{7,6},{8,9},{9,8},{10,11... | collective-permute-start | bytes 983048 | tf_op jit(solution)/shard_map/ppermute | solution.py:480
  34.9 8.1 %collective-permute-start.3 = (bf16[2,128,160]{2,1,0:T(8,128)(2,1)S(1)}, bf16[2,128,160]{2,1,0:T(8,128)(2,1)S(1)}, u32[]{:S(2)}, u32[]{:S(2)}) collective-permute-start(bf16[2,128,160]{2,1,0:T(8,128)(2,1)S(1)} %get-tuple-element.47), channel_id=1, source_target_pairs={{0,2},{2,0},{4,6},{6,4},{8,10},{10,8},{12,14},{14,12},{16,18},{18,... | collective-permute-start | bytes 245768 | tf_op jit(solution)/shard_map/ppermute | solution.py:490
  35.7 7.4 %collective-permute-start.4 = (bf16[2,128,160]{2,1,0:T(8,128)(2,1)S(1)}, bf16[2,128,160]{2,1,0:T(8,128)(2,1)S(1)}, u32[]{:S(2)}, u32[]{:S(2)}) collective-permute-start(bf16[2,128,160]{2,1,0:T(8,128)(2,1)S(1)} %get-tuple-element.48), channel_id=1, source_target_pairs={{0,4},{2,6},{4,0},{6,2},{8,12},{10,14},{12,8},{14,10},{16,20},{18,... | collective-permute-start | bytes 245768 | tf_op jit(solution)/shard_map/ppermute | solution.py:490
  35.7 8.0 %collective-permute-start.5 = (bf16[2,128,160]{2,1,0:T(8,128)(2,1)S(1)}, bf16[2,128,160]{2,1,0:T(8,128)(2,1)S(1)}, u32[]{:S(2)}, u32[]{:S(2)}) collective-permute-start(bf16[2,128,160]{2,1,0:T(8,128)(2,1)S(1)} %get-tuple-element.49), channel_id=1, source_target_pairs={{0,6},{2,4},{4,2},{6,0},{8,14},{10,12},{12,10},{14,8},{16,22},{18,... | collective-permute-start | bytes 245768 | tf_op jit(solution)/shard_map/ppermute | solution.py:490
  43.7 8.5 %collective-permute-start.6 = (bf16[64,2560]{1,0:T(8,128)(2,1)S(1)}, bf16[64,2560]{1,0:T(8,128)(2,1)S(1)}, u32[]{:S(2)}, u32[]{:S(2)}) collective-permute-start(bf16[64,2560]{1,0:T(8,128)(2,1)S(1)} %temporal_attention.1.refs_0_), channel_id=1, source_target_pairs={{1,0},{0,1},{3,2},{2,3},{5,4},{4,5},{7,6},{6,7},{9,8},{8,9},{11,10... | collective-permute-start | bytes 983048 | tf_op jit(solution)/shard_map/ppermute | solution.py:477
  44.6 10.2 %collective-permute-start.9 = (bf16[64,2560]{1,0:T(8,128)(2,1)S(1)}, bf16[64,2560]{1,0:T(8,128)(2,1)S(1)}, u32[]{:S(2)}, u32[]{:S(2)}) collective-permute-start(bf16[64,2560]{1,0:T(8,128)(2,1)S(1)} %temporal_attention.1.refs_0_), channel_id=1, source_target_pairs={{0,4},{2,6},{4,0},{6,2},{8,12},{10,14},{12,8},{14,10},{16,20},{18,... | collective-permute-start | bytes 983048 | tf_op jit(solution)/shard_map/ppermute | solution.py:490
  44.9 16.2 %collective-permute-start.7 = (bf16[64,2560]{1,0:T(8,128)(2,1)S(1)}, bf16[64,2560]{1,0:T(8,128)(2,1)S(1)}, u32[]{:S(2)}, u32[]{:S(2)}) collective-permute-start(bf16[64,2560]{1,0:T(8,128)(2,1)S(1)} %temporal_attention.1.refs_0_), channel_id=1, source_target_pairs={{0,2},{2,0},{4,6},{6,4},{8,10},{10,8},{12,14},{14,12},{16,18},{18,... | collective-permute-start | bytes 983048 | tf_op jit(solution)/shard_map/ppermute | solution.py:490
  54.8 6.4 %collective-permute-start.10 = (bf16[64,2560]{1,0:T(8,128)(2,1)S(1)}, bf16[64,2560]{1,0:T(8,128)(2,1)}, u32[]{:S(2)}, u32[]{:S(2)}) collective-permute-start(bf16[64,2560]{1,0:T(8,128)(2,1)S(1)} %collective-permute-done.9.refs_4_), channel_id=1, source_target_pairs={{0,2},{2,0},{4,6},{6,4},{8,10},{10,8},{12,14},{14,12},{16,18},{18,... | collective-permute-start | bytes 983048 | tf_op jit(solution)/shard_map/ppermute | solution.py:490
  56.3 4.8 %collective-permute-start.8 = (bf16[64,2560]{1,0:T(8,128)(2,1)S(1)}, bf16[64,2560]{1,0:T(8,128)(2,1)}, u32[]{:S(2)}, u32[]{:S(2)}) collective-permute-start(bf16[64,2560]{1,0:T(8,128)(2,1)S(1)} %collective-permute-done.6.refs_1_), channel_id=1, source_target_pairs={{0,2},{2,0},{4,6},{6,4},{8,10},{10,8},{12,14},{14,12},{16,18},{18,... | collective-permute-start | bytes 983048 | tf_op jit(solution)/shard_map/ppermute | solution.py:490
  56.3 9.1 %collective-permute-start.11 = (bf16[64,2560]{1,0:T(8,128)(2,1)S(1)}, bf16[64,2560]{1,0:T(8,128)(2,1)S(1)}, u32[]{:S(2)}, u32[]{:S(2)}) collective-permute-start(bf16[64,2560]{1,0:T(8,128)(2,1)S(1)} %collective-permute-done.6.refs_1_), channel_id=1, source_target_pairs={{0,4},{2,6},{4,0},{6,2},{8,12},{10,14},{12,8},{14,10},{16,20},{18,... | collective-permute-start | bytes 983048 | tf_op jit(solution)/shard_map/ppermute | solution.py:490
  57.0 14.8 %all-to-all-start.1 = ((bf16[16,16,640]{2,1,0:T(8,128)(2,1)}), bf16[16,16,640]{2,1,0:T(8,128)(2,1)S(1)}, u32[]{:S(2)}, u32[]{:S(2)}) async-start(bf16[16,16,640]{2,1,0:T(8,128)(2,1)} %get-tuple-element.54), calls=%async_computation.1 | async-start | bytes 655360 | tf_op jit(solution)/shard_map/all_to_all | solution.py:483
  63.4 36.5 %copy-start.4 = (bf16[4,16,1280]{2,1,0:T(8,128)(2,1)S(1)}, bf16[4,16,1280]{2,1,0:T(8,128)(2,1)}, u32[]{:S(2)}) copy-start(bf16[4,16,1280]{2,1,0:T(8,128)(2,1)} %refs_3_.3) | copy-start | bytes 491524
  65.5 4.0 %collective-permute-start.12 = (bf16[64,2560]{1,0:T(8,128)(2,1)S(1)}, bf16[64,2560]{1,0:T(8,128)(2,1)S(1)}, u32[]{:S(2)}, u32[]{:S(2)}) collective-permute-start(bf16[64,2560]{1,0:T(8,128)(2,1)S(1)} %collective-permute-done.11.refs_0_), channel_id=1, source_target_pairs={{0,2},{2,0},{4,6},{6,4},{8,10},{10,8},{12,14},{14,12},{16,18},{18,... | collective-permute-start | bytes 983048 | tf_op jit(solution)/shard_map/ppermute | solution.py:490
  71.0 5.9 %collective-permute-start.16 = (bf16[80,640]{1,0:T(8,128)(2,1)S(1)}, bf16[80,640]{1,0:T(8,128)(2,1)S(1)}, u32[]{:S(2)}, u32[]{:S(2)}) collective-permute-start(bf16[80,640]{1,0:T(8,128)(2,1)S(1)} %get-tuple-element.67), channel_id=1, source_target_pairs={{0,8},{2,10},{4,12},{6,14},{8,16},{10,18},{12,20},{14,22},{16,24},... | collective-permute-start | bytes 307208 | tf_op jit(solution)/shard_map/ppermute | solution.py:490
  71.8 28.2 %collective-permute-start.19 = (bf16[16,16,640]{2,1,0:T(8,128)(2,1)S(1)}, bf16[16,16,640]{2,1,0:T(8,128)(2,1)S(1)}, u32[]{:S(2)}, u32[]{:S(2)}) collective-permute-start(bf16[16,16,640]{2,1,0:T(8,128)(2,1)S(1)} %all-to-all-done.1.refs_1_), channel_id=1, source_target_pairs={{1,0},{0,1},{3,2},{2,3},{5,4},{4,5},{7,6},{6,7},{9,8},{8,9},{11,10... | collective-permute-start | bytes 983048 | tf_op jit(solution)/shard_map/ppermute | solution.py:477
  72.7 6.7 %collective-permute-start.13 = (bf16[88,640]{1,0:T(8,128)(2,1)S(1)}, bf16[88,640]{1,0:T(8,128)(2,1)S(1)}, u32[]{:S(2)}, u32[]{:S(2)}) collective-permute-start(bf16[88,640]{1,0:T(8,128)(2,1)S(1)} %get-tuple-element.62), channel_id=1, source_target_pairs={{0,8},{2,10},{4,12},{6,14},{8,16},{10,18},{12,20},{14,22},{16,24},... | collective-permute-start | bytes 337928 | tf_op jit(solution)/shard_map/ppermute | solution.py:490
  76.9 5.4 %collective-permute-start.17 = (bf16[80,640]{1,0:T(8,128)(2,1)S(1)}, bf16[80,640]{1,0:T(8,128)(2,1)S(1)}, u32[]{:S(2)}, u32[]{:S(2)}) collective-permute-start(bf16[80,640]{1,0:T(8,128)(2,1)S(1)} %add_convert_fusion.5), channel_id=1, source_target_pairs={{0,8},{2,10},{4,12},{6,14},{8,16},{10,18},{12,20},{14,22},{16,24},... | collective-permute-start | bytes 307208 | tf_op jit(solution)/shard_map/ppermute | solution.py:490
  79.5 6.8 %collective-permute-start.14 = (bf16[88,640]{1,0:T(8,128)(2,1)S(1)}, bf16[88,640]{1,0:T(8,128)(2,1)S(1)}, u32[]{:S(2)}, u32[]{:S(2)}) collective-permute-start(bf16[88,640]{1,0:T(8,128)(2,1)S(1)} %add_convert_fusion.2), channel_id=1, source_target_pairs={{0,8},{2,10},{4,12},{6,14},{8,16},{10,18},{12,20},{14,22},{16,24},... | collective-permute-start | bytes 337928 | tf_op jit(solution)/shard_map/ppermute | solution.py:490
  82.3 5.7 %collective-permute-start.18 = (bf16[80,640]{1,0:T(8,128)(2,1)S(1)}, bf16[80,640]{1,0:T(8,128)(2,1)S(1)}, u32[]{:S(2)}, u32[]{:S(2)}) collective-permute-start(bf16[80,640]{1,0:T(8,128)(2,1)S(1)} %add_convert_fusion.4), channel_id=1, source_target_pairs={{0,8},{2,10},{4,12},{6,14},{8,16},{10,18},{12,20},{14,22},{16,24},... | collective-permute-start | bytes 307208 | tf_op jit(solution)/shard_map/ppermute | solution.py:490
  86.3 6.9 %collective-permute-start.15 = (bf16[88,640]{1,0:T(8,128)(2,1)S(1)}, bf16[88,640]{1,0:T(8,128)(2,1)S(1)}, u32[]{:S(2)}, u32[]{:S(2)}) collective-permute-start(bf16[88,640]{1,0:T(8,128)(2,1)S(1)} %add_convert_fusion.1), channel_id=1, source_target_pairs={{0,8},{2,10},{4,12},{6,14},{8,16},{10,18},{12,20},{14,22},{16,24},... | collective-permute-start | bytes 337928 | tf_op jit(solution)/shard_map/ppermute | solution.py:490
  88.0 19.5 %collective-permute-start.21 = (bf16[80,640]{1,0:T(8,128)(2,1)S(1)}, bf16[80,640]{1,0:T(8,128)(2,1)S(1)}, u32[]{:S(2)}, u32[]{:S(2)}) collective-permute-start(bf16[80,640]{1,0:T(8,128)(2,1)S(1)} %add_convert_fusion.3), channel_id=1, source_target_pairs={{0,0},{1,16},{2,8},{3,24},{4,4},{5,20},{6,12},{7,28},{8,1},{9,17},... | collective-permute-start | bytes 307208 | tf_op jit(solution)/shard_map/ppermute | solution.py:610
  93.3 13.6 %collective-permute-start.20 = (bf16[88,640]{1,0:T(8,128)(2,1)S(1)}, bf16[88,640]{1,0:T(8,128)(2,1)S(1)}, u32[]{:S(2)}, u32[]{:S(2)}) collective-permute-start(bf16[88,640]{1,0:T(8,128)(2,1)S(1)} %add_convert_fusion), channel_id=1, source_target_pairs={{0,0},{1,16},{2,8},{3,24},{4,4},{5,20},{6,12},{7,28},{8,1},{9,17},... | collective-permute-start | bytes 337928 | tf_op jit(solution)/shard_map/ppermute | solution.py:610
  (14 other events, 136.2 us)

commit v6 on v4

--- a/solution.py
+++ b/solution.py
@@ -533,6 +533,7 @@
     factors = [factors[0]] + [move(factors[d], flipped(d)) for d in range(1, 4)]
     parts = [after(parts[0], factors[0])] + [to_quad(p, s + 1) for s, p in enumerate(parts[1:])]
     (terms,) = run(temporal_kernel, "temporal_attention", [sds(tokens, 4 * width)], parts, 2)
+    terms = after(terms, *factors)
     table, early_left, late_left = run(
         table_kernel,
         "positional_table_factors",
@@ -598,9 +599,9 @@
         for i in range(2):
             if step == stage - 2:
                 totals[i] = after(totals[i], back_recv)
-            if i == 1:
-                totals[i] = after(totals[i], totals[0])
             moved = move(totals[i], ring)
+            if step == stage - 1:
+                moved = after(moved, grad_hidden)
             totals[i] = add(moved, parts_w[(i + 1) * stage - 1 - step])
     final = []
     for g in range(nf):

time: 127 us -> 106 us (0.83)
  the two profiles are of different devices: /device:TPU:5 before, /device:TPU:1 now
where the time goes in v6:
time: 106 us; the launch traced here: 105 us
  starting transfers between devices  29.2 us (28%)
  waiting for transfers between devices  26.7 us (25%)
  Pallas kernels  22.5 us (21%)
  blocking collectives  17.5 us (17%)
  local copies, waits for them, and re-layouts  6.71 us (6%)
  other arithmetic  1.87 us (2%)
    pallas_call x12, Pallas kernels, call(): pl.pallas_call(kernel, out_shape=outs, in_specs=in_specs, out_specs=[pl.B...  22.5 us
    all_to_all x1, blocking collectives, swap(): return lax.all_to_all(x, 'frame', split_axis=0, concat_axis=0, tiled=True)  17.5 us
    ppermute x15, waiting for transfers between devices, move(): return lax.ppermute(x, 'frame', pairs)  16.9 us
    ppermute x15, starting transfers between devices, move(): return lax.ppermute(x, 'frame', pairs)  10.1 us
    ppermute x2, starting transfers between devices, local(): totals = [lax.ppermute(t, ('frame', 'quad'), final) for t in totals]  10 us
    unnamed x34, local copies, waits for them, and re-layouts  6.7 us
    ppermute x4, waiting for transfers between devices, from_quad(): return lax.ppermute(x, 'quad', [((d + s) % nq, d) for d in range(nq)])  4.6 us
    ppermute x1, waiting for transfers between devices, to_quad(): return lax.ppermute(x, 'quad', [(d, (d + s) % nq) for d in range(nq)])  4.6 us
  transfers between devices with their start and end apart: 23, of which 11 were waited for; matrix products, arithmetic and copies ran while one was open for 1% of the time, Pallas kernels for 19%

profile of v6, /device:TPU:1, one launch (start us, length us, event | category | flops | bytes accessed | tf_op | source)
XLA Modules:
  0.0 105.5 jit_solution(4361028871683010564)
XLA Ops:
  0.6 2.1 %collective-permute-start = (bf16[4,16,1280]{2,1,0:T(8,128)(2,1)}, bf16[4,16,1280]{2,1,0:T(8,128)(2,1)S(1)}, u32[]{:S(2)}, u32[]{:S(2)}) collective-permute-start(bf16[4,16,1280]{2,1,0:T(8,128)(2,1)} %xs.1), channel_id=1, source_target_pairs={{1,0},{0,1},{3,2},{2,3},{5,4},{4,5},{7,6},{6,7},{9,8},{8,9},{11,10... | collective-permute-start | bytes 491528 | tf_op jit(solution)/shard_map/ppermute | solution.py:477
  3.1 2.9 %copy-done = bf16[4,1280,640]{2,1,0:T(8,128)(2,1)S(1)} copy-done((bf16[4,1280,640]{2,1,0:T(8,128)(2,1)S(1)}, bf16[4,1280,640]{2,1,0:T(8,128)(2,1)}, u32[]{:S(2)}) %copy-start) | copy-done | bytes 6553624
  8.0 1.7 %copy-done.1 = bf16[4,1280,640]{2,1,0:T(8,128)(2,1)S(1)} copy-done((bf16[4,1280,640]{2,1,0:T(8,128)(2,1)S(1)}, bf16[4,1280,640]{2,1,0:T(8,128)(2,1)}, u32[]{:S(2)}) %copy-start.1) | copy-done | bytes 6553624
  9.8 3.4 %spatial_forward.1 = (bf16[128,3200]{1,0:T(8,128)(2,1)S(1)}, bf16[16,8,640]{2,1,0:T(8,128)(2,1)S(1)}) custom-call(s32[3]{0:T(128)S(1)} %pad_add_fusion.refs_0_.geo.quad_ref, bf16[4,16,1280]{2,1,0:T(8,128)(2,1)S(1)} %copy-done.8, bf16[4,16,1280]{2,1,0:T(8,128)(2,1)S(1)} %collective-permute-done.refs_2_, f32[1280]{0:T(1024)S(1)} %copy-done.12, ...), custom_call_target="tpu_custom_call" | custom-call | flops 3000000000 | bytes 1048576 | tf_op jit(solution)/shard_map/spatial_forward/pallas_call | solution.py:430
  14.0 17.5 %all_to_all.10.received = bf16[16,16,640]{2,1,0:T(8,128)(2,1)S(1)} all-to-all(bf16[16,16,640]{2,1,0:T(8,128)(2,1)S(1)} %join_sent.1), channel_id=1, replica_groups=mesh['frame'=16,'quad'=2] {'frame'}, dimensions={0} | all-to-all | bytes 655360 | tf_op jit(solution)/shard_map/all_to_all | solution.py:483
  35.7 1.7 %collective-permute-start.5 = (bf16[2,128,160]{2,1,0:T(8,128)(2,1)S(1)}, bf16[2,128,160]{2,1,0:T(8,128)(2,1)S(1)}, u32[]{:S(2)}, u32[]{:S(2)}) collective-permute-start(bf16[2,128,160]{2,1,0:T(8,128)(2,1)S(1)} %get-tuple-element.51), channel_id=1, source_target_pairs={{0,6},{2,4},{4,2},{6,0},{8,14},{10,12},{12,10},{14,8},{16,22},{18,... | collective-permute-start | bytes 245768 | tf_op jit(solution)/shard_map/ppermute | solution.py:490
  37.4 4.6 %collective-permute-done.2.refs_1_ = bf16[64,2560]{1,0:T(8,128)(2,1)S(1)} collective-permute-done((bf16[64,2560]{1,0:T(8,128)(2,1)S(1)}, bf16[64,2560]{1,0:T(8,128)(2,1)S(1)}, u32[]{:S(2)}, u32[]{:S(2)}) %collective-permute-start.2) | collective-permute-done | bytes 327712 | tf_op jit(solution)/shard_map/ppermute | solution.py:480
  46.0 1.7 %positional_table_factors.1 = (f32[64,1280]{1,0:T(8,128)S(1)}, bf16[2,384,160]{2,1,0:T(8,128)(2,1)S(1)}, bf16[2,128,160]{2,1,0:T(8,128)(2,1)S(1)}) custom-call(s32[3]{0:T(128)S(1)} %pad_add_fusion.refs_0_.geo.quad_ref, bf16[2,128,160]{2,1,0:T(8,128)(2,1)S(1)} %get-tuple-element.46.refs_0_, bf16[2,128,160]{2,1,0:T(8,128)(2,1)S(1)} %collective-permute-done.3.refs_1_, ...), custom_call_target="tpu_custom_call" | custom-call | flops 1500000000 | bytes 1048576 | tf_op jit(solution)/shard_map/positional_table_factors/pallas_call | solution.py:430
  47.6 4.6 %collective-permute-done.6.refs_1_ = bf16[64,2560]{1,0:T(8,128)(2,1)S(1)} collective-permute-done((bf16[64,2560]{1,0:T(8,128)(2,1)S(1)}, bf16[64,2560]{1,0:T(8,128)(2,1)S(1)}, u32[]{:S(2)}, u32[]{:S(2)}) %collective-permute-start.6) | collective-permute-done | bytes 327712 | tf_op jit(solution)/shard_map/ppermute | solution.py:477
  52.2 2.5 %temporal_back_projection.1 = (bf16[16,16,640]{2,1,0:T(8,128)(2,1)}, bf16[3,160,640]{2,1,0:T(8,128)(2,1)S(1)}) custom-call(s32[3]{0:T(128)S(1)} %pad_add_fusion.refs_0_.geo.quad_ref, bf16[64,2560]{1,0:T(8,128)(2,1)S(1)} %temporal_attention.1.refs_0_, bf16[64,2560]{1,0:T(8,128)(2,1)S(1)} %collective-permute-done.6.refs_1_, bf16[4,640,640]{2,1,0:T(8,128)(2,1)S(1)} %copy-done.2), custom_call_target="tpu_custom_call" | custom-call | flops 10000000 | bytes 4096 | tf_op jit(solution)/shard_map/temporal_back_projection/pallas_call | solution.py:430
  54.8 1.6 %collective-permute-start.11 = (bf16[64,2560]{1,0:T(8,128)(2,1)S(1)}, bf16[64,2560]{1,0:T(8,128)(2,1)}, u32[]{:S(2)}, u32[]{:S(2)}) collective-permute-start(bf16[64,2560]{1,0:T(8,128)(2,1)S(1)} %collective-permute-done.10.refs_4_), channel_id=1, source_target_pairs={{0,2},{2,0},{4,6},{6,4},{8,10},{10,8},{12,14},{14,12},{16,18},{18,... | collective-permute-start | bytes 983048 | tf_op jit(solution)/shard_map/ppermute | solution.py:490
  57.0 4.1 %all-to-all-start.1 = ((bf16[16,16,640]{2,1,0:T(8,128)(2,1)}), bf16[16,16,640]{2,1,0:T(8,128)(2,1)S(1)}, u32[]{:S(2)}, u32[]{:S(2)}) async-start(bf16[16,16,640]{2,1,0:T(8,128)(2,1)} %get-tuple-element.56), calls=%async_computation.1 | async-start | bytes 655360 | tf_op jit(solution)/shard_map/all_to_all | solution.py:483
  61.2 2.3 %weight_terms_first_tokens.1 = (f32[4,4,40,640]{3,2,1,0:T(8,128)S(1)}, f32[1,160]{1,0:T(1,128)S(1)}) custom-call(s32[3]{0:T(128)S(1)} %pad_add_fusion.refs_0_.geo.quad_ref, bf16[2,384,160]{2,1,0:T(8,128)(2,1)S(1)} %get-tuple-element.60.left, bf16[3,160,640]{2,1,0:T(8,128)(2,1)S(1)} %get-tuple-element.61.weights, f32[64,1280]{1,0:T(8,128)S(1)} %get-tuple-element.54.pos, ...), custom_call_target="tpu_custom_call" | custom-call | flops 10000000 | bytes 4096 | tf_op jit(solution)/shard_map/weight_terms_first_tokens/pallas_call | solution.py:430
  63.5 2.0 %collective-permute-done.12.refs_0_ = bf16[64,2560]{1,0:T(8,128)(2,1)S(1)} collective-permute-done((bf16[64,2560]{1,0:T(8,128)(2,1)S(1)}, bf16[64,2560]{1,0:T(8,128)(2,1)S(1)}, u32[]{:S(2)}, u32[]{:S(2)}) %collective-permute-start.12) | collective-permute-done | bytes 327712 | tf_op jit(solution)/shard_map/ppermute | solution.py:490
  65.4 2.8 %collective-permute-start.13 = (bf16[64,2560]{1,0:T(8,128)(2,1)S(1)}, bf16[64,2560]{1,0:T(8,128)(2,1)S(1)}, u32[]{:S(2)}, u32[]{:S(2)}) collective-permute-start(bf16[64,2560]{1,0:T(8,128)(2,1)S(1)} %collective-permute-done.12.refs_0_), channel_id=1, source_target_pairs={{0,2},{2,0},{4,6},{6,4},{8,10},{10,8},{12,14},{14,12},{16,18},{18,... | collective-permute-start | bytes 983048 | tf_op jit(solution)/shard_map/ppermute | solution.py:490
  69.5 1.5 %weight_terms_last_tokens.1 = (bf16[88,640]{1,0:T(8,128)(2,1)S(1)}, bf16[88,640]{1,0:T(8,128)(2,1)S(1)}, bf16[88,640]{1,0:T(8,128)(2,1)S(1)}, bf16[88,640]{1,0:T...) custom-call(s32[3]{0:T(128)S(1)} %pad_add_fusion.refs_0_.geo.quad_re, ...), custom_call_target="tpu_custom_call" | custom-call | flops 10000000 | bytes 4096 | tf_op jit(solution)/shard_map/weight_terms_last_tokens/pallas_call | solution.py:430
  73.3 3.6 %collective-permute-done.17 = bf16[80,640]{1,0:T(8,128)(2,1)S(1)} collective-permute-done((bf16[80,640]{1,0:T(8,128)(2,1)S(1)}, bf16[80,640]{1,0:T(8,128)(2,1)S(1)}, u32[]{:S(2)}, u32[]{:S(2)}) %collective-permute-start.17) | collective-permute-done | bytes 102432 | tf_op jit(solution)/shard_map/ppermute | solution.py:490
  77.0 2.5 %collective-permute-done.14 = bf16[88,640]{1,0:T(8,128)(2,1)S(1)} collective-permute-done((bf16[88,640]{1,0:T(8,128)(2,1)S(1)}, bf16[88,640]{1,0:T(8,128)(2,1)S(1)}, u32[]{:S(2)}, u32[]{:S(2)}) %collective-permute-start.14) | collective-permute-done | bytes 112672 | tf_op jit(solution)/shard_map/ppermute | solution.py:490
  79.6 2.7 %collective-permute-done.18 = bf16[80,640]{1,0:T(8,128)(2,1)S(1)} collective-permute-done((bf16[80,640]{1,0:T(8,128)(2,1)S(1)}, bf16[80,640]{1,0:T(8,128)(2,1)S(1)}, u32[]{:S(2)}, u32[]{:S(2)}) %collective-permute-start.18) | collective-permute-done | bytes 102432 | tf_op jit(solution)/shard_map/ppermute | solution.py:490
  82.4 3.9 %collective-permute-done.15 = bf16[88,640]{1,0:T(8,128)(2,1)S(1)} collective-permute-done((bf16[88,640]{1,0:T(8,128)(2,1)S(1)}, bf16[88,640]{1,0:T(8,128)(2,1)S(1)}, u32[]{:S(2)}, u32[]{:S(2)}) %collective-permute-start.15) | collective-permute-done | bytes 112672 | tf_op jit(solution)/shard_map/ppermute | solution.py:490
  87.8 1.7 %block_output_hidden_gradient.1 = (bf16[4,16,1280]{2,1,0:T(8,128)(2,1)}, bf16[128,1280]{1,0:T(8,128)(2,1)S(1)}) custom-call(s32[3]{0:T(128)S(1)} %pad_add_fusion.refs_0_.geo.quad_ref, bf16[16,16,640]{2,1,0:T(8,128)(2,1)S(1)} %all-to-all-done.1.refs_1_, bf16[16,16,640]{2,1,0:T(8,128)(2,1)S(1)} %collective-permute-done.7.refs_2_, ...), custom_call_target="tpu_custom_call" | custom-call | flops 6000000000 | bytes 1048576 | tf_op jit(solution)/shard_map/block_output_hidden_gradient/pallas_call | solution.py:430
  89.5 3.6 %collective-permute-start.21 = (bf16[80,640]{1,0:T(8,128)(2,1)S(1)}, bf16[80,640]{1,0:T(8,128)(2,1)S(1)}, u32[]{:S(2)}, u32[]{:S(2)}) collective-permute-start(bf16[80,640]{1,0:T(8,128)(2,1)S(1)} %add_convert_fusion.3), channel_id=1, source_target_pairs={{0,0},{1,16},{2,8},{3,24},{4,4},{5,20},{6,12},{7,28},{8,1},{9,17},... | collective-permute-start | bytes 307208 | tf_op jit(solution)/shard_map/ppermute | solution.py:612
  93.5 6.4 %collective-permute-start.20 = (bf16[88,640]{1,0:T(8,128)(2,1)S(1)}, bf16[88,640]{1,0:T(8,128)(2,1)S(1)}, u32[]{:S(2)}, u32[]{:S(2)}) collective-permute-start(bf16[88,640]{1,0:T(8,128)(2,1)S(1)} %add_convert_fusion), channel_id=1, source_target_pairs={{0,0},{1,16},{2,8},{3,24},{4,4},{5,20},{6,12},{7,28},{8,1},{9,17},... | collective-permute-start | bytes 337928 | tf_op jit(solution)/shard_map/ppermute | solution.py:612
  100.0 4.1 %spatial_backward.1 = bf16[4,16,1280]{2,1,0:T(8,128)(2,1)} custom-call(bf16[128,1280]{1,0:T(8,128)(2,1)S(1)} %get-tuple-element.79.grad_hidden, bf16[4,16,1280]{2,1,0:T(8,128)(2,1)S(1)} %copy-done.9, bf16[128,3200]{1,0:T(8,128)(2,1)S(1)} %copy-done.14, f32[1280]{0:T(1024)S(1)} %copy-done.12, bf16[4,1280,640]{2,1,0:T(8,128)(2,1)S(1)} %bitcast.7), custom_call_target="tpu_custom_call" | custom-call | flops 3500000000 | bytes 1048576 | tf_op jit(solution)/shard_map/spatial_backward/pallas_call | solution.py:430
  (84 shorter events, 19.1 us)
Async XLA Ops:
  0.6 7.0 %collective-permute-start = (bf16[4,16,1280]{2,1,0:T(8,128)(2,1)}, bf16[4,16,1280]{2,1,0:T(8,128)(2,1)S(1)}, u32[]{:S(2)}, u32[]{:S(2)}) collective-permute-start(bf16[4,16,1280]{2,1,0:T(8,128)(2,1)} %xs.1), channel_id=1, source_target_pairs={{1,0},{0,1},{3,2},{2,3},{5,4},{4,5},{7,6},{6,7},{9,8},{8,9},{11,10... | collective-permute-start | bytes 491528 | tf_op jit(solution)/shard_map/ppermute | solution.py:477
  7.6 5.6 %collective-permute-start.1 = (bf16[4,16,1280]{2,1,0:T(8,128)(2,1)S(1)}, bf16[4,16,1280]{2,1,0:T(8,128)(2,1)S(1)}, u32[]{:S(2)}, u32[]{:S(2)}) collective-permute-start(bf16[4,16,1280]{2,1,0:T(8,128)(2,1)S(1)} %copy-done.3), channel_id=1, source_target_pairs={{1,0},{0,1},{3,2},{2,3},{5,4},{4,5},{7,6},{6,7},{9,8},{8,9},{11,10... | collective-permute-start | bytes 491528 | tf_op jit(solution)/shard_map/ppermute | solution.py:477
  33.0 9.0 %collective-permute-start.2 = (bf16[64,2560]{1,0:T(8,128)(2,1)S(1)}, bf16[64,2560]{1,0:T(8,128)(2,1)S(1)}, u32[]{:S(2)}, u32[]{:S(2)}) collective-permute-start(bf16[64,2560]{1,0:T(8,128)(2,1)S(1)} %get-tuple-element.48), channel_id=1, source_target_pairs={{0,1},{1,0},{2,3},{3,2},{4,5},{5,4},{6,7},{7,6},{8,9},{9,8},{10,11... | collective-permute-start | bytes 983048 | tf_op jit(solution)/shard_map/ppermute | solution.py:480
  34.9 8.1 %collective-permute-start.3 = (bf16[2,128,160]{2,1,0:T(8,128)(2,1)S(1)}, bf16[2,128,160]{2,1,0:T(8,128)(2,1)S(1)}, u32[]{:S(2)}, u32[]{:S(2)}) collective-permute-start(bf16[2,128,160]{2,1,0:T(8,128)(2,1)S(1)} %get-tuple-element.49), channel_id=1, source_target_pairs={{0,2},{2,0},{4,6},{6,4},{8,10},{10,8},{12,14},{14,12},{16,18},{18,... | collective-permute-start | bytes 245768 | tf_op jit(solution)/shard_map/ppermute | solution.py:490
  35.7 7.4 %collective-permute-start.4 = (bf16[2,128,160]{2,1,0:T(8,128)(2,1)S(1)}, bf16[2,128,160]{2,1,0:T(8,128)(2,1)S(1)}, u32[]{:S(2)}, u32[]{:S(2)}) collective-permute-start(bf16[2,128,160]{2,1,0:T(8,128)(2,1)S(1)} %get-tuple-element.50), channel_id=1, source_target_pairs={{0,4},{2,6},{4,0},{6,2},{8,12},{10,14},{12,8},{14,10},{16,20},{18,... | collective-permute-start | bytes 245768 | tf_op jit(solution)/shard_map/ppermute | solution.py:490
  35.7 8.0 %collective-permute-start.5 = (bf16[2,128,160]{2,1,0:T(8,128)(2,1)S(1)}, bf16[2,128,160]{2,1,0:T(8,128)(2,1)S(1)}, u32[]{:S(2)}, u32[]{:S(2)}) collective-permute-start(bf16[2,128,160]{2,1,0:T(8,128)(2,1)S(1)} %get-tuple-element.51), channel_id=1, source_target_pairs={{0,6},{2,4},{4,2},{6,0},{8,14},{10,12},{12,10},{14,8},{16,22},{18,... | collective-permute-start | bytes 245768 | tf_op jit(solution)/shard_map/ppermute | solution.py:490
  43.7 8.5 %collective-permute-start.6 = (bf16[64,2560]{1,0:T(8,128)(2,1)S(1)}, bf16[64,2560]{1,0:T(8,128)(2,1)S(1)}, u32[]{:S(2)}, u32[]{:S(2)}) collective-permute-start(bf16[64,2560]{1,0:T(8,128)(2,1)S(1)} %temporal_attention.1.refs_0_), channel_id=1, source_target_pairs={{1,0},{0,1},{3,2},{2,3},{5,4},{4,5},{7,6},{6,7},{9,8},{8,9},{11,10... | collective-permute-start | bytes 983048 | tf_op jit(solution)/shard_map/ppermute | solution.py:477
  44.6 10.2 %collective-permute-start.10 = (bf16[64,2560]{1,0:T(8,128)(2,1)S(1)}, bf16[64,2560]{1,0:T(8,128)(2,1)S(1)}, u32[]{:S(2)}, u32[]{:S(2)}) collective-permute-start(bf16[64,2560]{1,0:T(8,128)(2,1)S(1)} %temporal_attention.1.refs_0_), channel_id=1, source_target_pairs={{0,4},{2,6},{4,0},{6,2},{8,12},{10,14},{12,8},{14,10},{16,20},{18,... | collective-permute-start | bytes 983048 | tf_op jit(solution)/shard_map/ppermute | solution.py:490
  44.9 16.2 %collective-permute-start.8 = (bf16[64,2560]{1,0:T(8,128)(2,1)S(1)}, bf16[64,2560]{1,0:T(8,128)(2,1)S(1)}, u32[]{:S(2)}, u32[]{:S(2)}) collective-permute-start(bf16[64,2560]{1,0:T(8,128)(2,1)S(1)} %temporal_attention.1.refs_0_), channel_id=1, source_target_pairs={{0,2},{2,0},{4,6},{6,4},{8,10},{10,8},{12,14},{14,12},{16,18},{18,... | collective-permute-start | bytes 983048 | tf_op jit(solution)/shard_map/ppermute | solution.py:490
  54.8 6.4 %collective-permute-start.11 = (bf16[64,2560]{1,0:T(8,128)(2,1)S(1)}, bf16[64,2560]{1,0:T(8,128)(2,1)}, u32[]{:S(2)}, u32[]{:S(2)}) collective-permute-start(bf16[64,2560]{1,0:T(8,128)(2,1)S(1)} %collective-permute-done.10.refs_4_), channel_id=1, source_target_pairs={{0,2},{2,0},{4,6},{6,4},{8,10},{10,8},{12,14},{14,12},{16,18},{18,... | collective-permute-start | bytes 983048 | tf_op jit(solution)/shard_map/ppermute | solution.py:490
  56.3 4.8 %collective-permute-start.9 = (bf16[64,2560]{1,0:T(8,128)(2,1)S(1)}, bf16[64,2560]{1,0:T(8,128)(2,1)}, u32[]{:S(2)}, u32[]{:S(2)}) collective-permute-start(bf16[64,2560]{1,0:T(8,128)(2,1)S(1)} %collective-permute-done.6.refs_1_), channel_id=1, source_target_pairs={{0,2},{2,0},{4,6},{6,4},{8,10},{10,8},{12,14},{14,12},{16,18},{18,... | collective-permute-start | bytes 983048 | tf_op jit(solution)/shard_map/ppermute | solution.py:490
  56.3 9.1 %collective-permute-start.12 = (bf16[64,2560]{1,0:T(8,128)(2,1)S(1)}, bf16[64,2560]{1,0:T(8,128)(2,1)S(1)}, u32[]{:S(2)}, u32[]{:S(2)}) collective-permute-start(bf16[64,2560]{1,0:T(8,128)(2,1)S(1)} %collective-permute-done.6.refs_1_), channel_id=1, source_target_pairs={{0,4},{2,6},{4,0},{6,2},{8,12},{10,14},{12,8},{14,10},{16,20},{18,... | collective-permute-start | bytes 983048 | tf_op jit(solution)/shard_map/ppermute | solution.py:490
  57.0 14.8 %all-to-all-start.1 = ((bf16[16,16,640]{2,1,0:T(8,128)(2,1)}), bf16[16,16,640]{2,1,0:T(8,128)(2,1)S(1)}, u32[]{:S(2)}, u32[]{:S(2)}) async-start(bf16[16,16,640]{2,1,0:T(8,128)(2,1)} %get-tuple-element.56), calls=%async_computation.1 | async-start | bytes 655360 | tf_op jit(solution)/shard_map/all_to_all | solution.py:483
  61.2 25.5 %copy-start.4 = (bf16[4,16,1280]{2,1,0:T(8,128)(2,1)S(1)}, bf16[4,16,1280]{2,1,0:T(8,128)(2,1)}, u32[]{:S(2)}) copy-start(bf16[4,16,1280]{2,1,0:T(8,128)(2,1)} %refs_3_.3) | copy-start | bytes 491524
  65.4 4.1 %collective-permute-start.13 = (bf16[64,2560]{1,0:T(8,128)(2,1)S(1)}, bf16[64,2560]{1,0:T(8,128)(2,1)S(1)}, u32[]{:S(2)}, u32[]{:S(2)}) collective-permute-start(bf16[64,2560]{1,0:T(8,128)(2,1)S(1)} %collective-permute-done.12.refs_0_), channel_id=1, source_target_pairs={{0,2},{2,0},{4,6},{6,4},{8,10},{10,8},{12,14},{14,12},{16,18},{18,... | collective-permute-start | bytes 983048 | tf_op jit(solution)/shard_map/ppermute | solution.py:490
  71.0 5.9 %collective-permute-start.17 = (bf16[80,640]{1,0:T(8,128)(2,1)S(1)}, bf16[80,640]{1,0:T(8,128)(2,1)S(1)}, u32[]{:S(2)}, u32[]{:S(2)}) collective-permute-start(bf16[80,640]{1,0:T(8,128)(2,1)S(1)} %get-tuple-element.73), channel_id=1, source_target_pairs={{0,8},{2,10},{4,12},{6,14},{8,16},{10,18},{12,20},{14,22},{16,24},... | collective-permute-start | bytes 307208 | tf_op jit(solution)/shard_map/ppermute | solution.py:490
  71.8 14.8 %collective-permute-start.7 = (bf16[16,16,640]{2,1,0:T(8,128)(2,1)S(1)}, bf16[16,16,640]{2,1,0:T(8,128)(2,1)S(1)}, u32[]{:S(2)}, u32[]{:S(2)}) collective-permute-start(bf16[16,16,640]{2,1,0:T(8,128)(2,1)S(1)} %all-to-all-done.1.refs_1_), channel_id=1, source_target_pairs={{1,0},{0,1},{3,2},{2,3},{5,4},{4,5},{7,6},{6,7},{9,8},{8,9},{11,10... | collective-permute-start | bytes 983048 | tf_op jit(solution)/shard_map/ppermute | solution.py:477
  72.7 6.8 %collective-permute-start.14 = (bf16[88,640]{1,0:T(8,128)(2,1)S(1)}, bf16[88,640]{1,0:T(8,128)(2,1)S(1)}, u32[]{:S(2)}, u32[]{:S(2)}) collective-permute-start(bf16[88,640]{1,0:T(8,128)(2,1)S(1)} %get-tuple-element.67), channel_id=1, source_target_pairs={{0,8},{2,10},{4,12},{6,14},{8,16},{10,18},{12,20},{14,22},{16,24},... | collective-permute-start | bytes 337928 | tf_op jit(solution)/shard_map/ppermute | solution.py:490
  77.0 5.4 %collective-permute-start.18 = (bf16[80,640]{1,0:T(8,128)(2,1)S(1)}, bf16[80,640]{1,0:T(8,128)(2,1)S(1)}, u32[]{:S(2)}, u32[]{:S(2)}) collective-permute-start(bf16[80,640]{1,0:T(8,128)(2,1)S(1)} %add_convert_fusion.5), channel_id=1, source_target_pairs={{0,8},{2,10},{4,12},{6,14},{8,16},{10,18},{12,20},{14,22},{16,24},... | collective-permute-start | bytes 307208 | tf_op jit(solution)/shard_map/ppermute | solution.py:490
  79.5 6.8 %collective-permute-start.15 = (bf16[88,640]{1,0:T(8,128)(2,1)S(1)}, bf16[88,640]{1,0:T(8,128)(2,1)S(1)}, u32[]{:S(2)}, u32[]{:S(2)}) collective-permute-start(bf16[88,640]{1,0:T(8,128)(2,1)S(1)} %add_convert_fusion.2), channel_id=1, source_target_pairs={{0,8},{2,10},{4,12},{6,14},{8,16},{10,18},{12,20},{14,22},{16,24},... | collective-permute-start | bytes 337928 | tf_op jit(solution)/shard_map/ppermute | solution.py:490
  82.3 7.1 %collective-permute-start.19 = (bf16[80,640]{1,0:T(8,128)(2,1)S(1)}, bf16[80,640]{1,0:T(8,128)(2,1)S(1)}, u32[]{:S(2)}, u32[]{:S(2)}) collective-permute-start(bf16[80,640]{1,0:T(8,128)(2,1)S(1)} %add_convert_fusion.4), channel_id=1, source_target_pairs={{0,8},{2,10},{4,12},{6,14},{8,16},{10,18},{12,20},{14,22},{16,24},... | collective-permute-start | bytes 307208 | tf_op jit(solution)/shard_map/ppermute | solution.py:490
  86.4 7.2 %collective-permute-start.16 = (bf16[88,640]{1,0:T(8,128)(2,1)S(1)}, bf16[88,640]{1,0:T(8,128)(2,1)S(1)}, u32[]{:S(2)}, u32[]{:S(2)}) collective-permute-start(bf16[88,640]{1,0:T(8,128)(2,1)S(1)} %add_convert_fusion.1), channel_id=1, source_target_pairs={{0,8},{2,10},{4,12},{6,14},{8,16},{10,18},{12,20},{14,22},{16,24},... | collective-permute-start | bytes 337928 | tf_op jit(solution)/shard_map/ppermute | solution.py:490
  89.5 15.2 %collective-permute-start.21 = (bf16[80,640]{1,0:T(8,128)(2,1)S(1)}, bf16[80,640]{1,0:T(8,128)(2,1)S(1)}, u32[]{:S(2)}, u32[]{:S(2)}) collective-permute-start(bf16[80,640]{1,0:T(8,128)(2,1)S(1)} %add_convert_fusion.3), channel_id=1, source_target_pairs={{0,0},{1,16},{2,8},{3,24},{4,4},{5,20},{6,12},{7,28},{8,1},{9,17},... | collective-permute-start | bytes 307208 | tf_op jit(solution)/shard_map/ppermute | solution.py:612
  93.5 10.5 %collective-permute-start.20 = (bf16[88,640]{1,0:T(8,128)(2,1)S(1)}, bf16[88,640]{1,0:T(8,128)(2,1)S(1)}, u32[]{:S(2)}, u32[]{:S(2)}) collective-permute-start(bf16[88,640]{1,0:T(8,128)(2,1)S(1)} %add_convert_fusion), channel_id=1, source_target_pairs={{0,0},{1,16},{2,8},{3,24},{4,4},{5,20},{6,12},{7,28},{8,1},{9,17},... | collective-permute-start | bytes 337928 | tf_op jit(solution)/shard_map/ppermute | solution.py:612
  (16 other events, 165.5 us)

commit v7 on v6

--- a/solution.py
+++ b/solution.py
@@ -255,6 +255,17 @@
             send[:, lanes] = product[(s + 1) * tokens : (s + 2) * tokens].astype(BF16)
 
 
+def gray(place):
+    return place ^ (place >> 1)
+
+
+def place_of(z, stage):
+    place, shift = z, z >> 1
+    for _ in range(log2(stage) - 1):
+        place, shift = place ^ shift, shift >> 1
+    return place
+
+
 def quarter_of(four):
     return ((four & 1) << 1) | (four >> 1)
 
@@ -376,7 +387,7 @@
     extra = jnp.concatenate([gain, jnp.zeros((1, width - rows), F32)], axis=1)
     extra = jnp.where(iota((8, width), 0) == 0, extra, 0.0)
     for r in range(stage):
-        z = (geo[2] + r) & (stage - 1)
+        z = gray((place_of(geo[2], stage) + r) & (stage - 1))
         rows_out = jnp.concatenate([blocks[0, z], blocks[1, z], extra], axis=0)
         outs[r][...] = rows_out.astype(BF16)
         rows_out = jnp.concatenate([blocks[2, z], blocks[3, z]], axis=0)
@@ -494,7 +505,8 @@
     def flipped(bits):
         return [(g, g ^ bits) for g in range(nf)]
 
-    ring = [(g, (g + 4) % nf) for g in range(nf)]
+    turns = [gray((place_of(z, nf // 4) + 1) % (nf // 4)) for z in range(nf // 4)]
+    ring = [(g, turns[g // 4] * 4 + g % 4) for g in range(nf)]
 
     gain1, gain2 = spatial_gain, motion_gain
     sent = sds(nf, nq * fr, half)
@@ -552,7 +564,7 @@
         back_kernel,
         "temporal_back_projection",
         [sds(nf, 2 * nq * fr, half), sds(3, half // 4, width)],
-        [geo] + all_terms + [motion_weights],
+        [geo, after(all_terms[0], core_terms[-1])] + all_terms[1:] + [motion_weights],
         0.01,
     )
     pair_terms[0] = after(pair_terms[0], back_send)

time: 106 us -> 112 us (1.057)
  waiting for transfers between devices: 26.7 us -> 35 us
  starting transfers between devices: 29.2 us -> 27.3 us
    ppermute x15, waiting for transfers between devices: 16.9 us -> 22.9 us  [move(): return lax.ppermute(x, 'frame', pairs)]
    ppermute x2, waiting for transfers between devices: 0.01 us -> 1.51 us  [local(): totals = [lax.ppermute(t, ('frame', 'quad'), final) for t in totals]]
    ppermute x4, waiting for transfers between devices: 4.6 us -> 5.99 us  [from_quad(): return lax.ppermute(x, 'quad', [((d + s) % nq, d) for d in range(nq)])]
  transfers between devices with their start and end apart: 23 -> 23, of which waited for: 11 -> 12; matrix products, arithmetic and copies ran while one was open for 1% -> 1% of each run, Pallas kernels for 19% -> 18%
where the time goes in v7:
time: 112 us
  waiting for transfers between devices  35 us (31%)
  starting transfers between devices  27.3 us (24%)
  Pallas kernels  22.3 us (20%)
  blocking collectives  17.5 us (16%)
  local copies, waits for them, and re-layouts  6.71 us (6%)
  other arithmetic  1.87 us (2%)
    ppermute x15, waiting for transfers between devices, move(): return lax.ppermute(x, 'frame', pairs)  22.9 us
    pallas_call x12, Pallas kernels, call(): pl.pallas_call(kernel, out_shape=outs, in_specs=in_specs, out_specs=[pl.B...  22.3 us
    all_to_all x1, blocking collectives, swap(): return lax.all_to_all(x, 'frame', split_axis=0, concat_axis=0, tiled=True)  17.5 us
    ppermute x2, starting transfers between devices, local(): totals = [lax.ppermute(t, ('frame', 'quad'), final) for t in totals]  9.7 us
    ppermute x15, starting transfers between devices, move(): return lax.ppermute(x, 'frame', pairs)  8.94 us
    unnamed x34, local copies, waits for them, and re-layouts  6.7 us
    ppermute x4, waiting for transfers between devices, from_quad(): return lax.ppermute(x, 'quad', [((d + s) % nq, d) for d in range(nq)])  5.99 us
    ppermute x1, waiting for transfers between devices, to_quad(): return lax.ppermute(x, 'quad', [(d, (d + s) % nq) for d in range(nq)])  4.6 us
  transfers between devices with their start and end apart: 23, of which 12 were waited for; matrix products, arithmetic and copies ran while one was open for 1% of the time, Pallas kernels for 18%

profile of v7, /device:TPU:1, one launch (start us, length us, event | category | flops | bytes accessed | tf_op | source)
XLA Modules:
  0.0 111.7 jit_solution(6306307485746584707)
XLA Ops:
  0.6 2.1 %collective-permute-start = (bf16[4,16,1280]{2,1,0:T(8,128)(2,1)}, bf16[4,16,1280]{2,1,0:T(8,128)(2,1)S(1)}, u32[]{:S(2)}, u32[]{:S(2)}) collective-permute-start(bf16[4,16,1280]{2,1,0:T(8,128)(2,1)} %xs.1), channel_id=1, source_target_pairs={{1,0},{0,1},{3,2},{2,3},{5,4},{4,5},{7,6},{6,7},{9,8},{8,9},{11,10... | collective-permute-start | bytes 491528 | tf_op jit(solution)/shard_map/ppermute | solution.py:488
  3.1 2.9 %copy-done = bf16[4,1280,640]{2,1,0:T(8,128)(2,1)S(1)} copy-done((bf16[4,1280,640]{2,1,0:T(8,128)(2,1)S(1)}, bf16[4,1280,640]{2,1,0:T(8,128)(2,1)}, u32[]{:S(2)}) %copy-start) | copy-done | bytes 6553624
  8.0 1.7 %copy-done.1 = bf16[4,1280,640]{2,1,0:T(8,128)(2,1)S(1)} copy-done((bf16[4,1280,640]{2,1,0:T(8,128)(2,1)S(1)}, bf16[4,1280,640]{2,1,0:T(8,128)(2,1)}, u32[]{:S(2)}) %copy-start.1) | copy-done | bytes 6553624
  9.8 3.4 %spatial_forward.1 = (bf16[128,3200]{1,0:T(8,128)(2,1)S(1)}, bf16[16,8,640]{2,1,0:T(8,128)(2,1)S(1)}) custom-call(s32[3]{0:T(128)S(1)} %pad_add_fusion.refs_0_.geo.quad_ref, bf16[4,16,1280]{2,1,0:T(8,128)(2,1)S(1)} %copy-done.8, bf16[4,16,1280]{2,1,0:T(8,128)(2,1)S(1)} %collective-permute-done.refs_2_, f32[1280]{0:T(1024)S(1)} %copy-done.12, ...), custom_call_target="tpu_custom_call" | custom-call | flops 3000000000 | bytes 1048576 | tf_op jit(solution)/shard_map/spatial_forward/pallas_call | solution.py:441
  14.0 17.5 %all_to_all.10.received = bf16[16,16,640]{2,1,0:T(8,128)(2,1)S(1)} all-to-all(bf16[16,16,640]{2,1,0:T(8,128)(2,1)S(1)} %join_sent.1), channel_id=1, replica_groups=mesh['frame'=16,'quad'=2] {'frame'}, dimensions={0} | all-to-all | bytes 655360 | tf_op jit(solution)/shard_map/all_to_all | solution.py:494
  35.7 1.7 %collective-permute-start.5 = (bf16[2,128,160]{2,1,0:T(8,128)(2,1)S(1)}, bf16[2,128,160]{2,1,0:T(8,128)(2,1)S(1)}, u32[]{:S(2)}, u32[]{:S(2)}) collective-permute-start(bf16[2,128,160]{2,1,0:T(8,128)(2,1)S(1)} %get-tuple-element.52), channel_id=1, source_target_pairs={{0,6},{2,4},{4,2},{6,0},{8,14},{10,12},{12,10},{14,8},{16,22},{18,... | collective-permute-start | bytes 245768 | tf_op jit(solution)/shard_map/ppermute | solution.py:501
  37.4 4.6 %collective-permute-done.2.refs_1_ = bf16[64,2560]{1,0:T(8,128)(2,1)S(1)} collective-permute-done((bf16[64,2560]{1,0:T(8,128)(2,1)S(1)}, bf16[64,2560]{1,0:T(8,128)(2,1)S(1)}, u32[]{:S(2)}, u32[]{:S(2)}) %collective-permute-start.2) | collective-permute-done | bytes 327712 | tf_op jit(solution)/shard_map/ppermute | solution.py:491
  44.6 1.7 %positional_table_factors.1 = (f32[64,1280]{1,0:T(8,128)S(1)}, bf16[2,384,160]{2,1,0:T(8,128)(2,1)S(1)}, bf16[2,128,160]{2,1,0:T(8,128)(2,1)S(1)}) custom-call(s32[3]{0:T(128)S(1)} %pad_add_fusion.refs_0_.geo.quad_ref, bf16[2,128,160]{2,1,0:T(8,128)(2,1)S(1)} %get-tuple-element.47.refs_0_, bf16[2,128,160]{2,1,0:T(8,128)(2,1)S(1)} %collective-permute-done.3.refs_1_, ...), custom_call_target="tpu_custom_call" | custom-call | flops 1500000000 | bytes 1048576 | tf_op jit(solution)/shard_map/positional_table_factors/pallas_call | solution.py:441
  46.3 6.0 %collective-permute-done.6.refs_1_ = bf16[64,2560]{1,0:T(8,128)(2,1)S(1)} collective-permute-done((bf16[64,2560]{1,0:T(8,128)(2,1)S(1)}, bf16[64,2560]{1,0:T(8,128)(2,1)S(1)}, u32[]{:S(2)}, u32[]{:S(2)}) %collective-permute-start.6) | collective-permute-done | bytes 327712 | tf_op jit(solution)/shard_map/ppermute | solution.py:488
  52.2 1.6 %collective-permute-start.7 = (bf16[64,2560]{1,0:T(8,128)(2,1)S(1)}, bf16[64,2560]{1,0:T(8,128)(2,1)S(1)}, u32[]{:S(2)}, u32[]{:S(2)}) collective-permute-start(bf16[64,2560]{1,0:T(8,128)(2,1)S(1)} %collective-permute-done.6.refs_1_), channel_id=1, source_target_pairs={{0,2},{2,0},{4,6},{6,4},{8,10},{10,8},{12,14},{14,12},{16,18},{18,... | collective-permute-start | bytes 983048 | tf_op jit(solution)/shard_map/ppermute | solution.py:501
  55.1 2.5 %temporal_back_projection.1 = (bf16[16,16,640]{2,1,0:T(8,128)(2,1)}, bf16[3,160,640]{2,1,0:T(8,128)(2,1)S(1)}) custom-call(s32[3]{0:T(128)S(1)} %pad_add_fusion.refs_0_.geo.quad_ref, bf16[64,2560]{1,0:T(8,128)(2,1)S(1)} %temporal_attention.1.refs_0_, bf16[64,2560]{1,0:T(8,128)(2,1)S(1)} %collective-permute-done.6.refs_1_, bf16[4,640,640]{2,1,0:T(8,128)(2,1)S(1)} %copy-done.2), custom_call_target="tpu_custom_call" | custom-call | flops 10000000 | bytes 4096 | tf_op jit(solution)/shard_map/temporal_back_projection/pallas_call | solution.py:441
  57.6 5.6 %collective-permute-done.10.refs_4_ = bf16[64,2560]{1,0:T(8,128)(2,1)S(1)} collective-permute-done((bf16[64,2560]{1,0:T(8,128)(2,1)S(1)}, bf16[64,2560]{1,0:T(8,128)(2,1)S(1)}, u32[]{:S(2)}, u32[]{:S(2)}) %collective-permute-start.10) | collective-permute-done | bytes 327712 | tf_op jit(solution)/shard_map/ppermute | solution.py:501
  64.6 3.6 %all-to-all-start.1 = ((bf16[16,16,640]{2,1,0:T(8,128)(2,1)}), bf16[16,16,640]{2,1,0:T(8,128)(2,1)S(1)}, u32[]{:S(2)}, u32[]{:S(2)}) async-start(bf16[16,16,640]{2,1,0:T(8,128)(2,1)} %get-tuple-element.58), calls=%async_computation.1 | async-start | bytes 655360 | tf_op jit(solution)/shard_map/all_to_all | solution.py:494
  68.3 2.3 %weight_terms_first_tokens.1 = (f32[4,4,40,640]{3,2,1,0:T(8,128)S(1)}, f32[1,160]{1,0:T(1,128)S(1)}) custom-call(s32[3]{0:T(128)S(1)} %pad_add_fusion.refs_0_.geo.quad_ref, bf16[2,384,160]{2,1,0:T(8,128)(2,1)S(1)} %get-tuple-element.62.left, bf16[3,160,640]{2,1,0:T(8,128)(2,1)S(1)} %get-tuple-element.63.weights, f32[64,1280]{1,0:T(8,128)S(1)} %get-tuple-element.55.pos, ...), custom_call_target="tpu_custom_call" | custom-call | flops 10000000 | bytes 4096 | tf_op jit(solution)/shard_map/weight_terms_first_tokens/pallas_call | solution.py:441
  70.6 4.0 %collective-permute-done.12.refs_0_ = bf16[64,2560]{1,0:T(8,128)(2,1)S(1)} collective-permute-done((bf16[64,2560]{1,0:T(8,128)(2,1)S(1)}, bf16[64,2560]{1,0:T(8,128)(2,1)S(1)}, u32[]{:S(2)}, u32[]{:S(2)}) %collective-permute-start.12) | collective-permute-done | bytes 327712 | tf_op jit(solution)/shard_map/ppermute | solution.py:501
  80.4 2.9 %collective-permute-done.17 = bf16[80,640]{1,0:T(8,128)(2,1)S(1)} collective-permute-done((bf16[80,640]{1,0:T(8,128)(2,1)S(1)}, bf16[80,640]{1,0:T(8,128)(2,1)S(1)}, u32[]{:S(2)}, u32[]{:S(2)}) %collective-permute-start.17) | collective-permute-done | bytes 102432 | tf_op jit(solution)/shard_map/ppermute | solution.py:501
  83.5 2.3 %collective-permute-done.14 = bf16[88,640]{1,0:T(8,128)(2,1)S(1)} collective-permute-done((bf16[88,640]{1,0:T(8,128)(2,1)S(1)}, bf16[88,640]{1,0:T(8,128)(2,1)S(1)}, u32[]{:S(2)}, u32[]{:S(2)}) %collective-permute-start.14) | collective-permute-done | bytes 112672 | tf_op jit(solution)/shard_map/ppermute | solution.py:501
  85.9 2.0 %collective-permute-done.18 = bf16[80,640]{1,0:T(8,128)(2,1)S(1)} collective-permute-done((bf16[80,640]{1,0:T(8,128)(2,1)S(1)}, bf16[80,640]{1,0:T(8,128)(2,1)S(1)}, u32[]{:S(2)}, u32[]{:S(2)}) %collective-permute-start.18) | collective-permute-done | bytes 102432 | tf_op jit(solution)/shard_map/ppermute | solution.py:501
  88.0 3.9 %collective-permute-done.15 = bf16[88,640]{1,0:T(8,128)(2,1)S(1)} collective-permute-done((bf16[88,640]{1,0:T(8,128)(2,1)S(1)}, bf16[88,640]{1,0:T(8,128)(2,1)S(1)}, u32[]{:S(2)}, u32[]{:S(2)}) %collective-permute-start.15) | collective-permute-done | bytes 112672 | tf_op jit(solution)/shard_map/ppermute | solution.py:501
  93.1 1.7 %block_output_hidden_gradient.1 = (bf16[4,16,1280]{2,1,0:T(8,128)(2,1)}, bf16[128,1280]{1,0:T(8,128)(2,1)S(1)}) custom-call(s32[3]{0:T(128)S(1)} %pad_add_fusion.refs_0_.geo.quad_ref, bf16[16,16,640]{2,1,0:T(8,128)(2,1)S(1)} %all-to-all-done.1.refs_1_, bf16[16,16,640]{2,1,0:T(8,128)(2,1)S(1)} %collective-permute-done.8.refs_2_, ...), custom_call_target="tpu_custom_call" | custom-call | flops 6000000000 | bytes 1048576 | tf_op jit(solution)/shard_map/block_output_hidden_gradient/pallas_call | solution.py:441
  94.8 5.4 %collective-permute-start.21 = (bf16[80,640]{1,0:T(8,128)(2,1)S(1)}, bf16[80,640]{1,0:T(8,128)(2,1)S(1)}, u32[]{:S(2)}, u32[]{:S(2)}) collective-permute-start(bf16[80,640]{1,0:T(8,128)(2,1)S(1)} %add_convert_fusion.3), channel_id=1, source_target_pairs={{0,0},{1,16},{2,8},{3,24},{4,4},{5,20},{6,12},{7,28},{8,1},{9,17},... | collective-permute-start | bytes 307208 | tf_op jit(solution)/shard_map/ppermute | solution.py:624
  100.3 4.3 %collective-permute-start.20 = (bf16[88,640]{1,0:T(8,128)(2,1)S(1)}, bf16[88,640]{1,0:T(8,128)(2,1)S(1)}, u32[]{:S(2)}, u32[]{:S(2)}) collective-permute-start(bf16[88,640]{1,0:T(8,128)(2,1)S(1)} %add_convert_fusion), channel_id=1, source_target_pairs={{0,0},{1,16},{2,8},{3,24},{4,4},{5,20},{6,12},{7,28},{8,1},{9,17},... | collective-permute-start | bytes 337928 | tf_op jit(solution)/shard_map/ppermute | solution.py:624
  104.6 4.1 %spatial_backward.1 = bf16[4,16,1280]{2,1,0:T(8,128)(2,1)} custom-call(bf16[128,1280]{1,0:T(8,128)(2,1)S(1)} %get-tuple-element.81.grad_hidden, bf16[4,16,1280]{2,1,0:T(8,128)(2,1)S(1)} %copy-done.9, bf16[128,3200]{1,0:T(8,128)(2,1)S(1)} %copy-done.14, f32[1280]{0:T(1024)S(1)} %copy-done.12, bf16[4,1280,640]{2,1,0:T(8,128)(2,1)S(1)} %bitcast.7), custom_call_target="tpu_custom_call" | custom-call | flops 3500000000 | bytes 1048576 | tf_op jit(solution)/shard_map/spatial_backward/pallas_call | solution.py:441
  108.7 1.5 %collective-permute-done.20 = bf16[88,640]{1,0:T(8,128)(2,1)S(1)} collective-permute-done((bf16[88,640]{1,0:T(8,128)(2,1)S(1)}, bf16[88,640]{1,0:T(8,128)(2,1)S(1)}, u32[]{:S(2)}, u32[]{:S(2)}) %collective-permute-start.20) | collective-permute-done | bytes 112672 | tf_op jit(solution)/shard_map/ppermute | solution.py:624
  (84 shorter events, 21.4 us)
Async XLA Ops:
  0.6 7.0 %collective-permute-start = (bf16[4,16,1280]{2,1,0:T(8,128)(2,1)}, bf16[4,16,1280]{2,1,0:T(8,128)(2,1)S(1)}, u32[]{:S(2)}, u32[]{:S(2)}) collective-permute-start(bf16[4,16,1280]{2,1,0:T(8,128)(2,1)} %xs.1), channel_id=1, source_target_pairs={{1,0},{0,1},{3,2},{2,3},{5,4},{4,5},{7,6},{6,7},{9,8},{8,9},{11,10... | collective-permute-start | bytes 491528 | tf_op jit(solution)/shard_map/ppermute | solution.py:488
  7.6 23.9 %copy-start.2 = (bf16[4,640,640]{2,1,0:T(8,128)(2,1)S(1)}, bf16[4,640,640]{2,1,0:T(8,128)(2,1)}, u32[]{:S(2)}) copy-start(bf16[4,640,640]{2,1,0:T(8,128)(2,1)} %refs_2_.1) | copy-start | bytes 9830404
  7.6 5.6 %collective-permute-start.1 = (bf16[4,16,1280]{2,1,0:T(8,128)(2,1)S(1)}, bf16[4,16,1280]{2,1,0:T(8,128)(2,1)S(1)}, u32[]{:S(2)}, u32[]{:S(2)}) collective-permute-start(bf16[4,16,1280]{2,1,0:T(8,128)(2,1)S(1)} %copy-done.3), channel_id=1, source_target_pairs={{1,0},{0,1},{3,2},{2,3},{5,4},{4,5},{7,6},{6,7},{9,8},{8,9},{11,10... | collective-permute-start | bytes 491528 | tf_op jit(solution)/shard_map/ppermute | solution.py:488
  33.0 9.0 %collective-permute-start.2 = (bf16[64,2560]{1,0:T(8,128)(2,1)S(1)}, bf16[64,2560]{1,0:T(8,128)(2,1)S(1)}, u32[]{:S(2)}, u32[]{:S(2)}) collective-permute-start(bf16[64,2560]{1,0:T(8,128)(2,1)S(1)} %get-tuple-element.49), channel_id=1, source_target_pairs={{0,1},{1,0},{2,3},{3,2},{4,5},{5,4},{6,7},{7,6},{8,9},{9,8},{10,11... | collective-permute-start | bytes 983048 | tf_op jit(solution)/shard_map/ppermute | solution.py:491
  34.9 8.1 %collective-permute-start.3 = (bf16[2,128,160]{2,1,0:T(8,128)(2,1)S(1)}, bf16[2,128,160]{2,1,0:T(8,128)(2,1)S(1)}, u32[]{:S(2)}, u32[]{:S(2)}) collective-permute-start(bf16[2,128,160]{2,1,0:T(8,128)(2,1)S(1)} %get-tuple-element.50), channel_id=1, source_target_pairs={{0,2},{2,0},{4,6},{6,4},{8,10},{10,8},{12,14},{14,12},{16,18},{18,... | collective-permute-start | bytes 245768 | tf_op jit(solution)/shard_map/ppermute | solution.py:501
  35.7 7.4 %collective-permute-start.4 = (bf16[2,128,160]{2,1,0:T(8,128)(2,1)S(1)}, bf16[2,128,160]{2,1,0:T(8,128)(2,1)S(1)}, u32[]{:S(2)}, u32[]{:S(2)}) collective-permute-start(bf16[2,128,160]{2,1,0:T(8,128)(2,1)S(1)} %get-tuple-element.51), channel_id=1, source_target_pairs={{0,4},{2,6},{4,0},{6,2},{8,12},{10,14},{12,8},{14,10},{16,20},{18,... | collective-permute-start | bytes 245768 | tf_op jit(solution)/shard_map/ppermute | solution.py:501
  35.7 8.0 %collective-permute-start.5 = (bf16[2,128,160]{2,1,0:T(8,128)(2,1)S(1)}, bf16[2,128,160]{2,1,0:T(8,128)(2,1)S(1)}, u32[]{:S(2)}, u32[]{:S(2)}) collective-permute-start(bf16[2,128,160]{2,1,0:T(8,128)(2,1)S(1)} %get-tuple-element.52), channel_id=1, source_target_pairs={{0,6},{2,4},{4,2},{6,0},{8,14},{10,12},{12,10},{14,8},{16,22},{18,... | collective-permute-start | bytes 245768 | tf_op jit(solution)/shard_map/ppermute | solution.py:501
  43.7 8.5 %collective-permute-start.6 = (bf16[64,2560]{1,0:T(8,128)(2,1)S(1)}, bf16[64,2560]{1,0:T(8,128)(2,1)S(1)}, u32[]{:S(2)}, u32[]{:S(2)}) collective-permute-start(bf16[64,2560]{1,0:T(8,128)(2,1)S(1)} %temporal_attention.1.refs_0_), channel_id=1, source_target_pairs={{1,0},{0,1},{3,2},{2,3},{5,4},{4,5},{7,6},{6,7},{9,8},{8,9},{11,10... | collective-permute-start | bytes 983048 | tf_op jit(solution)/shard_map/ppermute | solution.py:488
  52.2 2.8 %collective-permute-start.7 = (bf16[64,2560]{1,0:T(8,128)(2,1)S(1)}, bf16[64,2560]{1,0:T(8,128)(2,1)S(1)}, u32[]{:S(2)}, u32[]{:S(2)}) collective-permute-start(bf16[64,2560]{1,0:T(8,128)(2,1)S(1)} %collective-permute-done.6.refs_1_), channel_id=1, source_target_pairs={{0,2},{2,0},{4,6},{6,4},{8,10},{10,8},{12,14},{14,12},{16,18},{18,... | collective-permute-start | bytes 983048 | tf_op jit(solution)/shard_map/ppermute | solution.py:501
  53.8 9.3 %collective-permute-start.10 = (bf16[64,2560]{1,0:T(8,128)(2,1)S(1)}, bf16[64,2560]{1,0:T(8,128)(2,1)S(1)}, u32[]{:S(2)}, u32[]{:S(2)}) collective-permute-start(bf16[64,2560]{1,0:T(8,128)(2,1)S(1)} %temporal_attention.1.refs_0_), channel_id=1, source_target_pairs={{0,4},{2,6},{4,0},{6,2},{8,12},{10,14},{12,8},{14,10},{16,20},{18,... | collective-permute-start | bytes 983048 | tf_op jit(solution)/shard_map/ppermute | solution.py:501
  54.5 13.8 %collective-permute-start.9 = (bf16[64,2560]{1,0:T(8,128)(2,1)S(1)}, bf16[64,2560]{1,0:T(8,128)(2,1)}, u32[]{:S(2)}, u32[]{:S(2)}) collective-permute-start(bf16[64,2560]{1,0:T(8,128)(2,1)S(1)} %temporal_attention.1.refs_0_), channel_id=1, source_target_pairs={{0,2},{2,0},{4,6},{6,4},{8,10},{10,8},{12,14},{14,12},{16,18},{18,... | collective-permute-start | bytes 983048 | tf_op jit(solution)/shard_map/ppermute | solution.py:501
  63.2 5.1 %collective-permute-start.11 = (bf16[64,2560]{1,0:T(8,128)(2,1)S(1)}, bf16[64,2560]{1,0:T(8,128)(2,1)}, u32[]{:S(2)}, u32[]{:S(2)}) collective-permute-start(bf16[64,2560]{1,0:T(8,128)(2,1)S(1)} %collective-permute-done.10.refs_4_), channel_id=1, source_target_pairs={{0,2},{2,0},{4,6},{6,4},{8,10},{10,8},{12,14},{14,12},{16,18},{18,... | collective-permute-start | bytes 983048 | tf_op jit(solution)/shard_map/ppermute | solution.py:501
  64.0 10.7 %collective-permute-start.12 = (bf16[64,2560]{1,0:T(8,128)(2,1)S(1)}, bf16[64,2560]{1,0:T(8,128)(2,1)S(1)}, u32[]{:S(2)}, u32[]{:S(2)}) collective-permute-start(bf16[64,2560]{1,0:T(8,128)(2,1)S(1)} %collective-permute-done.6.refs_1_), channel_id=1, source_target_pairs={{0,4},{2,6},{4,0},{6,2},{8,12},{10,14},{12,8},{14,10},{16,20},{18,... | collective-permute-start | bytes 983048 | tf_op jit(solution)/shard_map/ppermute | solution.py:501
  64.6 14.3 %all-to-all-start.1 = ((bf16[16,16,640]{2,1,0:T(8,128)(2,1)}), bf16[16,16,640]{2,1,0:T(8,128)(2,1)S(1)}, u32[]{:S(2)}, u32[]{:S(2)}) async-start(bf16[16,16,640]{2,1,0:T(8,128)(2,1)} %get-tuple-element.58), calls=%async_computation.1 | async-start | bytes 655360 | tf_op jit(solution)/shard_map/all_to_all | solution.py:494
  74.6 2.4 %collective-permute-start.13 = (bf16[64,2560]{1,0:T(8,128)(2,1)S(1)}, bf16[64,2560]{1,0:T(8,128)(2,1)S(1)}, u32[]{:S(2)}, u32[]{:S(2)}) collective-permute-start(bf16[64,2560]{1,0:T(8,128)(2,1)S(1)} %collective-permute-done.12.refs_0_), channel_id=1, source_target_pairs={{0,2},{2,0},{4,6},{6,4},{8,10},{10,8},{12,14},{14,12},{16,18},{18,... | collective-permute-start | bytes 983048 | tf_op jit(solution)/shard_map/ppermute | solution.py:501
  78.3 5.0 %collective-permute-start.17 = (bf16[80,640]{1,0:T(8,128)(2,1)S(1)}, bf16[80,640]{1,0:T(8,128)(2,1)S(1)}, u32[]{:S(2)}, u32[]{:S(2)}) collective-permute-start(bf16[80,640]{1,0:T(8,128)(2,1)S(1)} %get-tuple-element.75), channel_id=1, source_target_pairs={{0,8},{2,10},{4,12},{6,14},{8,24},{10,26},{12,28},{14,30},{16,0},{... | collective-permute-start | bytes 307208 | tf_op jit(solution)/shard_map/ppermute | solution.py:501
  78.9 13.1 %collective-permute-start.8 = (bf16[16,16,640]{2,1,0:T(8,128)(2,1)S(1)}, bf16[16,16,640]{2,1,0:T(8,128)(2,1)S(1)}, u32[]{:S(2)}, u32[]{:S(2)}) collective-permute-start(bf16[16,16,640]{2,1,0:T(8,128)(2,1)S(1)} %all-to-all-done.1.refs_1_), channel_id=1, source_target_pairs={{1,0},{0,1},{3,2},{2,3},{5,4},{4,5},{7,6},{6,7},{9,8},{8,9},{11,10... | collective-permute-start | bytes 983048 | tf_op jit(solution)/shard_map/ppermute | solution.py:488
  79.8 6.0 %collective-permute-start.14 = (bf16[88,640]{1,0:T(8,128)(2,1)S(1)}, bf16[88,640]{1,0:T(8,128)(2,1)S(1)}, u32[]{:S(2)}, u32[]{:S(2)}) collective-permute-start(bf16[88,640]{1,0:T(8,128)(2,1)S(1)} %get-tuple-element.69), channel_id=1, source_target_pairs={{0,8},{2,10},{4,12},{6,14},{8,24},{10,26},{12,28},{14,30},{16,0},{... | collective-permute-start | bytes 337928 | tf_op jit(solution)/shard_map/ppermute | solution.py:501
  83.4 4.5 %collective-permute-start.18 = (bf16[80,640]{1,0:T(8,128)(2,1)S(1)}, bf16[80,640]{1,0:T(8,128)(2,1)S(1)}, u32[]{:S(2)}, u32[]{:S(2)}) collective-permute-start(bf16[80,640]{1,0:T(8,128)(2,1)S(1)} %add_convert_fusion.5), channel_id=1, source_target_pairs={{0,8},{2,10},{4,12},{6,14},{8,24},{10,26},{12,28},{14,30},{16,0},{... | collective-permute-start | bytes 307208 | tf_op jit(solution)/shard_map/ppermute | solution.py:501
  85.8 6.0 %collective-permute-start.15 = (bf16[88,640]{1,0:T(8,128)(2,1)S(1)}, bf16[88,640]{1,0:T(8,128)(2,1)S(1)}, u32[]{:S(2)}, u32[]{:S(2)}) collective-permute-start(bf16[88,640]{1,0:T(8,128)(2,1)S(1)} %add_convert_fusion.2), channel_id=1, source_target_pairs={{0,8},{2,10},{4,12},{6,14},{8,24},{10,26},{12,28},{14,30},{16,0},{... | collective-permute-start | bytes 337928 | tf_op jit(solution)/shard_map/ppermute | solution.py:501
  87.9 6.9 %collective-permute-start.19 = (bf16[80,640]{1,0:T(8,128)(2,1)S(1)}, bf16[80,640]{1,0:T(8,128)(2,1)S(1)}, u32[]{:S(2)}, u32[]{:S(2)}) collective-permute-start(bf16[80,640]{1,0:T(8,128)(2,1)S(1)} %add_convert_fusion.4), channel_id=1, source_target_pairs={{0,8},{2,10},{4,12},{6,14},{8,24},{10,26},{12,28},{14,30},{16,0},{... | collective-permute-start | bytes 307208 | tf_op jit(solution)/shard_map/ppermute | solution.py:501
  91.9 8.3 %collective-permute-start.16 = (bf16[88,640]{1,0:T(8,128)(2,1)S(1)}, bf16[88,640]{1,0:T(8,128)(2,1)S(1)}, u32[]{:S(2)}, u32[]{:S(2)}) collective-permute-start(bf16[88,640]{1,0:T(8,128)(2,1)S(1)} %add_convert_fusion.1), channel_id=1, source_target_pairs={{0,8},{2,10},{4,12},{6,14},{8,24},{10,26},{12,28},{14,30},{16,0},{... | collective-permute-start | bytes 337928 | tf_op jit(solution)/shard_map/ppermute | solution.py:501
  94.8 16.0 %collective-permute-start.21 = (bf16[80,640]{1,0:T(8,128)(2,1)S(1)}, bf16[80,640]{1,0:T(8,128)(2,1)S(1)}, u32[]{:S(2)}, u32[]{:S(2)}) collective-permute-start(bf16[80,640]{1,0:T(8,128)(2,1)S(1)} %add_convert_fusion.3), channel_id=1, source_target_pairs={{0,0},{1,16},{2,8},{3,24},{4,4},{5,20},{6,12},{7,28},{8,1},{9,17},... | collective-permute-start | bytes 307208 | tf_op jit(solution)/shard_map/ppermute | solution.py:624
  100.3 10.0 %collective-permute-start.20 = (bf16[88,640]{1,0:T(8,128)(2,1)S(1)}, bf16[88,640]{1,0:T(8,128)(2,1)S(1)}, u32[]{:S(2)}, u32[]{:S(2)}) collective-permute-start(bf16[88,640]{1,0:T(8,128)(2,1)S(1)} %add_convert_fusion), channel_id=1, source_target_pairs={{0,0},{1,16},{2,8},{3,24},{4,4},{5,20},{6,12},{7,28},{8,1},{9,17},... | collective-permute-start | bytes 337928 | tf_op jit(solution)/shard_map/ppermute | solution.py:624
  (16 other events, 168.7 us)

commit v8 on v7

--- a/solution.py
+++ b/solution.py
@@ -564,7 +564,7 @@
         back_kernel,
         "temporal_back_projection",
         [sds(nf, 2 * nq * fr, half), sds(3, half // 4, width)],
-        [geo, after(all_terms[0], core_terms[-1])] + all_terms[1:] + [motion_weights],
+        [geo] + all_terms + [motion_weights],
         0.01,
     )
     pair_terms[0] = after(pair_terms[0], back_send)

time: 112 us -> 104 us (0.929)
  waiting for transfers between devices: 35 us -> 25.5 us
  starting transfers between devices: 27.3 us -> 29.2 us
    ppermute x15, waiting for transfers between devices: 22.9 us -> 14 us  [move(): return lax.ppermute(x, 'frame', pairs)]
    ppermute x4, waiting for transfers between devices: 5.99 us -> 4.6 us  [from_quad(): return lax.ppermute(x, 'quad', [((d + s) % nq, d) for d in range(nq)])]
  transfers between devices with their start and end apart: 23 -> 23, of which waited for: 12 -> 11; matrix products, arithmetic and copies ran while one was open for 1% -> 1% of each run, Pallas kernels for 18% -> 19%
where the time goes in v8:
time: 104 us
  starting transfers between devices  29.2 us (28%)
  waiting for transfers between devices  25.5 us (25%)
  Pallas kernels  22.3 us (21%)
  blocking collectives  17.5 us (17%)
  local copies, waits for them, and re-layouts  6.71 us (6%)
  other arithmetic  1.87 us (2%)
    pallas_call x12, Pallas kernels, call(): pl.pallas_call(kernel, out_shape=outs, in_specs=in_specs, out_specs=[pl.B...  22.3 us
    all_to_all x1, blocking collectives, swap(): return lax.all_to_all(x, 'frame', split_axis=0, concat_axis=0, tiled=True)  17.5 us
    ppermute x15, waiting for transfers between devices, move(): return lax.ppermute(x, 'frame', pairs)  14 us
    ppermute x2, starting transfers between devices, local(): totals = [lax.ppermute(t, ('frame', 'quad'), final) for t in totals]  10.2 us
    ppermute x15, starting transfers between devices, move(): return lax.ppermute(x, 'frame', pairs)  9.88 us
    unnamed x34, local copies, waits for them, and re-layouts  6.7 us
    ppermute x4, waiting for transfers between devices, from_quad(): return lax.ppermute(x, 'quad', [((d + s) % nq, d) for d in range(nq)])  4.6 us
    ppermute x1, waiting for transfers between devices, to_quad(): return lax.ppermute(x, 'quad', [(d, (d + s) % nq) for d in range(nq)])  4.6 us
  transfers between devices with their start and end apart: 23, of which 11 were waited for; matrix products, arithmetic and copies ran while one was open for 1% of the time, Pallas kernels for 19%

profile of v8, /device:TPU:1, one launch (start us, length us, event | category | flops | bytes accessed | tf_op | source)
XLA Modules:
  0.0 104.1 jit_solution(6702224112449875089)
XLA Ops:
  0.6 2.1 %collective-permute-start = (bf16[4,16,1280]{2,1,0:T(8,128)(2,1)}, bf16[4,16,1280]{2,1,0:T(8,128)(2,1)S(1)}, u32[]{:S(2)}, u32[]{:S(2)}) collective-permute-start(bf16[4,16,1280]{2,1,0:T(8,128)(2,1)} %xs.1), channel_id=1, source_target_pairs={{1,0},{0,1},{3,2},{2,3},{5,4},{4,5},{7,6},{6,7},{9,8},{8,9},{11,10... | collective-permute-start | bytes 491528 | tf_op jit(solution)/shard_map/ppermute | solution.py:488
  3.1 2.9 %copy-done = bf16[4,1280,640]{2,1,0:T(8,128)(2,1)S(1)} copy-done((bf16[4,1280,640]{2,1,0:T(8,128)(2,1)S(1)}, bf16[4,1280,640]{2,1,0:T(8,128)(2,1)}, u32[]{:S(2)}) %copy-start) | copy-done | bytes 6553624
  8.0 1.7 %copy-done.1 = bf16[4,1280,640]{2,1,0:T(8,128)(2,1)S(1)} copy-done((bf16[4,1280,640]{2,1,0:T(8,128)(2,1)S(1)}, bf16[4,1280,640]{2,1,0:T(8,128)(2,1)}, u32[]{:S(2)}) %copy-start.1) | copy-done | bytes 6553624
  9.8 3.4 %spatial_forward.1 = (bf16[128,3200]{1,0:T(8,128)(2,1)S(1)}, bf16[16,8,640]{2,1,0:T(8,128)(2,1)S(1)}) custom-call(s32[3]{0:T(128)S(1)} %pad_add_fusion.refs_0_.geo.quad_ref, bf16[4,16,1280]{2,1,0:T(8,128)(2,1)S(1)} %copy-done.8, bf16[4,16,1280]{2,1,0:T(8,128)(2,1)S(1)} %collective-permute-done.refs_2_, f32[1280]{0:T(1024)S(1)} %copy-done.12, ...), custom_call_target="tpu_custom_call" | custom-call | flops 3000000000 | bytes 1048576 | tf_op jit(solution)/shard_map/spatial_forward/pallas_call | solution.py:441
  14.0 17.5 %all_to_all.10.received = bf16[16,16,640]{2,1,0:T(8,128)(2,1)S(1)} all-to-all(bf16[16,16,640]{2,1,0:T(8,128)(2,1)S(1)} %join_sent.1), channel_id=1, replica_groups=mesh['frame'=16,'quad'=2] {'frame'}, dimensions={0} | all-to-all | bytes 655360 | tf_op jit(solution)/shard_map/all_to_all | solution.py:494
  35.7 1.7 %collective-permute-start.5 = (bf16[2,128,160]{2,1,0:T(8,128)(2,1)S(1)}, bf16[2,128,160]{2,1,0:T(8,128)(2,1)S(1)}, u32[]{:S(2)}, u32[]{:S(2)}) collective-permute-start(bf16[2,128,160]{2,1,0:T(8,128)(2,1)S(1)} %get-tuple-element.51), channel_id=1, source_target_pairs={{0,6},{2,4},{4,2},{6,0},{8,14},{10,12},{12,10},{14,8},{16,22},{18,... | collective-permute-start | bytes 245768 | tf_op jit(solution)/shard_map/ppermute | solution.py:501
  37.4 4.6 %collective-permute-done.2.refs_1_ = bf16[64,2560]{1,0:T(8,128)(2,1)S(1)} collective-permute-done((bf16[64,2560]{1,0:T(8,128)(2,1)S(1)}, bf16[64,2560]{1,0:T(8,128)(2,1)S(1)}, u32[]{:S(2)}, u32[]{:S(2)}) %collective-permute-start.2) | collective-permute-done | bytes 327712 | tf_op jit(solution)/shard_map/ppermute | solution.py:491
  46.0 1.7 %positional_table_factors.1 = (f32[64,1280]{1,0:T(8,128)S(1)}, bf16[2,384,160]{2,1,0:T(8,128)(2,1)S(1)}, bf16[2,128,160]{2,1,0:T(8,128)(2,1)S(1)}) custom-call(s32[3]{0:T(128)S(1)} %pad_add_fusion.refs_0_.geo.quad_ref, bf16[2,128,160]{2,1,0:T(8,128)(2,1)S(1)} %get-tuple-element.46.refs_0_, bf16[2,128,160]{2,1,0:T(8,128)(2,1)S(1)} %collective-permute-done.3.refs_1_, ...), custom_call_target="tpu_custom_call" | custom-call | flops 1500000000 | bytes 1048576 | tf_op jit(solution)/shard_map/positional_table_factors/pallas_call | solution.py:441
  47.6 4.6 %collective-permute-done.6.refs_1_ = bf16[64,2560]{1,0:T(8,128)(2,1)S(1)} collective-permute-done((bf16[64,2560]{1,0:T(8,128)(2,1)S(1)}, bf16[64,2560]{1,0:T(8,128)(2,1)S(1)}, u32[]{:S(2)}, u32[]{:S(2)}) %collective-permute-start.6) | collective-permute-done | bytes 327712 | tf_op jit(solution)/shard_map/ppermute | solution.py:488
  52.2 2.5 %temporal_back_projection.1 = (bf16[16,16,640]{2,1,0:T(8,128)(2,1)}, bf16[3,160,640]{2,1,0:T(8,128)(2,1)S(1)}) custom-call(s32[3]{0:T(128)S(1)} %pad_add_fusion.refs_0_.geo.quad_ref, bf16[64,2560]{1,0:T(8,128)(2,1)S(1)} %temporal_attention.1.refs_0_, bf16[64,2560]{1,0:T(8,128)(2,1)S(1)} %collective-permute-done.6.refs_1_, bf16[4,640,640]{2,1,0:T(8,128)(2,1)S(1)} %copy-done.2), custom_call_target="tpu_custom_call" | custom-call | flops 10000000 | bytes 4096 | tf_op jit(solution)/shard_map/temporal_back_projection/pallas_call | solution.py:441
  54.8 1.6 %collective-permute-start.11 = (bf16[64,2560]{1,0:T(8,128)(2,1)S(1)}, bf16[64,2560]{1,0:T(8,128)(2,1)}, u32[]{:S(2)}, u32[]{:S(2)}) collective-permute-start(bf16[64,2560]{1,0:T(8,128)(2,1)S(1)} %collective-permute-done.10.refs_4_), channel_id=1, source_target_pairs={{0,2},{2,0},{4,6},{6,4},{8,10},{10,8},{12,14},{14,12},{16,18},{18,... | collective-permute-start | bytes 983048 | tf_op jit(solution)/shard_map/ppermute | solution.py:501
  57.0 4.1 %all-to-all-start.1 = ((bf16[16,16,640]{2,1,0:T(8,128)(2,1)}), bf16[16,16,640]{2,1,0:T(8,128)(2,1)S(1)}, u32[]{:S(2)}, u32[]{:S(2)}) async-start(bf16[16,16,640]{2,1,0:T(8,128)(2,1)} %get-tuple-element.56), calls=%async_computation.1 | async-start | bytes 655360 | tf_op jit(solution)/shard_map/all_to_all | solution.py:494
  61.2 2.3 %weight_terms_first_tokens.1 = (f32[4,4,40,640]{3,2,1,0:T(8,128)S(1)}, f32[1,160]{1,0:T(1,128)S(1)}) custom-call(s32[3]{0:T(128)S(1)} %pad_add_fusion.refs_0_.geo.quad_ref, bf16[2,384,160]{2,1,0:T(8,128)(2,1)S(1)} %get-tuple-element.60.left, bf16[3,160,640]{2,1,0:T(8,128)(2,1)S(1)} %get-tuple-element.61.weights, f32[64,1280]{1,0:T(8,128)S(1)} %get-tuple-element.54.pos, ...), custom_call_target="tpu_custom_call" | custom-call | flops 10000000 | bytes 4096 | tf_op jit(solution)/shard_map/weight_terms_first_tokens/pallas_call | solution.py:441
  63.5 2.0 %collective-permute-done.12.refs_0_ = bf16[64,2560]{1,0:T(8,128)(2,1)S(1)} collective-permute-done((bf16[64,2560]{1,0:T(8,128)(2,1)S(1)}, bf16[64,2560]{1,0:T(8,128)(2,1)S(1)}, u32[]{:S(2)}, u32[]{:S(2)}) %collective-permute-start.12) | collective-permute-done | bytes 327712 | tf_op jit(solution)/shard_map/ppermute | solution.py:501
  65.4 2.8 %collective-permute-start.13 = (bf16[64,2560]{1,0:T(8,128)(2,1)S(1)}, bf16[64,2560]{1,0:T(8,128)(2,1)S(1)}, u32[]{:S(2)}, u32[]{:S(2)}) collective-permute-start(bf16[64,2560]{1,0:T(8,128)(2,1)S(1)} %collective-permute-done.12.refs_0_), channel_id=1, source_target_pairs={{0,2},{2,0},{4,6},{6,4},{8,10},{10,8},{12,14},{14,12},{16,18},{18,... | collective-permute-start | bytes 983048 | tf_op jit(solution)/shard_map/ppermute | solution.py:501
  73.3 2.5 %collective-permute-done.17 = bf16[80,640]{1,0:T(8,128)(2,1)S(1)} collective-permute-done((bf16[80,640]{1,0:T(8,128)(2,1)S(1)}, bf16[80,640]{1,0:T(8,128)(2,1)S(1)}, u32[]{:S(2)}, u32[]{:S(2)}) %collective-permute-start.17) | collective-permute-done | bytes 102432 | tf_op jit(solution)/shard_map/ppermute | solution.py:501
  75.9 2.2 %collective-permute-done.14 = bf16[88,640]{1,0:T(8,128)(2,1)S(1)} collective-permute-done((bf16[88,640]{1,0:T(8,128)(2,1)S(1)}, bf16[88,640]{1,0:T(8,128)(2,1)S(1)}, u32[]{:S(2)}, u32[]{:S(2)}) %collective-permute-start.14) | collective-permute-done | bytes 112672 | tf_op jit(solution)/shard_map/ppermute | solution.py:501
  78.2 2.1 %collective-permute-done.18 = bf16[80,640]{1,0:T(8,128)(2,1)S(1)} collective-permute-done((bf16[80,640]{1,0:T(8,128)(2,1)S(1)}, bf16[80,640]{1,0:T(8,128)(2,1)S(1)}, u32[]{:S(2)}, u32[]{:S(2)}) %collective-permute-start.18) | collective-permute-done | bytes 102432 | tf_op jit(solution)/shard_map/ppermute | solution.py:501
  80.4 3.4 %collective-permute-done.15 = bf16[88,640]{1,0:T(8,128)(2,1)S(1)} collective-permute-done((bf16[88,640]{1,0:T(8,128)(2,1)S(1)}, bf16[88,640]{1,0:T(8,128)(2,1)S(1)}, u32[]{:S(2)}, u32[]{:S(2)}) %collective-permute-start.15) | collective-permute-done | bytes 112672 | tf_op jit(solution)/shard_map/ppermute | solution.py:501
  85.1 1.7 %block_output_hidden_gradient.1 = (bf16[4,16,1280]{2,1,0:T(8,128)(2,1)}, bf16[128,1280]{1,0:T(8,128)(2,1)S(1)}) custom-call(s32[3]{0:T(128)S(1)} %pad_add_fusion.refs_0_.geo.quad_ref, bf16[16,16,640]{2,1,0:T(8,128)(2,1)S(1)} %all-to-all-done.1.refs_1_, bf16[16,16,640]{2,1,0:T(8,128)(2,1)S(1)} %collective-permute-done.7.refs_2_, ...), custom_call_target="tpu_custom_call" | custom-call | flops 6000000000 | bytes 1048576 | tf_op jit(solution)/shard_map/block_output_hidden_gradient/pallas_call | solution.py:441
  86.8 5.8 %collective-permute-start.21 = (bf16[80,640]{1,0:T(8,128)(2,1)S(1)}, bf16[80,640]{1,0:T(8,128)(2,1)S(1)}, u32[]{:S(2)}, u32[]{:S(2)}) collective-permute-start(bf16[80,640]{1,0:T(8,128)(2,1)S(1)} %add_convert_fusion.3), channel_id=1, source_target_pairs={{0,0},{1,16},{2,8},{3,24},{4,4},{5,20},{6,12},{7,28},{8,1},{9,17},... | collective-permute-start | bytes 307208 | tf_op jit(solution)/shard_map/ppermute | solution.py:624
  92.7 4.4 %collective-permute-start.20 = (bf16[88,640]{1,0:T(8,128)(2,1)S(1)}, bf16[88,640]{1,0:T(8,128)(2,1)S(1)}, u32[]{:S(2)}, u32[]{:S(2)}) collective-permute-start(bf16[88,640]{1,0:T(8,128)(2,1)S(1)} %add_convert_fusion), channel_id=1, source_target_pairs={{0,0},{1,16},{2,8},{3,24},{4,4},{5,20},{6,12},{7,28},{8,1},{9,17},... | collective-permute-start | bytes 337928 | tf_op jit(solution)/shard_map/ppermute | solution.py:624
  97.1 4.1 %spatial_backward.1 = bf16[4,16,1280]{2,1,0:T(8,128)(2,1)} custom-call(bf16[128,1280]{1,0:T(8,128)(2,1)S(1)} %get-tuple-element.79.grad_hidden, bf16[4,16,1280]{2,1,0:T(8,128)(2,1)S(1)} %copy-done.9, bf16[128,3200]{1,0:T(8,128)(2,1)S(1)} %copy-done.14, f32[1280]{0:T(1024)S(1)} %copy-done.12, bf16[4,1280,640]{2,1,0:T(8,128)(2,1)S(1)} %bitcast.7), custom_call_target="tpu_custom_call" | custom-call | flops 3500000000 | bytes 1048576 | tf_op jit(solution)/shard_map/spatial_backward/pallas_call | solution.py:441
  101.2 1.5 %collective-permute-done.20 = bf16[88,640]{1,0:T(8,128)(2,1)S(1)} collective-permute-done((bf16[88,640]{1,0:T(8,128)(2,1)S(1)}, bf16[88,640]{1,0:T(8,128)(2,1)S(1)}, u32[]{:S(2)}, u32[]{:S(2)}) %collective-permute-start.20) | collective-permute-done | bytes 112672 | tf_op jit(solution)/shard_map/ppermute | solution.py:624
  (84 shorter events, 20.0 us)
Async XLA Ops:
  0.6 7.0 %collective-permute-start = (bf16[4,16,1280]{2,1,0:T(8,128)(2,1)}, bf16[4,16,1280]{2,1,0:T(8,128)(2,1)S(1)}, u32[]{:S(2)}, u32[]{:S(2)}) collective-permute-start(bf16[4,16,1280]{2,1,0:T(8,128)(2,1)} %xs.1), channel_id=1, source_target_pairs={{1,0},{0,1},{3,2},{2,3},{5,4},{4,5},{7,6},{6,7},{9,8},{8,9},{11,10... | collective-permute-start | bytes 491528 | tf_op jit(solution)/shard_map/ppermute | solution.py:488
  7.6 23.9 %copy-start.2 = (bf16[4,640,640]{2,1,0:T(8,128)(2,1)S(1)}, bf16[4,640,640]{2,1,0:T(8,128)(2,1)}, u32[]{:S(2)}) copy-start(bf16[4,640,640]{2,1,0:T(8,128)(2,1)} %refs_2_.1) | copy-start | bytes 9830404
  7.6 5.6 %collective-permute-start.1 = (bf16[4,16,1280]{2,1,0:T(8,128)(2,1)S(1)}, bf16[4,16,1280]{2,1,0:T(8,128)(2,1)S(1)}, u32[]{:S(2)}, u32[]{:S(2)}) collective-permute-start(bf16[4,16,1280]{2,1,0:T(8,128)(2,1)S(1)} %copy-done.3), channel_id=1, source_target_pairs={{1,0},{0,1},{3,2},{2,3},{5,4},{4,5},{7,6},{6,7},{9,8},{8,9},{11,10... | collective-permute-start | bytes 491528 | tf_op jit(solution)/shard_map/ppermute | solution.py:488
  33.0 9.0 %collective-permute-start.2 = (bf16[64,2560]{1,0:T(8,128)(2,1)S(1)}, bf16[64,2560]{1,0:T(8,128)(2,1)S(1)}, u32[]{:S(2)}, u32[]{:S(2)}) collective-permute-start(bf16[64,2560]{1,0:T(8,128)(2,1)S(1)} %get-tuple-element.48), channel_id=1, source_target_pairs={{0,1},{1,0},{2,3},{3,2},{4,5},{5,4},{6,7},{7,6},{8,9},{9,8},{10,11... | collective-permute-start | bytes 983048 | tf_op jit(solution)/shard_map/ppermute | solution.py:491
  34.9 8.1 %collective-permute-start.3 = (bf16[2,128,160]{2,1,0:T(8,128)(2,1)S(1)}, bf16[2,128,160]{2,1,0:T(8,128)(2,1)S(1)}, u32[]{:S(2)}, u32[]{:S(2)}) collective-permute-start(bf16[2,128,160]{2,1,0:T(8,128)(2,1)S(1)} %get-tuple-element.49), channel_id=1, source_target_pairs={{0,2},{2,0},{4,6},{6,4},{8,10},{10,8},{12,14},{14,12},{16,18},{18,... | collective-permute-start | bytes 245768 | tf_op jit(solution)/shard_map/ppermute | solution.py:501
  35.7 7.4 %collective-permute-start.4 = (bf16[2,128,160]{2,1,0:T(8,128)(2,1)S(1)}, bf16[2,128,160]{2,1,0:T(8,128)(2,1)S(1)}, u32[]{:S(2)}, u32[]{:S(2)}) collective-permute-start(bf16[2,128,160]{2,1,0:T(8,128)(2,1)S(1)} %get-tuple-element.50), channel_id=1, source_target_pairs={{0,4},{2,6},{4,0},{6,2},{8,12},{10,14},{12,8},{14,10},{16,20},{18,... | collective-permute-start | bytes 245768 | tf_op jit(solution)/shard_map/ppermute | solution.py:501
  35.7 8.0 %collective-permute-start.5 = (bf16[2,128,160]{2,1,0:T(8,128)(2,1)S(1)}, bf16[2,128,160]{2,1,0:T(8,128)(2,1)S(1)}, u32[]{:S(2)}, u32[]{:S(2)}) collective-permute-start(bf16[2,128,160]{2,1,0:T(8,128)(2,1)S(1)} %get-tuple-element.51), channel_id=1, source_target_pairs={{0,6},{2,4},{4,2},{6,0},{8,14},{10,12},{12,10},{14,8},{16,22},{18,... | collective-permute-start | bytes 245768 | tf_op jit(solution)/shard_map/ppermute | solution.py:501
  43.7 8.5 %collective-permute-start.6 = (bf16[64,2560]{1,0:T(8,128)(2,1)S(1)}, bf16[64,2560]{1,0:T(8,128)(2,1)S(1)}, u32[]{:S(2)}, u32[]{:S(2)}) collective-permute-start(bf16[64,2560]{1,0:T(8,128)(2,1)S(1)} %temporal_attention.1.refs_0_), channel_id=1, source_target_pairs={{1,0},{0,1},{3,2},{2,3},{5,4},{4,5},{7,6},{6,7},{9,8},{8,9},{11,10... | collective-permute-start | bytes 983048 | tf_op jit(solution)/shard_map/ppermute | solution.py:488
  44.6 10.2 %collective-permute-start.10 = (bf16[64,2560]{1,0:T(8,128)(2,1)S(1)}, bf16[64,2560]{1,0:T(8,128)(2,1)S(1)}, u32[]{:S(2)}, u32[]{:S(2)}) collective-permute-start(bf16[64,2560]{1,0:T(8,128)(2,1)S(1)} %temporal_attention.1.refs_0_), channel_id=1, source_target_pairs={{0,4},{2,6},{4,0},{6,2},{8,12},{10,14},{12,8},{14,10},{16,20},{18,... | collective-permute-start | bytes 983048 | tf_op jit(solution)/shard_map/ppermute | solution.py:501
  44.9 16.2 %collective-permute-start.8 = (bf16[64,2560]{1,0:T(8,128)(2,1)S(1)}, bf16[64,2560]{1,0:T(8,128)(2,1)S(1)}, u32[]{:S(2)}, u32[]{:S(2)}) collective-permute-start(bf16[64,2560]{1,0:T(8,128)(2,1)S(1)} %temporal_attention.1.refs_0_), channel_id=1, source_target_pairs={{0,2},{2,0},{4,6},{6,4},{8,10},{10,8},{12,14},{14,12},{16,18},{18,... | collective-permute-start | bytes 983048 | tf_op jit(solution)/shard_map/ppermute | solution.py:501
  54.8 6.4 %collective-permute-start.11 = (bf16[64,2560]{1,0:T(8,128)(2,1)S(1)}, bf16[64,2560]{1,0:T(8,128)(2,1)}, u32[]{:S(2)}, u32[]{:S(2)}) collective-permute-start(bf16[64,2560]{1,0:T(8,128)(2,1)S(1)} %collective-permute-done.10.refs_4_), channel_id=1, source_target_pairs={{0,2},{2,0},{4,6},{6,4},{8,10},{10,8},{12,14},{14,12},{16,18},{18,... | collective-permute-start | bytes 983048 | tf_op jit(solution)/shard_map/ppermute | solution.py:501
  56.3 4.8 %collective-permute-start.9 = (bf16[64,2560]{1,0:T(8,128)(2,1)S(1)}, bf16[64,2560]{1,0:T(8,128)(2,1)}, u32[]{:S(2)}, u32[]{:S(2)}) collective-permute-start(bf16[64,2560]{1,0:T(8,128)(2,1)S(1)} %collective-permute-done.6.refs_1_), channel_id=1, source_target_pairs={{0,2},{2,0},{4,6},{6,4},{8,10},{10,8},{12,14},{14,12},{16,18},{18,... | collective-permute-start | bytes 983048 | tf_op jit(solution)/shard_map/ppermute | solution.py:501
  56.3 9.1 %collective-permute-start.12 = (bf16[64,2560]{1,0:T(8,128)(2,1)S(1)}, bf16[64,2560]{1,0:T(8,128)(2,1)S(1)}, u32[]{:S(2)}, u32[]{:S(2)}) collective-permute-start(bf16[64,2560]{1,0:T(8,128)(2,1)S(1)} %collective-permute-done.6.refs_1_), channel_id=1, source_target_pairs={{0,4},{2,6},{4,0},{6,2},{8,12},{10,14},{12,8},{14,10},{16,20},{18,... | collective-permute-start | bytes 983048 | tf_op jit(solution)/shard_map/ppermute | solution.py:501
  57.0 14.8 %all-to-all-start.1 = ((bf16[16,16,640]{2,1,0:T(8,128)(2,1)}), bf16[16,16,640]{2,1,0:T(8,128)(2,1)S(1)}, u32[]{:S(2)}, u32[]{:S(2)}) async-start(bf16[16,16,640]{2,1,0:T(8,128)(2,1)} %get-tuple-element.56), calls=%async_computation.1 | async-start | bytes 655360 | tf_op jit(solution)/shard_map/all_to_all | solution.py:494
  65.4 4.1 %collective-permute-start.13 = (bf16[64,2560]{1,0:T(8,128)(2,1)S(1)}, bf16[64,2560]{1,0:T(8,128)(2,1)S(1)}, u32[]{:S(2)}, u32[]{:S(2)}) collective-permute-start(bf16[64,2560]{1,0:T(8,128)(2,1)S(1)} %collective-permute-done.12.refs_0_), channel_id=1, source_target_pairs={{0,2},{2,0},{4,6},{6,4},{8,10},{10,8},{12,14},{14,12},{16,18},{18,... | collective-permute-start | bytes 983048 | tf_op jit(solution)/shard_map/ppermute | solution.py:501
  70.8 5.0 %collective-permute-start.17 = (bf16[80,640]{1,0:T(8,128)(2,1)S(1)}, bf16[80,640]{1,0:T(8,128)(2,1)S(1)}, u32[]{:S(2)}, u32[]{:S(2)}) collective-permute-start(bf16[80,640]{1,0:T(8,128)(2,1)S(1)} %get-tuple-element.73), channel_id=1, source_target_pairs={{0,8},{2,10},{4,12},{6,14},{8,24},{10,26},{12,28},{14,30},{16,0},{... | collective-permute-start | bytes 307208 | tf_op jit(solution)/shard_map/ppermute | solution.py:501
  71.8 12.1 %collective-permute-start.7 = (bf16[16,16,640]{2,1,0:T(8,128)(2,1)S(1)}, bf16[16,16,640]{2,1,0:T(8,128)(2,1)S(1)}, u32[]{:S(2)}, u32[]{:S(2)}) collective-permute-start(bf16[16,16,640]{2,1,0:T(8,128)(2,1)S(1)} %all-to-all-done.1.refs_1_), channel_id=1, source_target_pairs={{1,0},{0,1},{3,2},{2,3},{5,4},{4,5},{7,6},{6,7},{9,8},{8,9},{11,10... | collective-permute-start | bytes 983048 | tf_op jit(solution)/shard_map/ppermute | solution.py:488
  72.7 5.4 %collective-permute-start.14 = (bf16[88,640]{1,0:T(8,128)(2,1)S(1)}, bf16[88,640]{1,0:T(8,128)(2,1)S(1)}, u32[]{:S(2)}, u32[]{:S(2)}) collective-permute-start(bf16[88,640]{1,0:T(8,128)(2,1)S(1)} %get-tuple-element.67), channel_id=1, source_target_pairs={{0,8},{2,10},{4,12},{6,14},{8,24},{10,26},{12,28},{14,30},{16,0},{... | collective-permute-start | bytes 337928 | tf_op jit(solution)/shard_map/ppermute | solution.py:501
  75.8 4.5 %collective-permute-start.18 = (bf16[80,640]{1,0:T(8,128)(2,1)S(1)}, bf16[80,640]{1,0:T(8,128)(2,1)S(1)}, u32[]{:S(2)}, u32[]{:S(2)}) collective-permute-start(bf16[80,640]{1,0:T(8,128)(2,1)S(1)} %add_convert_fusion.5), channel_id=1, source_target_pairs={{0,8},{2,10},{4,12},{6,14},{8,24},{10,26},{12,28},{14,30},{16,0},{... | collective-permute-start | bytes 307208 | tf_op jit(solution)/shard_map/ppermute | solution.py:501
  78.2 5.6 %collective-permute-start.15 = (bf16[88,640]{1,0:T(8,128)(2,1)S(1)}, bf16[88,640]{1,0:T(8,128)(2,1)S(1)}, u32[]{:S(2)}, u32[]{:S(2)}) collective-permute-start(bf16[88,640]{1,0:T(8,128)(2,1)S(1)} %add_convert_fusion.2), channel_id=1, source_target_pairs={{0,8},{2,10},{4,12},{6,14},{8,24},{10,26},{12,28},{14,30},{16,0},{... | collective-permute-start | bytes 337928 | tf_op jit(solution)/shard_map/ppermute | solution.py:501
  80.3 6.4 %collective-permute-start.19 = (bf16[80,640]{1,0:T(8,128)(2,1)S(1)}, bf16[80,640]{1,0:T(8,128)(2,1)S(1)}, u32[]{:S(2)}, u32[]{:S(2)}) collective-permute-start(bf16[80,640]{1,0:T(8,128)(2,1)S(1)} %add_convert_fusion.4), channel_id=1, source_target_pairs={{0,8},{2,10},{4,12},{6,14},{8,24},{10,26},{12,28},{14,30},{16,0},{... | collective-permute-start | bytes 307208 | tf_op jit(solution)/shard_map/ppermute | solution.py:501
  83.8 8.8 %collective-permute-start.16 = (bf16[88,640]{1,0:T(8,128)(2,1)S(1)}, bf16[88,640]{1,0:T(8,128)(2,1)S(1)}, u32[]{:S(2)}, u32[]{:S(2)}) collective-permute-start(bf16[88,640]{1,0:T(8,128)(2,1)S(1)} %add_convert_fusion.1), channel_id=1, source_target_pairs={{0,8},{2,10},{4,12},{6,14},{8,24},{10,26},{12,28},{14,30},{16,0},{... | collective-permute-start | bytes 337928 | tf_op jit(solution)/shard_map/ppermute | solution.py:501
  86.8 16.5 %collective-permute-start.21 = (bf16[80,640]{1,0:T(8,128)(2,1)S(1)}, bf16[80,640]{1,0:T(8,128)(2,1)S(1)}, u32[]{:S(2)}, u32[]{:S(2)}) collective-permute-start(bf16[80,640]{1,0:T(8,128)(2,1)S(1)} %add_convert_fusion.3), channel_id=1, source_target_pairs={{0,0},{1,16},{2,8},{3,24},{4,4},{5,20},{6,12},{7,28},{8,1},{9,17},... | collective-permute-start | bytes 307208 | tf_op jit(solution)/shard_map/ppermute | solution.py:624
  92.7 10.0 %collective-permute-start.20 = (bf16[88,640]{1,0:T(8,128)(2,1)S(1)}, bf16[88,640]{1,0:T(8,128)(2,1)S(1)}, u32[]{:S(2)}, u32[]{:S(2)}) collective-permute-start(bf16[88,640]{1,0:T(8,128)(2,1)S(1)} %add_convert_fusion), channel_id=1, source_target_pairs={{0,0},{1,16},{2,8},{3,24},{4,4},{5,20},{6,12},{7,28},{8,1},{9,17},... | collective-permute-start | bytes 337928 | tf_op jit(solution)/shard_map/ppermute | solution.py:624
  (16 other events, 159.9 us)

commit v9 on v8

--- a/solution.py
+++ b/solution.py
@@ -388,9 +388,9 @@
     extra = jnp.where(iota((8, width), 0) == 0, extra, 0.0)
     for r in range(stage):
         z = gray((place_of(geo[2], stage) + r) & (stage - 1))
-        rows_out = jnp.concatenate([blocks[0, z], blocks[1, z], extra], axis=0)
+        rows_out = jnp.concatenate([blocks[0, z], blocks[1, z]], axis=0)
         outs[r][...] = rows_out.astype(BF16)
-        rows_out = jnp.concatenate([blocks[2, z], blocks[3, z]], axis=0)
+        rows_out = jnp.concatenate([blocks[2, z], blocks[3, z], extra], axis=0)
         outs[stage + r][...] = rows_out.astype(BF16)
 
 
@@ -564,10 +564,9 @@
         back_kernel,
         "temporal_back_projection",
         [sds(nf, 2 * nq * fr, half), sds(3, half // 4, width)],
-        [geo] + all_terms + [motion_weights],
+        [geo, after(all_terms[0], pair_terms[0])] + all_terms[1:] + [motion_weights],
         0.01,
     )
-    pair_terms[0] = after(pair_terms[0], back_send)
     last_terms = [move(pair_terms[0], flipped(1))]
 
     stage, block = nf // 4, half // nf
@@ -587,7 +586,7 @@
     parts_w = run(
         second_weight_kernel,
         "weight_terms_last_tokens",
-        [sds(2 * block + 8, width)] * stage + [sds(2 * block, width)] * stage,
+        [sds(2 * block, width)] * stage + [sds(2 * block + 8, width)] * stage,
         [geo, sums, gain_sum, late_left, quarter, table, gain2] + late_terms,
         0.01,
         scratch=[pltpu.VMEM((4, stage, block, width), F32)],
@@ -632,10 +631,10 @@
     )
     everyone = nf * nq
     factor = 1.0 / math.sqrt(everyone * fr * pq)
-    weight_grad = jnp.concatenate([totals[0][: 2 * block], totals[1]], axis=0)
+    weight_grad = jnp.concatenate([totals[0], totals[1][: 2 * block]], axis=0)
     weight_grad = weight_grad.reshape(4, block, width).astype(F32) * factor
     place = ((frame * nq + quad) % stage) * block
-    gain_grad = lax.dynamic_slice(totals[0][2 * block], (place,), (block,)).astype(F32) * factor
+    gain_grad = lax.dynamic_slice(totals[1][2 * block], (place,), (block,)).astype(F32) * factor
     return block_output, input_grad, weight_grad, gain_grad
 
 

time: 104 us -> 105 us (level)
  starting transfers between devices: 29.2 us -> 31.6 us
  waiting for transfers between devices: 25.5 us -> 23.6 us
    ppermute x15, waiting for transfers between devices: 14 us -> 6.89 us  [move(): return lax.ppermute(x, 'frame', pairs)]
    ppermute x15, starting transfers between devices: 9.88 us -> 13.4 us  [move(): return lax.ppermute(x, 'frame', pairs)]
    all_to_all x1, waiting for transfers between devices: 0.83 us -> 4.04 us  [swap(): return lax.all_to_all(x, 'frame', split_axis=0, concat_axis=0, tiled=True)]
    ppermute x2, waiting for transfers between devices: 1.47 us -> 3.44 us  [local(): totals = [lax.ppermute(t, ('frame', 'quad'), final) for t in totals]]
where the time goes in v9:
time: 105 us
  starting transfers between devices  31.6 us (30%)
  waiting for transfers between devices  23.6 us (22%)
  Pallas kernels  22.3 us (21%)
  blocking collectives  17.5 us (17%)
  local copies, waits for them, and re-layouts  6.71 us (6%)
  other arithmetic  1.87 us (2%)
    pallas_call x12, Pallas kernels, call(): pl.pallas_call(kernel, out_shape=outs, in_specs=in_specs, out_specs=[pl.B...  22.3 us
    all_to_all x1, blocking collectives, swap(): return lax.all_to_all(x, 'frame', split_axis=0, concat_axis=0, tiled=True)  17.5 us
    ppermute x15, starting transfers between devices, move(): return lax.ppermute(x, 'frame', pairs)  13.4 us
    ppermute x2, starting transfers between devices, local(): totals = [lax.ppermute(t, ('frame', 'quad'), final) for t in totals]  9.83 us
    ppermute x15, waiting for transfers between devices, move(): return lax.ppermute(x, 'frame', pairs)  6.89 us
    unnamed x34, local copies, waits for them, and re-layouts  6.7 us
    ppermute x4, waiting for transfers between devices, from_quad(): return lax.ppermute(x, 'quad', [((d + s) % nq, d) for d in range(nq)])  4.6 us
    ppermute x1, waiting for transfers between devices, to_quad(): return lax.ppermute(x, 'quad', [(d, (d + s) % nq) for d in range(nq)])  4.6 us
  transfers between devices with their start and end apart: 23, of which 11 were waited for; matrix products, arithmetic and copies ran while one was open for 1% of the time, Pallas kernels for 19%

profile of v9, /device:TPU:1, one launch (start us, length us, event | category | flops | bytes accessed | tf_op | source)
XLA Modules:
  0.0 104.5 jit_solution(12166723458033114880)
XLA Ops:
  0.6 2.1 %collective-permute-start = (bf16[4,16,1280]{2,1,0:T(8,128)(2,1)}, bf16[4,16,1280]{2,1,0:T(8,128)(2,1)S(1)}, u32[]{:S(2)}, u32[]{:S(2)}) collective-permute-start(bf16[4,16,1280]{2,1,0:T(8,128)(2,1)} %xs.1), channel_id=1, source_target_pairs={{1,0},{0,1},{3,2},{2,3},{5,4},{4,5},{7,6},{6,7},{9,8},{8,9},{11,10... | collective-permute-start | bytes 491528 | tf_op jit(solution)/shard_map/ppermute | solution.py:488
  3.1 2.9 %copy-done = bf16[4,1280,640]{2,1,0:T(8,128)(2,1)S(1)} copy-done((bf16[4,1280,640]{2,1,0:T(8,128)(2,1)S(1)}, bf16[4,1280,640]{2,1,0:T(8,128)(2,1)}, u32[]{:S(2)}) %copy-start) | copy-done | bytes 6553624
  8.0 1.7 %copy-done.1 = bf16[4,1280,640]{2,1,0:T(8,128)(2,1)S(1)} copy-done((bf16[4,1280,640]{2,1,0:T(8,128)(2,1)S(1)}, bf16[4,1280,640]{2,1,0:T(8,128)(2,1)}, u32[]{:S(2)}) %copy-start.1) | copy-done | bytes 6553624
  9.8 3.4 %spatial_forward.1 = (bf16[128,3200]{1,0:T(8,128)(2,1)S(1)}, bf16[16,8,640]{2,1,0:T(8,128)(2,1)S(1)}) custom-call(s32[3]{0:T(128)S(1)} %pad_add_fusion.refs_0_.geo.quad_ref, bf16[4,16,1280]{2,1,0:T(8,128)(2,1)S(1)} %copy-done.8, bf16[4,16,1280]{2,1,0:T(8,128)(2,1)S(1)} %collective-permute-done.refs_2_, f32[1280]{0:T(1024)S(1)} %copy-done.12, ...), custom_call_target="tpu_custom_call" | custom-call | flops 3000000000 | bytes 1048576 | tf_op jit(solution)/shard_map/spatial_forward/pallas_call | solution.py:441
  14.0 17.5 %all_to_all.10.received = bf16[16,16,640]{2,1,0:T(8,128)(2,1)S(1)} all-to-all(bf16[16,16,640]{2,1,0:T(8,128)(2,1)S(1)} %join_sent.1), channel_id=1, replica_groups=mesh['frame'=16,'quad'=2] {'frame'}, dimensions={0} | all-to-all | bytes 655360 | tf_op jit(solution)/shard_map/all_to_all | solution.py:494
  31.5 1.5 %motion_projection.1 = (f32[64,2560]{1,0:T(8,128)S(1)}, bf16[64,2560]{1,0:T(8,128)(2,1)S(1)}) custom-call(s32[3]{0:T(128)S(1)} %pad_add_fusion.refs_0_.geo.quad_ref, bf16[16,16,640]{2,1,0:T(8,128)(2,1)S(1)} %all_to_all.10.received, bf16[4,640,640]{2,1,0:T(8,128)(2,1)S(1)} %copy-done.2), custom_call_target="tpu_custom_call" | custom-call | flops 1500000000 | bytes 1048576 | tf_op jit(solution)/shard_map/motion_projection/pallas_call | solution.py:441
  33.7 1.3 %cut_factors.1 = (bf16[2,128,160]{2,1,0:T(8,128)(2,1)S(1)}, bf16[2,128,160]{2,1,0:T(8,128)(2,1)S(1)}, bf16[2,128,160]{2,1,0:T(8,128)(2,1)S(1)}, bf16[2,128,160]{2,1,0:T(8,128)(2,1)S(1)}) custom-call(s32[3]{0:T(128)S(1)} %pad_add_fusion.refs_0_.geo.quad_ref, bf16[16,16,640]{2,1,0:T(8,128)(2,1)S(1)} %all_to_all.10.received), custom_call_target="tpu_custom_call" | custom-call | flops 500000000 | bytes 1048576 | tf_op jit(solution)/shard_map/cut_factors/pallas_call | solution.py:441
  35.7 1.7 %collective-permute-start.5 = (bf16[2,128,160]{2,1,0:T(8,128)(2,1)S(1)}, bf16[2,128,160]{2,1,0:T(8,128)(2,1)S(1)}, u32[]{:S(2)}, u32[]{:S(2)}) collective-permute-start(bf16[2,128,160]{2,1,0:T(8,128)(2,1)S(1)} %get-tuple-element.51), channel_id=1, source_target_pairs={{0,6},{2,4},{4,2},{6,0},{8,14},{10,12},{12,10},{14,8},{16,22},{18,... | collective-permute-start | bytes 245768 | tf_op jit(solution)/shard_map/ppermute | solution.py:501
  37.4 4.6 %collective-permute-done.2.refs_1_ = bf16[64,2560]{1,0:T(8,128)(2,1)S(1)} collective-permute-done((bf16[64,2560]{1,0:T(8,128)(2,1)S(1)}, bf16[64,2560]{1,0:T(8,128)(2,1)S(1)}, u32[]{:S(2)}, u32[]{:S(2)}) %collective-permute-start.2) | collective-permute-done | bytes 327712 | tf_op jit(solution)/shard_map/ppermute | solution.py:491
  46.0 1.7 %positional_table_factors.1 = (f32[64,1280]{1,0:T(8,128)S(1)}, bf16[2,384,160]{2,1,0:T(8,128)(2,1)S(1)}, bf16[2,128,160]{2,1,0:T(8,128)(2,1)S(1)}) custom-call(s32[3]{0:T(128)S(1)} %pad_add_fusion.refs_0_.geo.quad_ref, bf16[2,128,160]{2,1,0:T(8,128)(2,1)S(1)} %get-tuple-element.46.refs_0_, bf16[2,128,160]{2,1,0:T(8,128)(2,1)S(1)} %collective-permute-done.3.refs_1_, ...), custom_call_target="tpu_custom_call" | custom-call | flops 1500000000 | bytes 1048576 | tf_op jit(solution)/shard_map/positional_table_factors/pallas_call | solution.py:441
  47.6 4.6 %collective-permute-done.7.refs_1_ = bf16[64,2560]{1,0:T(8,128)(2,1)S(1)} collective-permute-done((bf16[64,2560]{1,0:T(8,128)(2,1)S(1)}, bf16[64,2560]{1,0:T(8,128)(2,1)S(1)}, u32[]{:S(2)}, u32[]{:S(2)}) %collective-permute-start.7) | collective-permute-done | bytes 327712 | tf_op jit(solution)/shard_map/ppermute | solution.py:488
  52.2 1.6 %collective-permute-start.10 = (bf16[64,2560]{1,0:T(8,128)(2,1)S(1)}, bf16[64,2560]{1,0:T(8,128)(2,1)}, u32[]{:S(2)}, u32[]{:S(2)}) collective-permute-start(bf16[64,2560]{1,0:T(8,128)(2,1)S(1)} %collective-permute-done.7.refs_1_), channel_id=1, source_target_pairs={{0,2},{2,0},{4,6},{6,4},{8,10},{10,8},{12,14},{14,12},{16,18},{18,... | collective-permute-start | bytes 983048 | tf_op jit(solution)/shard_map/ppermute | solution.py:501
  55.1 2.5 %temporal_back_projection.1 = (bf16[16,16,640]{2,1,0:T(8,128)(2,1)}, bf16[3,160,640]{2,1,0:T(8,128)(2,1)S(1)}) custom-call(s32[3]{0:T(128)S(1)} %pad_add_fusion.refs_0_.geo.quad_ref, bf16[64,2560]{1,0:T(8,128)(2,1)S(1)} %temporal_attention.1.refs_0_, bf16[64,2560]{1,0:T(8,128)(2,1)S(1)} %collective-permute-done.7.refs_1_, bf16[4,640,640]{2,1,0:T(8,128)(2,1)S(1)} %copy-done.2), custom_call_target="tpu_custom_call" | custom-call | flops 10000000 | bytes 4096 | tf_op jit(solution)/shard_map/temporal_back_projection/pallas_call | solution.py:441
  57.6 3.8 %all-to-all-start.1 = ((bf16[16,16,640]{2,1,0:T(8,128)(2,1)}), bf16[16,16,640]{2,1,0:T(8,128)(2,1)S(1)}, u32[]{:S(2)}, u32[]{:S(2)}) async-start(bf16[16,16,640]{2,1,0:T(8,128)(2,1)} %get-tuple-element.57), calls=%async_computation.1 | async-start | bytes 655360 | tf_op jit(solution)/shard_map/all_to_all | solution.py:494
  61.5 2.3 %weight_terms_first_tokens.1 = (f32[4,4,40,640]{3,2,1,0:T(8,128)S(1)}, f32[1,160]{1,0:T(1,128)S(1)}) custom-call(s32[3]{0:T(128)S(1)} %pad_add_fusion.refs_0_.geo.quad_ref, bf16[2,384,160]{2,1,0:T(8,128)(2,1)S(1)} %get-tuple-element.61.left, bf16[3,160,640]{2,1,0:T(8,128)(2,1)S(1)} %get-tuple-element.62.weights, f32[64,1280]{1,0:T(8,128)S(1)} %get-tuple-element.55.pos, ...), custom_call_target="tpu_custom_call" | custom-call | flops 10000000 | bytes 4096 | tf_op jit(solution)/shard_map/weight_terms_first_tokens/pallas_call | solution.py:441
  68.2 4.0 %all-to-all-done.1.refs_1_ = bf16[16,16,640]{2,1,0:T(8,128)(2,1)S(1)} async-done(((bf16[16,16,640]{2,1,0:T(8,128)(2,1)}), bf16[16,16,640]{2,1,0:T(8,128)(2,1)S(1)}, u32[]{:S(2)}, u32[]{:S(2)}) %all-to-all-start.1) | async-done | bytes 327712 | tf_op jit(solution)/shard_map/all_to_all | solution.py:494
  74.4 2.8 %collective-permute-done.17 = bf16[88,640]{1,0:T(8,128)(2,1)S(1)} collective-permute-done((bf16[88,640]{1,0:T(8,128)(2,1)S(1)}, bf16[88,640]{1,0:T(8,128)(2,1)S(1)}, u32[]{:S(2)}, u32[]{:S(2)}) %collective-permute-start.17) | collective-permute-done | bytes 112672 | tf_op jit(solution)/shard_map/ppermute | solution.py:501
  77.3 1.5 %collective-permute-start.18 = (bf16[88,640]{1,0:T(8,128)(2,1)S(1)}, bf16[88,640]{1,0:T(8,128)(2,1)S(1)}, u32[]{:S(2)}, u32[]{:S(2)}) collective-permute-start(bf16[88,640]{1,0:T(8,128)(2,1)S(1)} %add_convert_fusion.2), channel_id=1, source_target_pairs={{0,8},{2,10},{4,12},{6,14},{8,24},{10,26},{12,28},{14,30},{16,0},{... | collective-permute-start | bytes 337928 | tf_op jit(solution)/shard_map/ppermute | solution.py:501
  79.7 1.3 %collective-permute-start.16 = (bf16[80,640]{1,0:T(8,128)(2,1)S(1)}, bf16[80,640]{1,0:T(8,128)(2,1)S(1)}, u32[]{:S(2)}, u32[]{:S(2)}) collective-permute-start(bf16[80,640]{1,0:T(8,128)(2,1)S(1)} %add_convert_fusion.4), channel_id=1, source_target_pairs={{0,8},{2,10},{4,12},{6,14},{8,24},{10,26},{12,28},{14,30},{16,0},{... | collective-permute-start | bytes 307208 | tf_op jit(solution)/shard_map/ppermute | solution.py:501
  83.9 1.7 %block_output_hidden_gradient.1 = (bf16[4,16,1280]{2,1,0:T(8,128)(2,1)}, bf16[128,1280]{1,0:T(8,128)(2,1)S(1)}) custom-call(s32[3]{0:T(128)S(1)} %pad_add_fusion.refs_0_.geo.quad_ref, bf16[16,16,640]{2,1,0:T(8,128)(2,1)S(1)} %all-to-all-done.1.refs_1_, bf16[16,16,640]{2,1,0:T(8,128)(2,1)S(1)} %collective-permute-done.8.refs_2_, ...), custom_call_target="tpu_custom_call" | custom-call | flops 6000000000 | bytes 1048576 | tf_op jit(solution)/shard_map/block_output_hidden_gradient/pallas_call | solution.py:441
  85.6 7.8 %collective-permute-start.20 = (bf16[80,640]{1,0:T(8,128)(2,1)S(1)}, bf16[80,640]{1,0:T(8,128)(2,1)S(1)}, u32[]{:S(2)}, u32[]{:S(2)}) collective-permute-start(bf16[80,640]{1,0:T(8,128)(2,1)S(1)} %add_convert_fusion.3), channel_id=1, source_target_pairs={{0,0},{1,16},{2,8},{3,24},{4,4},{5,20},{6,12},{7,28},{8,1},{9,17},... | collective-permute-start | bytes 307208 | tf_op jit(solution)/shard_map/ppermute | solution.py:623
  93.4 2.1 %collective-permute-start.21 = (bf16[88,640]{1,0:T(8,128)(2,1)S(1)}, bf16[88,640]{1,0:T(8,128)(2,1)S(1)}, u32[]{:S(2)}, u32[]{:S(2)}) collective-permute-start(bf16[88,640]{1,0:T(8,128)(2,1)S(1)} %add_convert_fusion), channel_id=1, source_target_pairs={{0,0},{1,16},{2,8},{3,24},{4,4},{5,20},{6,12},{7,28},{8,1},{9,17},... | collective-permute-start | bytes 337928 | tf_op jit(solution)/shard_map/ppermute | solution.py:623
  95.6 4.1 %spatial_backward.1 = bf16[4,16,1280]{2,1,0:T(8,128)(2,1)} custom-call(bf16[128,1280]{1,0:T(8,128)(2,1)S(1)} %get-tuple-element.79.grad_hidden, bf16[4,16,1280]{2,1,0:T(8,128)(2,1)S(1)} %copy-done.9, bf16[128,3200]{1,0:T(8,128)(2,1)S(1)} %copy-done.14, f32[1280]{0:T(1024)S(1)} %copy-done.12, bf16[4,1280,640]{2,1,0:T(8,128)(2,1)S(1)} %bitcast.7), custom_call_target="tpu_custom_call" | custom-call | flops 3500000000 | bytes 1048576 | tf_op jit(solution)/shard_map/spatial_backward/pallas_call | solution.py:441
  99.7 3.4 %collective-permute-done.21 = bf16[88,640]{1,0:T(8,128)(2,1)S(1)} collective-permute-done((bf16[88,640]{1,0:T(8,128)(2,1)S(1)}, bf16[88,640]{1,0:T(8,128)(2,1)S(1)}, u32[]{:S(2)}, u32[]{:S(2)}) %collective-permute-start.21) | collective-permute-done | bytes 112672 | tf_op jit(solution)/shard_map/ppermute | solution.py:623
  (84 shorter events, 21.8 us)
Async XLA Ops:
  0.6 7.0 %collective-permute-start = (bf16[4,16,1280]{2,1,0:T(8,128)(2,1)}, bf16[4,16,1280]{2,1,0:T(8,128)(2,1)S(1)}, u32[]{:S(2)}, u32[]{:S(2)}) collective-permute-start(bf16[4,16,1280]{2,1,0:T(8,128)(2,1)} %xs.1), channel_id=1, source_target_pairs={{1,0},{0,1},{3,2},{2,3},{5,4},{4,5},{7,6},{6,7},{9,8},{8,9},{11,10... | collective-permute-start | bytes 491528 | tf_op jit(solution)/shard_map/ppermute | solution.py:488
  7.6 23.9 %copy-start.2 = (bf16[4,640,640]{2,1,0:T(8,128)(2,1)S(1)}, bf16[4,640,640]{2,1,0:T(8,128)(2,1)}, u32[]{:S(2)}) copy-start(bf16[4,640,640]{2,1,0:T(8,128)(2,1)} %refs_2_.1) | copy-start | bytes 9830404
  7.6 5.6 %collective-permute-start.1 = (bf16[4,16,1280]{2,1,0:T(8,128)(2,1)S(1)}, bf16[4,16,1280]{2,1,0:T(8,128)(2,1)S(1)}, u32[]{:S(2)}, u32[]{:S(2)}) collective-permute-start(bf16[4,16,1280]{2,1,0:T(8,128)(2,1)S(1)} %copy-done.3), channel_id=1, source_target_pairs={{1,0},{0,1},{3,2},{2,3},{5,4},{4,5},{7,6},{6,7},{9,8},{8,9},{11,10... | collective-permute-start | bytes 491528 | tf_op jit(solution)/shard_map/ppermute | solution.py:488
  33.0 9.0 %collective-permute-start.2 = (bf16[64,2560]{1,0:T(8,128)(2,1)S(1)}, bf16[64,2560]{1,0:T(8,128)(2,1)S(1)}, u32[]{:S(2)}, u32[]{:S(2)}) collective-permute-start(bf16[64,2560]{1,0:T(8,128)(2,1)S(1)} %get-tuple-element.48), channel_id=1, source_target_pairs={{0,1},{1,0},{2,3},{3,2},{4,5},{5,4},{6,7},{7,6},{8,9},{9,8},{10,11... | collective-permute-start | bytes 983048 | tf_op jit(solution)/shard_map/ppermute | solution.py:491
  34.9 8.1 %collective-permute-start.3 = (bf16[2,128,160]{2,1,0:T(8,128)(2,1)S(1)}, bf16[2,128,160]{2,1,0:T(8,128)(2,1)S(1)}, u32[]{:S(2)}, u32[]{:S(2)}) collective-permute-start(bf16[2,128,160]{2,1,0:T(8,128)(2,1)S(1)} %get-tuple-element.49), channel_id=1, source_target_pairs={{0,2},{2,0},{4,6},{6,4},{8,10},{10,8},{12,14},{14,12},{16,18},{18,... | collective-permute-start | bytes 245768 | tf_op jit(solution)/shard_map/ppermute | solution.py:501
  35.7 7.4 %collective-permute-start.4 = (bf16[2,128,160]{2,1,0:T(8,128)(2,1)S(1)}, bf16[2,128,160]{2,1,0:T(8,128)(2,1)S(1)}, u32[]{:S(2)}, u32[]{:S(2)}) collective-permute-start(bf16[2,128,160]{2,1,0:T(8,128)(2,1)S(1)} %get-tuple-element.50), channel_id=1, source_target_pairs={{0,4},{2,6},{4,0},{6,2},{8,12},{10,14},{12,8},{14,10},{16,20},{18,... | collective-permute-start | bytes 245768 | tf_op jit(solution)/shard_map/ppermute | solution.py:501
  35.7 8.0 %collective-permute-start.5 = (bf16[2,128,160]{2,1,0:T(8,128)(2,1)S(1)}, bf16[2,128,160]{2,1,0:T(8,128)(2,1)S(1)}, u32[]{:S(2)}, u32[]{:S(2)}) collective-permute-start(bf16[2,128,160]{2,1,0:T(8,128)(2,1)S(1)} %get-tuple-element.51), channel_id=1, source_target_pairs={{0,6},{2,4},{4,2},{6,0},{8,14},{10,12},{12,10},{14,8},{16,22},{18,... | collective-permute-start | bytes 245768 | tf_op jit(solution)/shard_map/ppermute | solution.py:501
  43.7 8.5 %collective-permute-start.7 = (bf16[64,2560]{1,0:T(8,128)(2,1)S(1)}, bf16[64,2560]{1,0:T(8,128)(2,1)S(1)}, u32[]{:S(2)}, u32[]{:S(2)}) collective-permute-start(bf16[64,2560]{1,0:T(8,128)(2,1)S(1)} %temporal_attention.1.refs_0_), channel_id=1, source_target_pairs={{1,0},{0,1},{3,2},{2,3},{5,4},{4,5},{7,6},{6,7},{9,8},{8,9},{11,10... | collective-permute-start | bytes 983048 | tf_op jit(solution)/shard_map/ppermute | solution.py:488
  44.6 9.2 %collective-permute-start.6 = (bf16[64,2560]{1,0:T(8,128)(2,1)S(1)}, bf16[64,2560]{1,0:T(8,128)(2,1)S(1)}, u32[]{:S(2)}, u32[]{:S(2)}) collective-permute-start(bf16[64,2560]{1,0:T(8,128)(2,1)S(1)} %temporal_attention.1.refs_0_), channel_id=1, source_target_pairs={{0,4},{2,6},{4,0},{6,2},{8,12},{10,14},{12,8},{14,10},{16,20},{18,... | collective-permute-start | bytes 983048 | tf_op jit(solution)/shard_map/ppermute | solution.py:501
  44.9 16.5 %collective-permute-start.9 = (bf16[64,2560]{1,0:T(8,128)(2,1)S(1)}, bf16[64,2560]{1,0:T(8,128)(2,1)S(1)}, u32[]{:S(2)}, u32[]{:S(2)}) collective-permute-start(bf16[64,2560]{1,0:T(8,128)(2,1)S(1)} %temporal_attention.1.refs_0_), channel_id=1, source_target_pairs={{0,2},{2,0},{4,6},{6,4},{8,10},{10,8},{12,14},{14,12},{16,18},{18,... | collective-permute-start | bytes 983048 | tf_op jit(solution)/shard_map/ppermute | solution.py:501
  52.2 9.2 %collective-permute-start.10 = (bf16[64,2560]{1,0:T(8,128)(2,1)S(1)}, bf16[64,2560]{1,0:T(8,128)(2,1)}, u32[]{:S(2)}, u32[]{:S(2)}) collective-permute-start(bf16[64,2560]{1,0:T(8,128)(2,1)S(1)} %collective-permute-done.7.refs_1_), channel_id=1, source_target_pairs={{0,2},{2,0},{4,6},{6,4},{8,10},{10,8},{12,14},{14,12},{16,18},{18,... | collective-permute-start | bytes 983048 | tf_op jit(solution)/shard_map/ppermute | solution.py:501
  53.8 7.6 %collective-permute-start.11 = (bf16[64,2560]{1,0:T(8,128)(2,1)S(1)}, bf16[64,2560]{1,0:T(8,128)(2,1)}, u32[]{:S(2)}, u32[]{:S(2)}) collective-permute-start(bf16[64,2560]{1,0:T(8,128)(2,1)S(1)} %collective-permute-done.6.refs_4_), channel_id=1, source_target_pairs={{0,2},{2,0},{4,6},{6,4},{8,10},{10,8},{12,14},{14,12},{16,18},{18,... | collective-permute-start | bytes 983048 | tf_op jit(solution)/shard_map/ppermute | solution.py:501
  54.7 9.3 %collective-permute-start.12 = (bf16[64,2560]{1,0:T(8,128)(2,1)S(1)}, bf16[64,2560]{1,0:T(8,128)(2,1)S(1)}, u32[]{:S(2)}, u32[]{:S(2)}) collective-permute-start(bf16[64,2560]{1,0:T(8,128)(2,1)S(1)} %collective-permute-done.7.refs_1_), channel_id=1, source_target_pairs={{0,4},{2,6},{4,0},{6,2},{8,12},{10,14},{12,8},{14,10},{16,20},{18,... | collective-permute-start | bytes 983048 | tf_op jit(solution)/shard_map/ppermute | solution.py:501
  57.6 14.6 %all-to-all-start.1 = ((bf16[16,16,640]{2,1,0:T(8,128)(2,1)}), bf16[16,16,640]{2,1,0:T(8,128)(2,1)S(1)}, u32[]{:S(2)}, u32[]{:S(2)}) async-start(bf16[16,16,640]{2,1,0:T(8,128)(2,1)} %get-tuple-element.57), calls=%async_computation.1 | async-start | bytes 655360 | tf_op jit(solution)/shard_map/all_to_all | solution.py:494
  64.1 2.2 %collective-permute-start.13 = (bf16[64,2560]{1,0:T(8,128)(2,1)S(1)}, bf16[64,2560]{1,0:T(8,128)(2,1)S(1)}, u32[]{:S(2)}, u32[]{:S(2)}) collective-permute-start(bf16[64,2560]{1,0:T(8,128)(2,1)S(1)} %collective-permute-done.12.refs_0_), channel_id=1, source_target_pairs={{0,2},{2,0},{4,6},{6,4},{8,10},{10,8},{12,14},{14,12},{16,18},{18,... | collective-permute-start | bytes 983048 | tf_op jit(solution)/shard_map/ppermute | solution.py:501
  67.5 6.4 %collective-permute-start.14 = (bf16[80,640]{1,0:T(8,128)(2,1)S(1)}, bf16[80,640]{1,0:T(8,128)(2,1)S(1)}, u32[]{:S(2)}, u32[]{:S(2)}) collective-permute-start(bf16[80,640]{1,0:T(8,128)(2,1)S(1)} %get-tuple-element.67), channel_id=1, source_target_pairs={{0,8},{2,10},{4,12},{6,14},{8,24},{10,26},{12,28},{14,30},{16,0},{... | collective-permute-start | bytes 307208 | tf_op jit(solution)/shard_map/ppermute | solution.py:501
  72.2 10.5 %collective-permute-start.8 = (bf16[16,16,640]{2,1,0:T(8,128)(2,1)S(1)}, bf16[16,16,640]{2,1,0:T(8,128)(2,1)S(1)}, u32[]{:S(2)}, u32[]{:S(2)}) collective-permute-start(bf16[16,16,640]{2,1,0:T(8,128)(2,1)S(1)} %all-to-all-done.1.refs_1_), channel_id=1, source_target_pairs={{1,0},{0,1},{3,2},{2,3},{5,4},{4,5},{7,6},{6,7},{9,8},{8,9},{11,10... | collective-permute-start | bytes 983048 | tf_op jit(solution)/shard_map/ppermute | solution.py:488
  72.7 4.5 %collective-permute-start.17 = (bf16[88,640]{1,0:T(8,128)(2,1)S(1)}, bf16[88,640]{1,0:T(8,128)(2,1)S(1)}, u32[]{:S(2)}, u32[]{:S(2)}) collective-permute-start(bf16[88,640]{1,0:T(8,128)(2,1)S(1)} %get-tuple-element.73), channel_id=1, source_target_pairs={{0,8},{2,10},{4,12},{6,14},{8,24},{10,26},{12,28},{14,30},{16,0},{... | collective-permute-start | bytes 337928 | tf_op jit(solution)/shard_map/ppermute | solution.py:501
  73.9 5.7 %collective-permute-start.15 = (bf16[80,640]{1,0:T(8,128)(2,1)S(1)}, bf16[80,640]{1,0:T(8,128)(2,1)S(1)}, u32[]{:S(2)}, u32[]{:S(2)}) collective-permute-start(bf16[80,640]{1,0:T(8,128)(2,1)S(1)} %add_convert_fusion.5), channel_id=1, source_target_pairs={{0,8},{2,10},{4,12},{6,14},{8,24},{10,26},{12,28},{14,30},{16,0},{... | collective-permute-start | bytes 307208 | tf_op jit(solution)/shard_map/ppermute | solution.py:501
  77.3 4.6 %collective-permute-start.18 = (bf16[88,640]{1,0:T(8,128)(2,1)S(1)}, bf16[88,640]{1,0:T(8,128)(2,1)S(1)}, u32[]{:S(2)}, u32[]{:S(2)}) collective-permute-start(bf16[88,640]{1,0:T(8,128)(2,1)S(1)} %add_convert_fusion.2), channel_id=1, source_target_pairs={{0,8},{2,10},{4,12},{6,14},{8,24},{10,26},{12,28},{14,30},{16,0},{... | collective-permute-start | bytes 337928 | tf_op jit(solution)/shard_map/ppermute | solution.py:501
  79.7 5.9 %collective-permute-start.16 = (bf16[80,640]{1,0:T(8,128)(2,1)S(1)}, bf16[80,640]{1,0:T(8,128)(2,1)S(1)}, u32[]{:S(2)}, u32[]{:S(2)}) collective-permute-start(bf16[80,640]{1,0:T(8,128)(2,1)S(1)} %add_convert_fusion.4), channel_id=1, source_target_pairs={{0,8},{2,10},{4,12},{6,14},{8,24},{10,26},{12,28},{14,30},{16,0},{... | collective-permute-start | bytes 307208 | tf_op jit(solution)/shard_map/ppermute | solution.py:501
  81.9 11.5 %collective-permute-start.19 = (bf16[88,640]{1,0:T(8,128)(2,1)S(1)}, bf16[88,640]{1,0:T(8,128)(2,1)S(1)}, u32[]{:S(2)}, u32[]{:S(2)}) collective-permute-start(bf16[88,640]{1,0:T(8,128)(2,1)S(1)} %add_convert_fusion.1), channel_id=1, source_target_pairs={{0,8},{2,10},{4,12},{6,14},{8,24},{10,26},{12,28},{14,30},{16,0},{... | collective-permute-start | bytes 337928 | tf_op jit(solution)/shard_map/ppermute | solution.py:501
  85.6 18.1 %collective-permute-start.20 = (bf16[80,640]{1,0:T(8,128)(2,1)S(1)}, bf16[80,640]{1,0:T(8,128)(2,1)S(1)}, u32[]{:S(2)}, u32[]{:S(2)}) collective-permute-start(bf16[80,640]{1,0:T(8,128)(2,1)S(1)} %add_convert_fusion.3), channel_id=1, source_target_pairs={{0,0},{1,16},{2,8},{3,24},{4,4},{5,20},{6,12},{7,28},{8,1},{9,17},... | collective-permute-start | bytes 307208 | tf_op jit(solution)/shard_map/ppermute | solution.py:623
  93.4 9.7 %collective-permute-start.21 = (bf16[88,640]{1,0:T(8,128)(2,1)S(1)}, bf16[88,640]{1,0:T(8,128)(2,1)S(1)}, u32[]{:S(2)}, u32[]{:S(2)}) collective-permute-start(bf16[88,640]{1,0:T(8,128)(2,1)S(1)} %add_convert_fusion), channel_id=1, source_target_pairs={{0,0},{1,16},{2,8},{3,24},{4,4},{5,20},{6,12},{7,28},{8,1},{9,17},... | collective-permute-start | bytes 337928 | tf_op jit(solution)/shard_map/ppermute | solution.py:623
  (16 other events, 152.6 us)

commit v10 on v8

--- a/solution.py
+++ b/solution.py
@@ -564,10 +564,9 @@
         back_kernel,
         "temporal_back_projection",
         [sds(nf, 2 * nq * fr, half), sds(3, half // 4, width)],
-        [geo] + all_terms + [motion_weights],
+        [geo, after(all_terms[0], pair_terms[0])] + all_terms[1:] + [motion_weights],
         0.01,
     )
-    pair_terms[0] = after(pair_terms[0], back_send)
     last_terms = [move(pair_terms[0], flipped(1))]
 
     stage, block = nf // 4, half // nf

time: 104 us -> 105 us (level)
  starting transfers between devices: 29.2 us -> 31.6 us
  waiting for transfers between devices: 25.5 us -> 23.6 us
    ppermute x15, waiting for transfers between devices: 14 us -> 6.89 us  [move(): return lax.ppermute(x, 'frame', pairs)]
    ppermute x15, starting transfers between devices: 9.88 us -> 13.4 us  [move(): return lax.ppermute(x, 'frame', pairs)]
    all_to_all x1, waiting for transfers between devices: 0.83 us -> 4.04 us  [swap(): return lax.all_to_all(x, 'frame', split_axis=0, concat_axis=0, tiled=True)]
    ppermute x2, waiting for transfers between devices: 1.47 us -> 3.44 us  [local(): totals = [lax.ppermute(t, ('frame', 'quad'), final) for t in totals]]
where the time goes in v10:
time: 105 us
  starting transfers between devices  31.6 us (30%)
  waiting for transfers between devices  23.6 us (22%)
  Pallas kernels  22.3 us (21%)
  blocking collectives  17.5 us (17%)
  local copies, waits for them, and re-layouts  6.71 us (6%)
  other arithmetic  1.87 us (2%)
    pallas_call x12, Pallas kernels, call(): pl.pallas_call(kernel, out_shape=outs, in_specs=in_specs, out_specs=[pl.B...  22.3 us
    all_to_all x1, blocking collectives, swap(): return lax.all_to_all(x, 'frame', split_axis=0, concat_axis=0, tiled=True)  17.5 us
    ppermute x15, starting transfers between devices, move(): return lax.ppermute(x, 'frame', pairs)  13.4 us
    ppermute x2, starting transfers between devices, local(): totals = [lax.ppermute(t, ('frame', 'quad'), final) for t in totals]  9.83 us
    ppermute x15, waiting for transfers between devices, move(): return lax.ppermute(x, 'frame', pairs)  6.89 us
    unnamed x34, local copies, waits for them, and re-layouts  6.7 us
    ppermute x4, waiting for transfers between devices, from_quad(): return lax.ppermute(x, 'quad', [((d + s) % nq, d) for d in range(nq)])  4.6 us
    ppermute x1, waiting for transfers between devices, to_quad(): return lax.ppermute(x, 'quad', [(d, (d + s) % nq) for d in range(nq)])  4.6 us
  transfers between devices with their start and end apart: 23, of which 11 were waited for; matrix products, arithmetic and copies ran while one was open for 1% of the time, Pallas kernels for 19%

profile of v10, /device:TPU:1, one launch (start us, length us, event | category | flops | bytes accessed | tf_op | source)
XLA Modules:
  0.0 104.5 jit_solution(15494742778668451654)
XLA Ops:
  0.6 2.1 %collective-permute-start = (bf16[4,16,1280]{2,1,0:T(8,128)(2,1)}, bf16[4,16,1280]{2,1,0:T(8,128)(2,1)S(1)}, u32[]{:S(2)}, u32[]{:S(2)}) collective-permute-start(bf16[4,16,1280]{2,1,0:T(8,128)(2,1)} %xs.1), channel_id=1, source_target_pairs={{1,0},{0,1},{3,2},{2,3},{5,4},{4,5},{7,6},{6,7},{9,8},{8,9},{11,10... | collective-permute-start | bytes 491528 | tf_op jit(solution)/shard_map/ppermute | solution.py:488
  3.1 2.9 %copy-done = bf16[4,1280,640]{2,1,0:T(8,128)(2,1)S(1)} copy-done((bf16[4,1280,640]{2,1,0:T(8,128)(2,1)S(1)}, bf16[4,1280,640]{2,1,0:T(8,128)(2,1)}, u32[]{:S(2)}) %copy-start) | copy-done | bytes 6553624
  8.0 1.7 %copy-done.1 = bf16[4,1280,640]{2,1,0:T(8,128)(2,1)S(1)} copy-done((bf16[4,1280,640]{2,1,0:T(8,128)(2,1)S(1)}, bf16[4,1280,640]{2,1,0:T(8,128)(2,1)}, u32[]{:S(2)}) %copy-start.1) | copy-done | bytes 6553624
  9.8 3.4 %spatial_forward.1 = (bf16[128,3200]{1,0:T(8,128)(2,1)S(1)}, bf16[16,8,640]{2,1,0:T(8,128)(2,1)S(1)}) custom-call(s32[3]{0:T(128)S(1)} %pad_add_fusion.refs_0_.geo.quad_ref, bf16[4,16,1280]{2,1,0:T(8,128)(2,1)S(1)} %copy-done.8, bf16[4,16,1280]{2,1,0:T(8,128)(2,1)S(1)} %collective-permute-done.refs_2_, f32[1280]{0:T(1024)S(1)} %copy-done.12, ...), custom_call_target="tpu_custom_call" | custom-call | flops 3000000000 | bytes 1048576 | tf_op jit(solution)/shard_map/spatial_forward/pallas_call | solution.py:441
  14.0 17.5 %all_to_all.10.received = bf16[16,16,640]{2,1,0:T(8,128)(2,1)S(1)} all-to-all(bf16[16,16,640]{2,1,0:T(8,128)(2,1)S(1)} %join_sent.1), channel_id=1, replica_groups=mesh['frame'=16,'quad'=2] {'frame'}, dimensions={0} | all-to-all | bytes 655360 | tf_op jit(solution)/shard_map/all_to_all | solution.py:494
  31.5 1.5 %motion_projection.1 = (f32[64,2560]{1,0:T(8,128)S(1)}, bf16[64,2560]{1,0:T(8,128)(2,1)S(1)}) custom-call(s32[3]{0:T(128)S(1)} %pad_add_fusion.refs_0_.geo.quad_ref, bf16[16,16,640]{2,1,0:T(8,128)(2,1)S(1)} %all_to_all.10.received, bf16[4,640,640]{2,1,0:T(8,128)(2,1)S(1)} %copy-done.2), custom_call_target="tpu_custom_call" | custom-call | flops 1500000000 | bytes 1048576 | tf_op jit(solution)/shard_map/motion_projection/pallas_call | solution.py:441
  33.7 1.3 %cut_factors.1 = (bf16[2,128,160]{2,1,0:T(8,128)(2,1)S(1)}, bf16[2,128,160]{2,1,0:T(8,128)(2,1)S(1)}, bf16[2,128,160]{2,1,0:T(8,128)(2,1)S(1)}, bf16[2,128,160]{2,1,0:T(8,128)(2,1)S(1)}) custom-call(s32[3]{0:T(128)S(1)} %pad_add_fusion.refs_0_.geo.quad_ref, bf16[16,16,640]{2,1,0:T(8,128)(2,1)S(1)} %all_to_all.10.received), custom_call_target="tpu_custom_call" | custom-call | flops 500000000 | bytes 1048576 | tf_op jit(solution)/shard_map/cut_factors/pallas_call | solution.py:441
  35.7 1.7 %collective-permute-start.5 = (bf16[2,128,160]{2,1,0:T(8,128)(2,1)S(1)}, bf16[2,128,160]{2,1,0:T(8,128)(2,1)S(1)}, u32[]{:S(2)}, u32[]{:S(2)}) collective-permute-start(bf16[2,128,160]{2,1,0:T(8,128)(2,1)S(1)} %get-tuple-element.51), channel_id=1, source_target_pairs={{0,6},{2,4},{4,2},{6,0},{8,14},{10,12},{12,10},{14,8},{16,22},{18,... | collective-permute-start | bytes 245768 | tf_op jit(solution)/shard_map/ppermute | solution.py:501
  37.4 4.6 %collective-permute-done.2.refs_1_ = bf16[64,2560]{1,0:T(8,128)(2,1)S(1)} collective-permute-done((bf16[64,2560]{1,0:T(8,128)(2,1)S(1)}, bf16[64,2560]{1,0:T(8,128)(2,1)S(1)}, u32[]{:S(2)}, u32[]{:S(2)}) %collective-permute-start.2) | collective-permute-done | bytes 327712 | tf_op jit(solution)/shard_map/ppermute | solution.py:491
  46.0 1.7 %positional_table_factors.1 = (f32[64,1280]{1,0:T(8,128)S(1)}, bf16[2,384,160]{2,1,0:T(8,128)(2,1)S(1)}, bf16[2,128,160]{2,1,0:T(8,128)(2,1)S(1)}) custom-call(s32[3]{0:T(128)S(1)} %pad_add_fusion.refs_0_.geo.quad_ref, bf16[2,128,160]{2,1,0:T(8,128)(2,1)S(1)} %get-tuple-element.46.refs_0_, bf16[2,128,160]{2,1,0:T(8,128)(2,1)S(1)} %collective-permute-done.3.refs_1_, ...), custom_call_target="tpu_custom_call" | custom-call | flops 1500000000 | bytes 1048576 | tf_op jit(solution)/shard_map/positional_table_factors/pallas_call | solution.py:441
  47.6 4.6 %collective-permute-done.7.refs_1_ = bf16[64,2560]{1,0:T(8,128)(2,1)S(1)} collective-permute-done((bf16[64,2560]{1,0:T(8,128)(2,1)S(1)}, bf16[64,2560]{1,0:T(8,128)(2,1)S(1)}, u32[]{:S(2)}, u32[]{:S(2)}) %collective-permute-start.7) | collective-permute-done | bytes 327712 | tf_op jit(solution)/shard_map/ppermute | solution.py:488
  52.2 1.6 %collective-permute-start.10 = (bf16[64,2560]{1,0:T(8,128)(2,1)S(1)}, bf16[64,2560]{1,0:T(8,128)(2,1)}, u32[]{:S(2)}, u32[]{:S(2)}) collective-permute-start(bf16[64,2560]{1,0:T(8,128)(2,1)S(1)} %collective-permute-done.7.refs_1_), channel_id=1, source_target_pairs={{0,2},{2,0},{4,6},{6,4},{8,10},{10,8},{12,14},{14,12},{16,18},{18,... | collective-permute-start | bytes 983048 | tf_op jit(solution)/shard_map/ppermute | solution.py:501
  55.1 2.5 %temporal_back_projection.1 = (bf16[16,16,640]{2,1,0:T(8,128)(2,1)}, bf16[3,160,640]{2,1,0:T(8,128)(2,1)S(1)}) custom-call(s32[3]{0:T(128)S(1)} %pad_add_fusion.refs_0_.geo.quad_ref, bf16[64,2560]{1,0:T(8,128)(2,1)S(1)} %temporal_attention.1.refs_0_, bf16[64,2560]{1,0:T(8,128)(2,1)S(1)} %collective-permute-done.7.refs_1_, bf16[4,640,640]{2,1,0:T(8,128)(2,1)S(1)} %copy-done.2), custom_call_target="tpu_custom_call" | custom-call | flops 10000000 | bytes 4096 | tf_op jit(solution)/shard_map/temporal_back_projection/pallas_call | solution.py:441
  57.6 3.8 %all-to-all-start.1 = ((bf16[16,16,640]{2,1,0:T(8,128)(2,1)}), bf16[16,16,640]{2,1,0:T(8,128)(2,1)S(1)}, u32[]{:S(2)}, u32[]{:S(2)}) async-start(bf16[16,16,640]{2,1,0:T(8,128)(2,1)} %get-tuple-element.57), calls=%async_computation.1 | async-start | bytes 655360 | tf_op jit(solution)/shard_map/all_to_all | solution.py:494
  61.5 2.3 %weight_terms_first_tokens.1 = (f32[4,4,40,640]{3,2,1,0:T(8,128)S(1)}, f32[1,160]{1,0:T(1,128)S(1)}) custom-call(s32[3]{0:T(128)S(1)} %pad_add_fusion.refs_0_.geo.quad_ref, bf16[2,384,160]{2,1,0:T(8,128)(2,1)S(1)} %get-tuple-element.61.left, bf16[3,160,640]{2,1,0:T(8,128)(2,1)S(1)} %get-tuple-element.62.weights, f32[64,1280]{1,0:T(8,128)S(1)} %get-tuple-element.55.pos, ...), custom_call_target="tpu_custom_call" | custom-call | flops 10000000 | bytes 4096 | tf_op jit(solution)/shard_map/weight_terms_first_tokens/pallas_call | solution.py:441
  68.2 4.0 %all-to-all-done.1.refs_1_ = bf16[16,16,640]{2,1,0:T(8,128)(2,1)S(1)} async-done(((bf16[16,16,640]{2,1,0:T(8,128)(2,1)}), bf16[16,16,640]{2,1,0:T(8,128)(2,1)S(1)}, u32[]{:S(2)}, u32[]{:S(2)}) %all-to-all-start.1) | async-done | bytes 327712 | tf_op jit(solution)/shard_map/all_to_all | solution.py:494
  74.4 2.8 %collective-permute-done.14 = bf16[88,640]{1,0:T(8,128)(2,1)S(1)} collective-permute-done((bf16[88,640]{1,0:T(8,128)(2,1)S(1)}, bf16[88,640]{1,0:T(8,128)(2,1)S(1)}, u32[]{:S(2)}, u32[]{:S(2)}) %collective-permute-start.14) | collective-permute-done | bytes 112672 | tf_op jit(solution)/shard_map/ppermute | solution.py:501
  77.3 1.5 %collective-permute-start.15 = (bf16[88,640]{1,0:T(8,128)(2,1)S(1)}, bf16[88,640]{1,0:T(8,128)(2,1)S(1)}, u32[]{:S(2)}, u32[]{:S(2)}) collective-permute-start(bf16[88,640]{1,0:T(8,128)(2,1)S(1)} %add_convert_fusion.2), channel_id=1, source_target_pairs={{0,8},{2,10},{4,12},{6,14},{8,24},{10,26},{12,28},{14,30},{16,0},{... | collective-permute-start | bytes 337928 | tf_op jit(solution)/shard_map/ppermute | solution.py:501
  79.7 1.3 %collective-permute-start.19 = (bf16[80,640]{1,0:T(8,128)(2,1)S(1)}, bf16[80,640]{1,0:T(8,128)(2,1)S(1)}, u32[]{:S(2)}, u32[]{:S(2)}) collective-permute-start(bf16[80,640]{1,0:T(8,128)(2,1)S(1)} %add_convert_fusion.4), channel_id=1, source_target_pairs={{0,8},{2,10},{4,12},{6,14},{8,24},{10,26},{12,28},{14,30},{16,0},{... | collective-permute-start | bytes 307208 | tf_op jit(solution)/shard_map/ppermute | solution.py:501
  83.9 1.7 %block_output_hidden_gradient.1 = (bf16[4,16,1280]{2,1,0:T(8,128)(2,1)}, bf16[128,1280]{1,0:T(8,128)(2,1)S(1)}) custom-call(s32[3]{0:T(128)S(1)} %pad_add_fusion.refs_0_.geo.quad_ref, bf16[16,16,640]{2,1,0:T(8,128)(2,1)S(1)} %all-to-all-done.1.refs_1_, bf16[16,16,640]{2,1,0:T(8,128)(2,1)S(1)} %collective-permute-done.8.refs_2_, ...), custom_call_target="tpu_custom_call" | custom-call | flops 6000000000 | bytes 1048576 | tf_op jit(solution)/shard_map/block_output_hidden_gradient/pallas_call | solution.py:441
  85.6 7.8 %collective-permute-start.21 = (bf16[80,640]{1,0:T(8,128)(2,1)S(1)}, bf16[80,640]{1,0:T(8,128)(2,1)S(1)}, u32[]{:S(2)}, u32[]{:S(2)}) collective-permute-start(bf16[80,640]{1,0:T(8,128)(2,1)S(1)} %add_convert_fusion.3), channel_id=1, source_target_pairs={{0,0},{1,16},{2,8},{3,24},{4,4},{5,20},{6,12},{7,28},{8,1},{9,17},... | collective-permute-start | bytes 307208 | tf_op jit(solution)/shard_map/ppermute | solution.py:623
  93.4 2.1 %collective-permute-start.20 = (bf16[88,640]{1,0:T(8,128)(2,1)S(1)}, bf16[88,640]{1,0:T(8,128)(2,1)S(1)}, u32[]{:S(2)}, u32[]{:S(2)}) collective-permute-start(bf16[88,640]{1,0:T(8,128)(2,1)S(1)} %add_convert_fusion), channel_id=1, source_target_pairs={{0,0},{1,16},{2,8},{3,24},{4,4},{5,20},{6,12},{7,28},{8,1},{9,17},... | collective-permute-start | bytes 337928 | tf_op jit(solution)/shard_map/ppermute | solution.py:623
  95.6 4.1 %spatial_backward.1 = bf16[4,16,1280]{2,1,0:T(8,128)(2,1)} custom-call(bf16[128,1280]{1,0:T(8,128)(2,1)S(1)} %get-tuple-element.79.grad_hidden, bf16[4,16,1280]{2,1,0:T(8,128)(2,1)S(1)} %copy-done.9, bf16[128,3200]{1,0:T(8,128)(2,1)S(1)} %copy-done.14, f32[1280]{0:T(1024)S(1)} %copy-done.12, bf16[4,1280,640]{2,1,0:T(8,128)(2,1)S(1)} %bitcast.7), custom_call_target="tpu_custom_call" | custom-call | flops 3500000000 | bytes 1048576 | tf_op jit(solution)/shard_map/spatial_backward/pallas_call | solution.py:441
  99.7 3.4 %collective-permute-done.20 = bf16[88,640]{1,0:T(8,128)(2,1)S(1)} collective-permute-done((bf16[88,640]{1,0:T(8,128)(2,1)S(1)}, bf16[88,640]{1,0:T(8,128)(2,1)S(1)}, u32[]{:S(2)}, u32[]{:S(2)}) %collective-permute-start.20) | collective-permute-done | bytes 112672 | tf_op jit(solution)/shard_map/ppermute | solution.py:623
  (84 shorter events, 21.8 us)
Async XLA Ops:
  0.6 7.0 %collective-permute-start = (bf16[4,16,1280]{2,1,0:T(8,128)(2,1)}, bf16[4,16,1280]{2,1,0:T(8,128)(2,1)S(1)}, u32[]{:S(2)}, u32[]{:S(2)}) collective-permute-start(bf16[4,16,1280]{2,1,0:T(8,128)(2,1)} %xs.1), channel_id=1, source_target_pairs={{1,0},{0,1},{3,2},{2,3},{5,4},{4,5},{7,6},{6,7},{9,8},{8,9},{11,10... | collective-permute-start | bytes 491528 | tf_op jit(solution)/shard_map/ppermute | solution.py:488
  7.6 23.9 %copy-start.2 = (bf16[4,640,640]{2,1,0:T(8,128)(2,1)S(1)}, bf16[4,640,640]{2,1,0:T(8,128)(2,1)}, u32[]{:S(2)}) copy-start(bf16[4,640,640]{2,1,0:T(8,128)(2,1)} %refs_2_.1) | copy-start | bytes 9830404
  7.6 5.6 %collective-permute-start.1 = (bf16[4,16,1280]{2,1,0:T(8,128)(2,1)S(1)}, bf16[4,16,1280]{2,1,0:T(8,128)(2,1)S(1)}, u32[]{:S(2)}, u32[]{:S(2)}) collective-permute-start(bf16[4,16,1280]{2,1,0:T(8,128)(2,1)S(1)} %copy-done.3), channel_id=1, source_target_pairs={{1,0},{0,1},{3,2},{2,3},{5,4},{4,5},{7,6},{6,7},{9,8},{8,9},{11,10... | collective-permute-start | bytes 491528 | tf_op jit(solution)/shard_map/ppermute | solution.py:488
  33.0 9.0 %collective-permute-start.2 = (bf16[64,2560]{1,0:T(8,128)(2,1)S(1)}, bf16[64,2560]{1,0:T(8,128)(2,1)S(1)}, u32[]{:S(2)}, u32[]{:S(2)}) collective-permute-start(bf16[64,2560]{1,0:T(8,128)(2,1)S(1)} %get-tuple-element.48), channel_id=1, source_target_pairs={{0,1},{1,0},{2,3},{3,2},{4,5},{5,4},{6,7},{7,6},{8,9},{9,8},{10,11... | collective-permute-start | bytes 983048 | tf_op jit(solution)/shard_map/ppermute | solution.py:491
  34.9 8.1 %collective-permute-start.3 = (bf16[2,128,160]{2,1,0:T(8,128)(2,1)S(1)}, bf16[2,128,160]{2,1,0:T(8,128)(2,1)S(1)}, u32[]{:S(2)}, u32[]{:S(2)}) collective-permute-start(bf16[2,128,160]{2,1,0:T(8,128)(2,1)S(1)} %get-tuple-element.49), channel_id=1, source_target_pairs={{0,2},{2,0},{4,6},{6,4},{8,10},{10,8},{12,14},{14,12},{16,18},{18,... | collective-permute-start | bytes 245768 | tf_op jit(solution)/shard_map/ppermute | solution.py:501
  35.7 7.4 %collective-permute-start.4 = (bf16[2,128,160]{2,1,0:T(8,128)(2,1)S(1)}, bf16[2,128,160]{2,1,0:T(8,128)(2,1)S(1)}, u32[]{:S(2)}, u32[]{:S(2)}) collective-permute-start(bf16[2,128,160]{2,1,0:T(8,128)(2,1)S(1)} %get-tuple-element.50), channel_id=1, source_target_pairs={{0,4},{2,6},{4,0},{6,2},{8,12},{10,14},{12,8},{14,10},{16,20},{18,... | collective-permute-start | bytes 245768 | tf_op jit(solution)/shard_map/ppermute | solution.py:501
  35.7 8.0 %collective-permute-start.5 = (bf16[2,128,160]{2,1,0:T(8,128)(2,1)S(1)}, bf16[2,128,160]{2,1,0:T(8,128)(2,1)S(1)}, u32[]{:S(2)}, u32[]{:S(2)}) collective-permute-start(bf16[2,128,160]{2,1,0:T(8,128)(2,1)S(1)} %get-tuple-element.51), channel_id=1, source_target_pairs={{0,6},{2,4},{4,2},{6,0},{8,14},{10,12},{12,10},{14,8},{16,22},{18,... | collective-permute-start | bytes 245768 | tf_op jit(solution)/shard_map/ppermute | solution.py:501
  43.7 8.5 %collective-permute-start.7 = (bf16[64,2560]{1,0:T(8,128)(2,1)S(1)}, bf16[64,2560]{1,0:T(8,128)(2,1)S(1)}, u32[]{:S(2)}, u32[]{:S(2)}) collective-permute-start(bf16[64,2560]{1,0:T(8,128)(2,1)S(1)} %temporal_attention.1.refs_0_), channel_id=1, source_target_pairs={{1,0},{0,1},{3,2},{2,3},{5,4},{4,5},{7,6},{6,7},{9,8},{8,9},{11,10... | collective-permute-start | bytes 983048 | tf_op jit(solution)/shard_map/ppermute | solution.py:488
  44.6 9.2 %collective-permute-start.6 = (bf16[64,2560]{1,0:T(8,128)(2,1)S(1)}, bf16[64,2560]{1,0:T(8,128)(2,1)S(1)}, u32[]{:S(2)}, u32[]{:S(2)}) collective-permute-start(bf16[64,2560]{1,0:T(8,128)(2,1)S(1)} %temporal_attention.1.refs_0_), channel_id=1, source_target_pairs={{0,4},{2,6},{4,0},{6,2},{8,12},{10,14},{12,8},{14,10},{16,20},{18,... | collective-permute-start | bytes 983048 | tf_op jit(solution)/shard_map/ppermute | solution.py:501
  44.9 16.5 %collective-permute-start.9 = (bf16[64,2560]{1,0:T(8,128)(2,1)S(1)}, bf16[64,2560]{1,0:T(8,128)(2,1)S(1)}, u32[]{:S(2)}, u32[]{:S(2)}) collective-permute-start(bf16[64,2560]{1,0:T(8,128)(2,1)S(1)} %temporal_attention.1.refs_0_), channel_id=1, source_target_pairs={{0,2},{2,0},{4,6},{6,4},{8,10},{10,8},{12,14},{14,12},{16,18},{18,... | collective-permute-start | bytes 983048 | tf_op jit(solution)/shard_map/ppermute | solution.py:501
  52.2 9.2 %collective-permute-start.10 = (bf16[64,2560]{1,0:T(8,128)(2,1)S(1)}, bf16[64,2560]{1,0:T(8,128)(2,1)}, u32[]{:S(2)}, u32[]{:S(2)}) collective-permute-start(bf16[64,2560]{1,0:T(8,128)(2,1)S(1)} %collective-permute-done.7.refs_1_), channel_id=1, source_target_pairs={{0,2},{2,0},{4,6},{6,4},{8,10},{10,8},{12,14},{14,12},{16,18},{18,... | collective-permute-start | bytes 983048 | tf_op jit(solution)/shard_map/ppermute | solution.py:501
  53.8 7.6 %collective-permute-start.11 = (bf16[64,2560]{1,0:T(8,128)(2,1)S(1)}, bf16[64,2560]{1,0:T(8,128)(2,1)}, u32[]{:S(2)}, u32[]{:S(2)}) collective-permute-start(bf16[64,2560]{1,0:T(8,128)(2,1)S(1)} %collective-permute-done.6.refs_4_), channel_id=1, source_target_pairs={{0,2},{2,0},{4,6},{6,4},{8,10},{10,8},{12,14},{14,12},{16,18},{18,... | collective-permute-start | bytes 983048 | tf_op jit(solution)/shard_map/ppermute | solution.py:501
  54.7 9.3 %collective-permute-start.12 = (bf16[64,2560]{1,0:T(8,128)(2,1)S(1)}, bf16[64,2560]{1,0:T(8,128)(2,1)S(1)}, u32[]{:S(2)}, u32[]{:S(2)}) collective-permute-start(bf16[64,2560]{1,0:T(8,128)(2,1)S(1)} %collective-permute-done.7.refs_1_), channel_id=1, source_target_pairs={{0,4},{2,6},{4,0},{6,2},{8,12},{10,14},{12,8},{14,10},{16,20},{18,... | collective-permute-start | bytes 983048 | tf_op jit(solution)/shard_map/ppermute | solution.py:501
  57.6 14.6 %all-to-all-start.1 = ((bf16[16,16,640]{2,1,0:T(8,128)(2,1)}), bf16[16,16,640]{2,1,0:T(8,128)(2,1)S(1)}, u32[]{:S(2)}, u32[]{:S(2)}) async-start(bf16[16,16,640]{2,1,0:T(8,128)(2,1)} %get-tuple-element.57), calls=%async_computation.1 | async-start | bytes 655360 | tf_op jit(solution)/shard_map/all_to_all | solution.py:494
  64.1 2.2 %collective-permute-start.13 = (bf16[64,2560]{1,0:T(8,128)(2,1)S(1)}, bf16[64,2560]{1,0:T(8,128)(2,1)S(1)}, u32[]{:S(2)}, u32[]{:S(2)}) collective-permute-start(bf16[64,2560]{1,0:T(8,128)(2,1)S(1)} %collective-permute-done.12.refs_0_), channel_id=1, source_target_pairs={{0,2},{2,0},{4,6},{6,4},{8,10},{10,8},{12,14},{14,12},{16,18},{18,... | collective-permute-start | bytes 983048 | tf_op jit(solution)/shard_map/ppermute | solution.py:501
  67.5 6.4 %collective-permute-start.17 = (bf16[80,640]{1,0:T(8,128)(2,1)S(1)}, bf16[80,640]{1,0:T(8,128)(2,1)S(1)}, u32[]{:S(2)}, u32[]{:S(2)}) collective-permute-start(bf16[80,640]{1,0:T(8,128)(2,1)S(1)} %get-tuple-element.73), channel_id=1, source_target_pairs={{0,8},{2,10},{4,12},{6,14},{8,24},{10,26},{12,28},{14,30},{16,0},{... | collective-permute-start | bytes 307208 | tf_op jit(solution)/shard_map/ppermute | solution.py:501
  72.2 10.5 %collective-permute-start.8 = (bf16[16,16,640]{2,1,0:T(8,128)(2,1)S(1)}, bf16[16,16,640]{2,1,0:T(8,128)(2,1)S(1)}, u32[]{:S(2)}, u32[]{:S(2)}) collective-permute-start(bf16[16,16,640]{2,1,0:T(8,128)(2,1)S(1)} %all-to-all-done.1.refs_1_), channel_id=1, source_target_pairs={{1,0},{0,1},{3,2},{2,3},{5,4},{4,5},{7,6},{6,7},{9,8},{8,9},{11,10... | collective-permute-start | bytes 983048 | tf_op jit(solution)/shard_map/ppermute | solution.py:488
  72.7 4.5 %collective-permute-start.14 = (bf16[88,640]{1,0:T(8,128)(2,1)S(1)}, bf16[88,640]{1,0:T(8,128)(2,1)S(1)}, u32[]{:S(2)}, u32[]{:S(2)}) collective-permute-start(bf16[88,640]{1,0:T(8,128)(2,1)S(1)} %get-tuple-element.67), channel_id=1, source_target_pairs={{0,8},{2,10},{4,12},{6,14},{8,24},{10,26},{12,28},{14,30},{16,0},{... | collective-permute-start | bytes 337928 | tf_op jit(solution)/shard_map/ppermute | solution.py:501
  73.9 5.7 %collective-permute-start.18 = (bf16[80,640]{1,0:T(8,128)(2,1)S(1)}, bf16[80,640]{1,0:T(8,128)(2,1)S(1)}, u32[]{:S(2)}, u32[]{:S(2)}) collective-permute-start(bf16[80,640]{1,0:T(8,128)(2,1)S(1)} %add_convert_fusion.5), channel_id=1, source_target_pairs={{0,8},{2,10},{4,12},{6,14},{8,24},{10,26},{12,28},{14,30},{16,0},{... | collective-permute-start | bytes 307208 | tf_op jit(solution)/shard_map/ppermute | solution.py:501
  77.3 4.6 %collective-permute-start.15 = (bf16[88,640]{1,0:T(8,128)(2,1)S(1)}, bf16[88,640]{1,0:T(8,128)(2,1)S(1)}, u32[]{:S(2)}, u32[]{:S(2)}) collective-permute-start(bf16[88,640]{1,0:T(8,128)(2,1)S(1)} %add_convert_fusion.2), channel_id=1, source_target_pairs={{0,8},{2,10},{4,12},{6,14},{8,24},{10,26},{12,28},{14,30},{16,0},{... | collective-permute-start | bytes 337928 | tf_op jit(solution)/shard_map/ppermute | solution.py:501
  79.7 5.9 %collective-permute-start.19 = (bf16[80,640]{1,0:T(8,128)(2,1)S(1)}, bf16[80,640]{1,0:T(8,128)(2,1)S(1)}, u32[]{:S(2)}, u32[]{:S(2)}) collective-permute-start(bf16[80,640]{1,0:T(8,128)(2,1)S(1)} %add_convert_fusion.4), channel_id=1, source_target_pairs={{0,8},{2,10},{4,12},{6,14},{8,24},{10,26},{12,28},{14,30},{16,0},{... | collective-permute-start | bytes 307208 | tf_op jit(solution)/shard_map/ppermute | solution.py:501
  81.9 11.5 %collective-permute-start.16 = (bf16[88,640]{1,0:T(8,128)(2,1)S(1)}, bf16[88,640]{1,0:T(8,128)(2,1)S(1)}, u32[]{:S(2)}, u32[]{:S(2)}) collective-permute-start(bf16[88,640]{1,0:T(8,128)(2,1)S(1)} %add_convert_fusion.1), channel_id=1, source_target_pairs={{0,8},{2,10},{4,12},{6,14},{8,24},{10,26},{12,28},{14,30},{16,0},{... | collective-permute-start | bytes 337928 | tf_op jit(solution)/shard_map/ppermute | solution.py:501
  85.6 18.1 %collective-permute-start.21 = (bf16[80,640]{1,0:T(8,128)(2,1)S(1)}, bf16[80,640]{1,0:T(8,128)(2,1)S(1)}, u32[]{:S(2)}, u32[]{:S(2)}) collective-permute-start(bf16[80,640]{1,0:T(8,128)(2,1)S(1)} %add_convert_fusion.3), channel_id=1, source_target_pairs={{0,0},{1,16},{2,8},{3,24},{4,4},{5,20},{6,12},{7,28},{8,1},{9,17},... | collective-permute-start | bytes 307208 | tf_op jit(solution)/shard_map/ppermute | solution.py:623
  93.4 9.7 %collective-permute-start.20 = (bf16[88,640]{1,0:T(8,128)(2,1)S(1)}, bf16[88,640]{1,0:T(8,128)(2,1)S(1)}, u32[]{:S(2)}, u32[]{:S(2)}) collective-permute-start(bf16[88,640]{1,0:T(8,128)(2,1)S(1)} %add_convert_fusion), channel_id=1, source_target_pairs={{0,0},{1,16},{2,8},{3,24},{4,4},{5,20},{6,12},{7,28},{8,1},{9,17},... | collective-permute-start | bytes 337928 | tf_op jit(solution)/shard_map/ppermute | solution.py:623
  (16 other events, 152.6 us)
